TPU v7x, 128 devices: a whole 4x4x4 slice. The times are simulated.
128 devices in a mesh: ctx: 16 (over x, y), db: 8 (over z, core).
Axes of the slice: x: 4, y: 4, z: 4, core: 2. Of those that a mesh axis runs over, the one named last changes fastest.
Arguments:
- states: bfloat16 [4096, 4096], P('ctx', 'db'), may hold values from -60 to 60
- cotangent: bfloat16 [4096, 4096], P('ctx', 'db'), may hold values from -6 to 6
- w_query: bfloat16 [4096, 4096], P(None, 'db'), may hold values from -0.09375 to 0.09375
- w_key: bfloat16 [896, 4096], P(None, 'db'), may hold values from -0.1875 to 0.1875
- w_value: bfloat16 [896, 4096], P(None, 'db'), may hold values from -0.1875 to 0.1875
- w_out: bfloat16 [4096, 4096], P('db'), may hold values from -0.09375 to 0.09375
- database: bfloat16 [768, 128, 896], P('db'), may hold values from -6 to 6
- neighbour_shard: int32 [64, 2], P('ctx'), may hold values from 0 to 7, all different within a row; in each aligned block of 4 rows (0 to 3, 4 to 7, ...) at most 2 rows name the same one
- neighbour_row: int32 [64, 2], P('ctx'), may hold values from 0 to 95
Outputs:
- grad_states: float32 [4096, 4096], P('ctx', 'db')
- grad_database: float32 [768, 128, 896], P('db', 'ctx')
Inputs may be any that keep to these rules, and one draw needn't show every extreme that they name: `neighbour_shard`: the 2 neighbours of a span lie in different shards. Among the 4 spans of one index of ctx, at most 2 neighbours lie in one shard, and some shard holds exactly 2.
All inputs are finite; a program needn't handle non-finite values.
Results may differ from a plain program's by a relative error of at most 0.022.
The roundings to bfloat16 on the way count: a program that leaves them out, or rounds other values in their place, can miss the bound.
Values may be sent and summed in bfloat16 or wider, within the bound.
No kernel may reach another device: no remote copies, remote signals or barrier semaphores. Data moves between devices by JAX's collectives and lax.ppermute only.
A program may use at most 192 MiB of HBM per device.

v0:
```python
import jax
import jax.numpy as jnp
from jax import lax
from jax.sharding import PartitionSpec as P

HDIM = 128
DE = 896
CH = 64
R = 128
K = 2


def passed_along(shard, axis, by):
    peers = lax.axis_size(axis)
    pairs = [(i, i + by) for i in range(peers) if 0 <= i + by < peers]
    return lax.ppermute(shard, axis, pairs)


def per_device(
    states, cotangent, w_query, w_key, w_value, w_out, database, neighbour_shard, neighbour_row
):
    db_count = lax.axis_size("db")
    my_shard = lax.axis_index("db")
    token_rows = states.shape[0]
    border = CH - 1
    span_count = token_rows // CH
    local_width = w_query.shape[1]
    local_heads = local_width // HDIM
    shard_rows = database.shape[0]
    capacity = max(2, span_count * K * 2 // db_count)
    request_count = span_count * K
    lead_states, lead_cotangent = passed_along((states[:border], cotangent[:border]), "ctx", -1)
    att_states = jnp.concatenate([states[border:], lead_states], 0)
    att_cotangent = jnp.concatenate([cotangent[border:], lead_cotangent], 0)
    full_states, full_cotangent = (
        lax.all_gather(att_states, "db", axis=1, tiled=True),
        lax.all_gather(att_cotangent, "db", axis=1, tiled=True),
    )
    query = jnp.dot(full_states, w_query, preferred_element_type=jnp.float32).astype(jnp.bfloat16)
    grad_out = lax.dot_general(
        full_cotangent, w_out, (((1,), (1,)), ((), ())), preferred_element_type=jnp.float32
    ).astype(jnp.bfloat16)
    shard_flat = neighbour_shard.reshape(-1)
    row_flat = neighbour_row.reshape(-1)
    request_order = jnp.arange(request_count, dtype=jnp.int32)
    earlier = (shard_flat[None, :] == shard_flat[:, None]) & (
        request_order[None, :] < request_order[:, None]
    )
    rank_in_shard = jnp.sum(earlier.astype(jnp.int32), 1)
    slot_of = shard_flat * capacity + rank_in_shard
    slot_range = jnp.arange(capacity, dtype=jnp.int32)
    my_match = (shard_flat[None, :] == my_shard) & (rank_in_shard[None, :] == slot_range[:, None])
    owned_row = jnp.sum(jnp.where(my_match, row_flat[None, :], 0), 1)
    owned_live = jnp.any(my_match, 1)
    outgoing = jnp.where(
        owned_live[:, None, None],
        jnp.take(database, owned_row, axis=0),
        jnp.zeros((), jnp.bfloat16),
    )
    w_both = jnp.concatenate([w_key, w_value], 1)
    piece = lax.all_gather(outgoing, "db", axis=0, tiled=True)
    count = piece.shape[0]
    flat = jnp.dot(piece.reshape(count * R, DE), w_both, preferred_element_type=jnp.float32)
    slot_states = flat.astype(jnp.bfloat16).reshape(count, R, 2 * local_width)
    request_states = jnp.take(slot_states, slot_of, axis=0).reshape(
        span_count, K * R, 2 * local_width
    )
    keys = request_states[:, :, :local_width].reshape(span_count, K * R, local_heads, HDIM)
    values = request_states[:, :, local_width:].reshape(span_count, K * R, local_heads, HDIM)
    query_blocks = query.reshape(span_count, CH, local_heads, HDIM)
    grad_blocks = grad_out.reshape(span_count, CH, local_heads, HDIM)
    scale = HDIM ** (-0.5)
    scores = (
        jnp.einsum("cqhd,ckhd->chqk", query_blocks, keys, preferred_element_type=jnp.float32)
        * scale
    )
    attention = jax.nn.softmax(scores, axis=-1)
    attention_b = attention.astype(jnp.bfloat16)
    dattention = jnp.einsum(
        "cqhd,ckhd->chqk", grad_blocks, values, preferred_element_type=jnp.float32
    )
    dscores = (
        attention * (dattention - jnp.sum(attention * dattention, -1, keepdims=True))
    ).astype(jnp.bfloat16)
    grad_query = (
        jnp.einsum("chqk,ckhd->cqhd", dscores, keys, preferred_element_type=jnp.float32) * scale
    ).astype(jnp.bfloat16)
    grad_keys = (
        jnp.einsum("chqk,cqhd->ckhd", dscores, query_blocks, preferred_element_type=jnp.float32)
        * scale
    ).astype(jnp.bfloat16)
    grad_values = jnp.einsum(
        "chqk,cqhd->ckhd", attention_b, grad_blocks, preferred_element_type=jnp.float32
    ).astype(jnp.bfloat16)
    grad_both = jnp.concatenate(
        [
            grad_keys.reshape(request_count, R, local_width),
            grad_values.reshape(request_count, R, local_width),
        ],
        -1,
    )
    cross_part = lax.dot_general(
        grad_query.reshape(token_rows, local_width),
        w_query,
        (((1,), (1,)), ((), ())),
        preferred_element_type=jnp.float32,
    )
    cross_local = lax.psum_scatter(
        cross_part.astype(jnp.bfloat16), "db", scatter_dimension=1, tiled=True
    ).astype(jnp.float32)
    carried = passed_along(
        cross_local[token_rows - border :].astype(jnp.bfloat16), "ctx", 1
    ).astype(jnp.float32)
    aligned = jnp.concatenate([carried, cross_local[: token_rows - border]], 0)
    grad_states = cotangent.astype(jnp.float32) + aligned
    wanted = jnp.arange(lax.axis_size("db") * capacity, dtype=jnp.int32)
    match = slot_of[None, :] == wanted[:, None]
    picked = jnp.sum(jnp.where(match, request_order[None, :], 0), 1)
    live = jnp.any(match, 1)
    rows_in = jnp.take(grad_both, picked, axis=0)
    term = lax.dot_general(
        rows_in, w_both, (((2,), (1,)), ((), ())), preferred_element_type=jnp.float32
    )
    slot_grads = lax.psum_scatter(
        jnp.where(live[:, None, None], term, 0.0).astype(jnp.bfloat16),
        "db",
        scatter_dimension=0,
        tiled=True,
    ).astype(jnp.float32)
    owned_id = jnp.where(owned_live, owned_row, -1)
    shard_range = jnp.arange(shard_rows, dtype=jnp.int32)
    table = (owned_id[None, :] == shard_range[:, None]).astype(jnp.float32)
    dense = jnp.einsum("bs,srd->brd", table, slot_grads, precision=lax.Precision.HIGHEST)
    grad_database = lax.psum_scatter(
        dense.astype(jnp.bfloat16), "ctx", scatter_dimension=1, tiled=True
    ).astype(jnp.float32)
    return (grad_states, grad_database)


def solution(mesh):
    in_specs = (
        P("ctx", "db"),
        P("ctx", "db"),
        P(None, "db"),
        P(None, "db"),
        P(None, "db"),
        P("db", None),
        P("db", None, None),
        P("ctx", None),
        P("ctx", None),
    )
    out_specs = (P("ctx", "db"), P("db", "ctx", None))
    return jax.shard_map(
        per_device, mesh=mesh, in_specs=in_specs, out_specs=out_specs, check_vma=False
    )
```

profile of v0, /device:TPU:2, one launch (start us, length us, event | category | flops | bytes accessed | tf_op | source)
XLA Modules:
  0.0 373.2 jit_solution(10441526508518602885)
XLA Ops:
  8.2 4.9 %collective-permute-start = (bf16[63,512]{1,0:T(8,128)(2,1)S(1)}, bf16[63,512]{1,0:T(8,128)(2,1)S(1)}, u32[]{:S(2)}, u32[]{:S(2)}) collective-permute-start(bf16[63,512]{1,0:T(8,128)(2,1)S(1)} %slice.28), channel_id=1, source_target_pairs={{8,0},{16,8},{24,16},{32,24},{40,32},{48,40},{56,48},{64,56},{72,6... | collective-permute-start | bytes 193544 | tf_op jit(solution)/shard_map/ppermute | solution.py:16
  16.6 6.4 %collective-permute-start.1 = (bf16[63,512]{1,0:T(8,128)(2,1)S(1)}, bf16[63,512]{1,0:T(8,128)(2,1)S(1)}, u32[]{:S(2)}, u32[]{:S(2)}) collective-permute-start(bf16[63,512]{1,0:T(8,128)(2,1)S(1)} %slice.30), channel_id=1, source_target_pairs={{8,0},{16,8},{24,16},{32,24},{40,32},{48,40},{56,48},{64,56},{72,6... | collective-permute-start | bytes 193544 | tf_op jit(solution)/shard_map/ppermute | solution.py:16
  27.8 8.2 %gather_fusion = bf16[2,128,896]{2,1,0:T(8,128)(2,1)S(1)} fusion(bf16[96,128,896]{2,1,0:T(8,128)(2,1)} %param.15, s32[1024]{0:T(1024)S(1)} %get-tuple-element.19), kind=kCustom, calls=%fused_computation | custom fusion | bytes 917512 | tf_op jit(solution)/shard_map/jit(_take)/gather | solution.py:57
  39.1 5.8 %all-gather.6.cloned.1.call-done = bf16[256,4096]{1,0:T(8,128)(2,1)} async-done(((bf16[256,512]{1,0:T(8,128)(2,1)}), bf16[256,4096]{1,0:T(8,128)(2,1)}) %all-gather.6.cloned.1.call-update) | async-done | bytes 2097168 | tf_op jit(solution)/shard_map/all_gather | solution.py:36
  44.9 4.1 %convolution_convert_fusion.5 = bf16[256,512]{1,0:T(8,128)(2,1)S(1)} fusion(bf16[256,4096]{1,0:T(8,128)(2,1)} %all-gather.6.cloned.1.call-done, bf16[4096,512]{1,0:T(8,128)(2,1)} %param.11), kind=kOutput, calls=%fused_computation.24 | convolution fusion | flops 1073872896 | bytes 6553600 | tf_op jit(solution)/shard_map/dot_general | solution.py:39
  49.1 23.3 %all-gather.8.cloned.1.call-done = bf16[256,4096]{1,0:T(8,128)(2,1)} async-done(((bf16[256,512]{1,0:T(8,128)(2,1)}), bf16[256,4096]{1,0:T(8,128)(2,1)}) %all-gather.8.cloned.1.call-update) | async-done | bytes 2097168 | tf_op jit(solution)/shard_map/all_gather | solution.py:37
  72.4 4.1 %convolution_convert_fusion.4 = bf16[256,512]{1,0:T(8,128)(2,1)S(1)} fusion(bf16[256,4096]{1,0:T(8,128)(2,1)} %all-gather.8.cloned.1.call-done, bf16[512,4096]{1,0:T(8,128)(2,1)} %param.14), kind=kOutput, calls=%fused_computation.23 | convolution fusion | flops 1073872896 | bytes 6553600 | tf_op jit(solution)/shard_map/dot_general | solution.py:40
  77.2 28.0 %all-gather.4.cloned.1.call-done = bf16[16,128,896]{2,1,0:T(8,128)(2,1)} async-done(((bf16[2,128,896]{2,1,0:T(8,128)(2,1)}), bf16[16,128,896]{2,1,0:T(8,128)(2,1)}) %all-gather.4.cloned.1.call-update) | async-done | bytes 3670032 | tf_op jit(solution)/shard_map/all_gather | solution.py:61
  105.2 8.2 %convolution_convert_fusion.2 = bf16[2048,1024]{1,0:T(8,128)(2,1)} fusion(bf16[2048,896]{1,0:T(8,128)(2,1)} %bitcast.60, bf16[896,1024]{1,0:T(8,128)(2,1)S(1)} %copy-done.6), kind=kOutput, calls=%fused_computation.10 | convolution fusion | flops 3760193536 | bytes 9699328 | tf_op jit(solution)/shard_map/dot_general | solution.py:63
  113.4 2.9 gather_fusion.1
  118.8 2.8 fusion.32
  121.7 4.1 %fusion.7 = bf16[4,256,4,128]{1,3,2,0:T(8,128)(2,1)} fusion(bf16[4,64,4,128]{3,2,1,0:T(4,128)(2,1)} %reshape.145, f32[4,4,64]{2,1,0:T(4,128)S(1)} %get-tuple-element.14, f32[4,4,64,256]{3,2,1,0:T(8,128)S(1)} %convolution_multiply_fusion), kind=kOutput, calls=%fused_computation.17 | convolution fusion | flops 68420864 | bytes 2363392 | tf_op jit(solution)/shard_map/chqk,cqhd->ckhd/dot_general | solution.py:92
  135.8 2.7 gather_fusion.2
  138.5 2.8 broadcast_select_fusion
  141.3 7.6 %select_convert_fusion = bf16[16,128,896]{2,0,1:T(8,128)(2,1)S(1)} fusion(pred[16]{0:T(512)(128)(4,1)S(1)} %fusion.21, bf16[16,128,1024]{2,1,0:T(8,128)(2,1)S(1)} %broadcast_select_fusion, bf16[896,1024]{1,0:T(8,128)(2,1)S(1)} %copy-done.7), kind=kOutput, calls=%fused_computation.5 | convolution fusion | flops 3761766400 | bytes 9699344 | tf_op jit(solution)/shard_map/dot_general | solution.py:121
  148.9 2.6 copy.89
  153.3 4.8 %convolution_convert_fusion.1 = bf16[256,4096]{1,0:T(8,128)(2,1)} fusion(bf16[4096,512]{1,0:T(8,128)(2,1)} %param.11, bf16[32,8,4,128]{3,2,1,0:T(4,128)(2,1)S(1)} %bitcast.57), kind=kOutput, calls=%fused_computation.6 | convolution fusion | flops 1074790400 | bytes 6553600 | tf_op jit(solution)/shard_map/dot_general | solution.py:102
  158.2 30.4 %reduce-scatter.6.cloned.1.call-done = bf16[2,128,896]{2,1,0:T(8,128)(2,1)} async-done(((bf16[16,128,896]{2,1,0:T(8,128)(2,1)}), bf16[2,128,896]{2,1,0:T(8,128)(2,1)}) %reduce-scatter.6.cloned.1.call-update) | async-done | bytes 458768 | tf_op jit(solution)/shard_map/reduce_scatter | solution.py:124
  188.6 11.6 %convolution_convert_fusion = bf16[96,128,896]{2,0,1:T(8,128)(2,1)} fusion(bf16[2,128,896]{2,1,0:T(8,128)(2,1)} %reduce-scatter.6.cloned.1.call-done, s32[2]{0:T(128)S(1)} %broadcast_select_fusion.1), kind=kOutput, calls=%fused_computation.4 | convolution fusion | flops 55050432 | bytes 22478856 | tf_op jit(solution)/shard_map/bs,srd->brd/dot_general | solution.py:133
  200.2 23.7 %reduce-scatter.4.cloned.1.call-done = bf16[256,512]{1,0:T(8,128)(2,1)} async-done(((bf16[256,4096]{1,0:T(8,128)(2,1)}), bf16[256,512]{1,0:T(8,128)(2,1)}) %reduce-scatter.4.cloned.1.call-update) | async-done | bytes 262160 | tf_op jit(solution)/shard_map/reduce_scatter | solution.py:108
  224.8 3.4 collective-permute-start.2
  229.2 3.9 %collective-permute-done.2 = bf16[63,512]{1,0:T(8,128)(2,1)S(1)} collective-permute-done((bf16[63,512]{1,0:T(8,128)(2,1)S(1)}, bf16[63,512]{1,0:T(8,128)(2,1)S(1)}, u32[]{:S(2)}, u32[]{:S(2)}) %collective-permute-start.2) | collective-permute-done | bytes 64544 | tf_op jit(solution)/shard_map/ppermute | solution.py:16
  234.0 129.1 %reduce-scatter.8.cloned.1.call-done = bf16[96,8,896]{2,0,1:T(8,128)(2,1)} async-done(((bf16[96,128,896]{2,0,1:T(8,128)(2,1)}), bf16[96,8,896]{2,0,1:T(8,128)(2,1)}) %reduce-scatter.8.cloned.1.call-update) | async-done | bytes 1376272 | tf_op jit(solution)/shard_map/reduce_scatter | solution.py:134
  363.1 3.3 copy.91
  (84 shorter events, 30.2 us)
Async XLA Ops:
  7.2 30.4 %copy-start.3 = (bf16[896,512]{1,0:T(8,128)(2,1)S(1)}, bf16[896,512]{1,0:T(8,128)(2,1)}, u32[]{:S(2)}) copy-start(bf16[896,512]{1,0:T(8,128)(2,1)} %param.12) | copy-start | bytes 2752516
  7.2 30.5 %copy-start.4 = (bf16[896,512]{1,0:T(8,128)(2,1)S(1)}, bf16[896,512]{1,0:T(8,128)(2,1)}, u32[]{:S(2)}) copy-start(bf16[896,512]{1,0:T(8,128)(2,1)} %param.13) | copy-start | bytes 2752516
  7.2 37.7 %all-gather.6.cloned.1.call-start = ((), (), s32[]{:S(2)}) async-start(), calls=%async_computation.4 | async-start | bytes 2359296 | tf_op jit(solution)/shard_map/all_gather | solution.py:36
  8.2 6.8 %collective-permute-start = (bf16[63,512]{1,0:T(8,128)(2,1)S(1)}, bf16[63,512]{1,0:T(8,128)(2,1)S(1)}, u32[]{:S(2)}, u32[]{:S(2)}) collective-permute-start(bf16[63,512]{1,0:T(8,128)(2,1)S(1)} %slice.28), channel_id=1, source_target_pairs={{8,0},{16,8},{24,16},{32,24},{40,32},{48,40},{56,48},{64,56},{72,6... | collective-permute-start | bytes 193544 | tf_op jit(solution)/shard_map/ppermute | solution.py:16
  15.7 56.6 %all-gather.8.cloned.1.call-start = ((), (), s32[]{:S(2)}) async-start(), calls=%async_computation.5 | async-start | bytes 2359296 | tf_op jit(solution)/shard_map/all_gather | solution.py:37
  16.6 8.3 %collective-permute-start.1 = (bf16[63,512]{1,0:T(8,128)(2,1)S(1)}, bf16[63,512]{1,0:T(8,128)(2,1)S(1)}, u32[]{:S(2)}, u32[]{:S(2)}) collective-permute-start(bf16[63,512]{1,0:T(8,128)(2,1)S(1)} %slice.30), channel_id=1, source_target_pairs={{8,0},{16,8},{24,16},{32,24},{40,32},{48,40},{56,48},{64,56},{72,6... | collective-permute-start | bytes 193544 | tf_op jit(solution)/shard_map/ppermute | solution.py:16
  25.6 79.5 %all-gather.4.cloned.1.call-start = ((), (), s32[]{:S(2)}) async-start(), calls=%async_computation.3 | async-start | bytes 4128768 | tf_op jit(solution)/shard_map/all_gather | solution.py:61
  37.1 151.5 %reduce-scatter.6.cloned.1.call-start = ((), (), s32[]{:S(2)}) async-start(), calls=%async_computation.7 | async-start | bytes 4128768 | tf_op jit(solution)/shard_map/reduce_scatter | solution.py:124
  37.8 1.2 copy-start.5
  49.1 56.1 %copy-start.6 = (bf16[896,1024]{1,0:T(8,128)(2,1)S(1)}, bf16[896,1024]{1,0:T(8,128)(2,1)}, u32[]{:S(2)}) copy-start(bf16[896,1024]{1,0:T(8,128)(2,1)} %copy-done.5) | copy-start | bytes 5505028
  130.7 0.8 copy-start
  138.5 2.8 copy-start.7
  151.6 1.0 copy-start.1
  151.6 72.3 %reduce-scatter.4.cloned.1.call-start = ((), (), s32[]{:S(2)}) async-start(), calls=%async_computation.6 | async-start | bytes 2359296 | tf_op jit(solution)/shard_map/reduce_scatter | solution.py:108
  158.2 204.9 %reduce-scatter.8.cloned.1.call-start = ((), (), s32[]{:S(2)}) async-start(), calls=%async_computation.8 | async-start | bytes 23396352 | tf_op jit(solution)/shard_map/reduce_scatter | solution.py:134
  200.2 32.9 %copy-start.2 = (bf16[256,512]{1,0:T(8,128)(2,1)S(1)}, bf16[256,512]{1,0:T(8,128)(2,1)}, u32[]{:S(2)}) copy-start(bf16[256,512]{1,0:T(8,128)(2,1)} %param.10) | copy-start | bytes 786436
  224.8 8.3 %collective-permute-start.2 = (bf16[63,512]{1,0:T(8,128)(2,1)S(1)}, bf16[63,512]{1,0:T(8,128)(2,1)S(1)}, u32[]{:S(2)}, u32[]{:S(2)}) collective-permute-start(bf16[63,512]{1,0:T(8,128)(2,1)S(1)} %slice.42), channel_id=1, source_target_pairs={{0,8},{8,16},{16,24},{24,32},{32,40},{40,48},{48,56},{56,64},{64,7... | collective-permute-start | bytes 193544 | tf_op jit(solution)/shard_map/ppermute | solution.py:16
Sparse Core Ops, SparseCore 0:
  15.8 29.0 all-gather.5
  46.6 25.6 all-gather.7
  74.6 30.5 all-gather.3
  151.7 36.7 reduce-scatter.5
  191.4 32.4 reduce-scatter.3
  227.3 135.7 reduce-scatter.7
where the time goes:
time: 375 us; the launch traced here: 373 us
  waiting for transfers between devices  246 us (66%)
  matrix products  47.4 us (13%)
  local copies, waits for them, and re-layouts  38.3 us (10%)
  starting transfers between devices  15.1 us (4%)
  between operations  14.4 us (4%)
  other arithmetic  12 us (3%)
    reduce_scatter x1, waiting for transfers between devices, per_device(): lax.psum_scatter(dense.astype(jnp.bfloat16), 'ctx', scatter_dimension=1,...  129 us
    reduce_scatter x1, waiting for transfers between devices, per_device(): lax.psum_scatter(jnp.where(live[:, None, None], term, 0.0).astype(jnp.bfl...  30.4 us
    all_gather x1, waiting for transfers between devices, per_device(): piece = lax.all_gather(outgoing, 'db', axis=0, tiled=True)  28 us
    reduce_scatter x1, waiting for transfers between devices, per_device(): lax.psum_scatter(cross_part.astype(jnp.bfloat16), 'db', scatter_dimension...  23.7 us
    all_gather x1, waiting for transfers between devices, per_device(): lax.all_gather(att_cotangent, 'db', axis=1, tiled=True)  23.3 us
    ppermute x3, starting transfers between devices, passed_along(): return lax.ppermute(shard, axis, pairs)  14.6 us
    dot_general x1, matrix products, per_device(): jnp.einsum('bs,srd->brd', table, slot_grads, precision=lax.Precision.HIGH...  11.6 us
    gather x1, local copies, waits for them, and re-layouts, per_device(): jnp.take(database, owned_row, axis=0)  8.19 us
  transfers between devices with their start and end apart: 9, of which 9 were waited for; matrix products, arithmetic and copies ran while one was open for 12% of the time, Pallas kernels for 0%

commit v1 on v0

v1 whole, which is shorter than its diff:
```python
import functools

import jax
import jax.numpy as jnp
from jax import lax
from jax.experimental import pallas as pl
from jax.experimental.pallas import tpu as pltpu
from jax.sharding import PartitionSpec as P

HDIM = 128
DE = 896
CH = 64
R = 128
K = 2
CAP = 2
BORDER = CH - 1
SCALE = HDIM ** (-0.5)
BF16, F32 = jnp.bfloat16, jnp.float32
NT = (((1,), (1,)), ((), ()))
TN = (((0,), (0,)), ((), ()))
PLACES = (0, 1, 3, 2)
VMEM = pl.BlockSpec(memory_space=pltpu.VMEM)
SMEM = pl.BlockSpec(memory_space=pltpu.SMEM)
ANY = pl.BlockSpec(memory_space=pl.ANY)


def up(x):
    return lax.ppermute(x, "db", [(s, (s + 2) % 8) for s in range(8)])


def down(x):
    return lax.ppermute(x, "db", [(s, (s - 2) % 8) for s in range(8)])


def across(x):
    return lax.ppermute(x, "db", [(s, s ^ 1) for s in range(8)])


def along_ctx(x, by):
    peers = lax.axis_size("ctx")
    return lax.ppermute(x, "ctx", [(i, i + by) for i in range(peers) if 0 <= i + by < peers])


def shape(dims, dtype=BF16):
    return jax.ShapeDtypeStruct(dims, dtype)


def cost(flops, size):
    return pl.CostEstimate(flops=flops, bytes_accessed=size, transcendentals=0)


def source_of(me, core, place):
    return lax.rem(me // 2 + place, 4) * 2 + (lax.rem(me, 2) + core) % 2


def pack_kernel(a_ref, b_ref, out_ref, sems):
    copies = [
        pltpu.make_async_copy(ref, out_ref.at[at], sems.at[at])
        for at, ref in enumerate((a_ref, b_ref))
    ]
    for copy in copies:
        copy.start()
    for copy in copies:
        copy.wait()


def named(shards, shard):
    count, found = jnp.int32(0), [jnp.int32(0)] * CAP
    for c in range(shards.shape[1]):
        for k in range(K):
            mine = shards[k, c] == shard
            for at in range(CAP):
                found[at] = jnp.where(mine & (count == at), c * K + k, found[at])
            count = count + mine.astype(jnp.int32)
    return found, count


def fetch_kernel(shard_ref, row_ref, database_ref, out_ref, sems):
    found, _ = named(shard_ref, lax.axis_index("db"))
    copies = [
        pltpu.make_async_copy(
            database_ref.at[row_ref[lax.rem(request, K), request // K]],
            out_ref.at[slot],
            sems.at[slot],
        )
        for slot, request in enumerate(found)
    ]
    for copy in copies:
        copy.start()
    for copy in copies:
        copy.wait()


def project_kernel(item, *refs):
    blocks, w_ref, out_ref, full = refs[:8], refs[8], refs[9], refs[10]
    me = lax.axis_index("db")
    width = w_ref.shape[1 - item]
    for index, block in enumerate(blocks):
        core, place = index // 4, PLACES[index % 4]
        spot = pl.multiple_of(source_of(me, core, place) * width, width)
        full[:, pl.ds(spot, width)] = block[...] if place == 2 else block[item]
    rows = full.shape[0]
    if item:
        total = lax.dot_general(full[...], w_ref[...], NT, preferred_element_type=F32)
    else:
        total = jnp.dot(full[...], w_ref[...], preferred_element_type=F32)
    out_ref[...] = pltpu.roll(total, rows - BORDER, 0).astype(BF16)


def attend_kernel(*refs):
    shard_ref, q_ref, q_tail, g_ref, g_tail = refs[:5]
    mems = refs[5:15]
    wk_ref, wv_ref = refs[15:17]
    gq_ref, gk_ref, gv_ref = refs[17:20]
    q_s, g_s, mem_s, k_s, v_s, gq_s = refs[20:]
    me = lax.axis_index("db")
    my_z, my_core = me // 2, lax.rem(me, 2)
    rows, width = q_ref.shape
    spans, heads = rows // CH, width // HDIM
    last = rows - CH
    first_row = lax.broadcasted_iota(jnp.int32, (CH, width), 0) == 0
    for src, tail, dst in ((q_ref, q_tail, q_s), (g_ref, g_tail, g_s)):
        dst[:last] = src[:last]
        dst[last:] = jnp.where(first_row, src[last:], tail[...])

    for c in range(spans):
        for k in range(K):
            request = c * K + k
            shard = shard_ref[k, c]
            rank = jnp.int32(0)
            for earlier in range(request):
                same = shard_ref[earlier % K, earlier // K] == shard
                rank = rank + same.astype(jnp.int32)
            rank = jnp.minimum(rank, CAP - 1)
            core = (lax.rem(shard, 2) + my_core) % 2
            place = lax.rem(shard // 2 - my_z + 4, 4)
            spot = pl.ds(request * R, R)
            for which in range(2):
                own, nxt, prv, far0, far1 = mems[which * 5 : which * 5 + 5]
                here = core == which
                for at, ref in ((0, own), (1, nxt), (3, prv)):

                    @pl.when(here & (place == at))
                    def _(ref=ref, rank=rank, spot=spot):
                        mem_s[spot, :] = ref[rank]

                for at, ref in ((0, far0), (1, far1)):

                    @pl.when(here & (place == 2) & (rank == at))
                    def _(ref=ref, spot=spot):
                        mem_s[spot, :] = ref[...]

    k_s[...] = jnp.dot(mem_s[...], wk_ref[...], preferred_element_type=F32).astype(BF16)
    v_s[...] = jnp.dot(mem_s[...], wv_ref[...], preferred_element_type=F32).astype(BF16)
    for c in range(spans):
        span, memory = pl.ds(c * CH, CH), pl.ds(c * K * R, K * R)
        at = [pl.ds(h * HDIM, HDIM) for h in range(heads)]
        q, g = [q_s[span, x] for x in at], [g_s[span, x] for x in at]
        k, v = [k_s[memory, x] for x in at], [v_s[memory, x] for x in at]
        some = range(heads)
        scores = [
            lax.dot_general(q[h], k[h], NT, preferred_element_type=F32) * SCALE for h in some
        ]
        dattention = [lax.dot_general(g[h], v[h], NT, preferred_element_type=F32) for h in some]
        raised = [jnp.exp(x - jnp.max(x, -1, keepdims=True)) for x in scores]
        attention = [x / jnp.sum(x, -1, keepdims=True) for x in raised]
        mean = [jnp.sum(attention[h] * dattention[h], -1, keepdims=True) for h in some]
        dscores = [(attention[h] * (dattention[h] - mean[h])).astype(BF16) for h in some]
        for h in some:
            gq_s[span, at[h]] = jnp.dot(dscores[h], k[h], preferred_element_type=F32) * SCALE
        for h in some:
            gk = lax.dot_general(dscores[h], q[h], TN, preferred_element_type=F32) * SCALE
            gk_ref[memory, at[h]] = gk.astype(BF16)
        for h in some:
            gv = lax.dot_general(
                attention[h].astype(BF16), g[h], TN, preferred_element_type=F32
            )
            gv_ref[memory, at[h]] = gv.astype(BF16)
    gq_ref[...] = pltpu.roll(gq_s[...], BORDER, 0).astype(BF16)


def term_kernel(core, shard_ref, gk_ref, gv_ref, wk_ref, wv_ref, out_ref):
    me = lax.axis_index("db")
    for place in range(4):
        found, count = named(shard_ref, source_of(me, core, place))
        for slot, request in enumerate(found):

            @pl.when(count > slot)
            def _(place=place, slot=slot, request=request):
                spot = pl.ds(pl.multiple_of(request * R, R), R)
                term = lax.dot_general(gk_ref[spot], wk_ref[...], NT, preferred_element_type=F32)
                term = term + lax.dot_general(
                    gv_ref[spot], wv_ref[...], NT, preferred_element_type=F32
                )
                out_ref[place, slot] = term.astype(BF16)


def cross_kernel(gq_ref, head_ref, w_ref, away_ref, own_ref, full):
    me = lax.axis_index("db")
    rows, width = gq_ref.shape
    last_row = lax.broadcasted_iota(jnp.int32, (CH, width), 0) == CH - 1
    full[:CH] = jnp.where(last_row, gq_ref[:CH], head_ref[...])
    full[CH:] = gq_ref[CH:]
    for core, out in ((1, away_ref), (0, own_ref)):
        for place in range(4):
            spot = pl.multiple_of(source_of(me, core, place) * width, width)
            out[place] = lax.dot_general(
                full[...], w_ref[pl.ds(spot, width), :], NT, preferred_element_type=F32
            ).astype(BF16)


def scatter_kernel(requests, ids_ref, parts_ref, out_ref):
    me = lax.axis_index("db")
    out_ref[...] = jnp.zeros_like(out_ref)

    def group(i, carry):
        count = jnp.int32(0)
        for r in range(requests):
            mine = ids_ref[i, 0, r] == me
            row = ids_ref[i, 0, requests + r]
            slot = jnp.minimum(count, CAP - 1)

            @pl.when(mine)
            def _(row=row, slot=slot):
                out_ref[row] += parts_ref[i * CAP + slot].astype(F32)

            count = count + mine.astype(jnp.int32)
        return carry

    lax.fori_loop(0, ids_ref.shape[0], group, 0)


def gather_blocks(own, early=None):
    nxt, prv = down(own), up(own)
    if early is not None:
        nxt, prv, _ = lax.optimization_barrier((nxt, prv, early))
    far_a, far_b = up(prv[0]), down(nxt[1])
    here = (own, nxt, prv, far_a, far_b)
    return here + tuple(across(x) for x in here)


def add(a, b):
    return (a.astype(F32) + b.astype(F32)).astype(BF16)


def reduce_blocks(own, away, halves):
    got = across(away)
    far_a, far_b = (add(x, y) for x, y in zip(halves(own[2]), halves(got[2])))
    via_up, via_down = up(far_a), down(far_b)
    nxt_a, nxt_b = (add(x, y) for x, y in zip(halves(own[1]), halves(got[1])))
    prv_a, prv_b = (add(x, y) for x, y in zip(halves(own[3]), halves(got[3])))
    nxt = jnp.concatenate([add(nxt_a, via_up), nxt_b], 0)
    prv = jnp.concatenate([prv_a, add(prv_b, via_down)], 0)
    from_prv, from_nxt = up(nxt), down(prv)
    return (own[0].astype(F32) + got[0].astype(F32)) + (
        from_prv.astype(F32) + from_nxt.astype(F32)
    )


def per_device(
    states, cotangent, w_query, w_key, w_value, w_out, database, neighbour_shard, neighbour_row
):
    rows, width = states.shape
    spans = rows // CH
    limit = pltpu.CompilerParams(vmem_limit_bytes=20 * 2**20)
    shards, named_rows = neighbour_shard.T, neighbour_row.T
    peers = lax.axis_size("ctx")

    pair = pl.pallas_call(
        pack_kernel,
        name="pack",
        out_shape=shape((2, rows, width)),
        in_specs=[ANY, ANY],
        out_specs=VMEM,
        scratch_shapes=[pltpu.SemaphoreType.DMA((2,))],
    )(states, cotangent)
    tokens = gather_blocks(pair)
    fetched = pl.pallas_call(
        fetch_kernel,
        name="fetch",
        out_shape=shape((CAP, R, DE)),
        in_specs=[SMEM, SMEM, ANY],
        out_specs=VMEM,
        scratch_shapes=[pltpu.SemaphoreType.DMA((CAP,))],
    )(shards, named_rows, database)
    ids = jnp.concatenate([neighbour_shard.reshape(1, -1), neighbour_row.reshape(1, -1)], 1)
    ids = jnp.pad(ids, ((0, 0), (0, 128 - ids.shape[1])))
    ids = lax.all_to_all(jnp.broadcast_to(ids, (peers, 1, 128)), "ctx", 0, 0, tiled=True)
    memory = gather_blocks(fetched, ids)

    def project(item, w, name):
        blocks = tokens[:3] + tokens[3 + item : 4 + item]
        blocks = blocks + tokens[5:8] + tokens[8 + item : 9 + item]
        return pl.pallas_call(
            functools.partial(project_kernel, item),
            name=name,
            out_shape=shape((rows, width)),
            in_specs=[VMEM] * 9,
            out_specs=VMEM,
            scratch_shapes=[pltpu.VMEM((rows, 8 * width), BF16)],
            compiler_params=limit,
            cost_estimate=cost(2 * rows * width * 8 * width, 16 * rows * width + 16 * width * width),
        )(*blocks, w)

    query = project(0, w_query, "query")
    query_tail = along_ctx(query[rows - CH :], -1)
    grad_out = project(1, w_out, "grad_out")
    grad_tail = along_ctx(grad_out[rows - CH :], -1)
    requests = spans * K
    grad_query, grad_keys, grad_values = pl.pallas_call(
        attend_kernel,
        name="attend",
        out_shape=(shape((rows, width)),) + (shape((requests * R, width)),) * 2,
        in_specs=[SMEM] + [VMEM] * 16,
        out_specs=(VMEM,) * 3,
        scratch_shapes=[
            pltpu.VMEM((rows, width), BF16),
            pltpu.VMEM((rows, width), BF16),
            pltpu.VMEM((requests * R, DE), BF16),
            pltpu.VMEM((requests * R, width), BF16),
            pltpu.VMEM((requests * R, width), BF16),
            pltpu.VMEM((rows, width), F32),
        ],
        compiler_params=limit,
        cost_estimate=cost(8 * requests * R * DE * width, 2**23),
    )(shards, query, query_tail, grad_out, grad_tail, *memory, w_key, w_value)
    head = along_ctx(grad_query[:CH], 1)

    def term(core, name):
        return pl.pallas_call(
            functools.partial(term_kernel, core),
            name=name,
            out_shape=shape((4, CAP, R, DE)),
            in_specs=[SMEM] + [VMEM] * 4,
            out_specs=VMEM,
            compiler_params=limit,
            cost_estimate=cost(2 * requests * R * DE * width, 2**22),
        )(shards, grad_keys, grad_values, w_key, w_value)

    away, own = term(1, "term_away"), term(0, "term_own")
    slots = reduce_blocks(own, away, lambda x: (x[:1], x[1:])).astype(BF16)
    cross_away, cross_own = pl.pallas_call(
        cross_kernel,
        name="cross",
        out_shape=(shape((4, rows, width)), shape((4, rows, width))),
        in_specs=[VMEM] * 3,
        out_specs=(VMEM, VMEM),
        scratch_shapes=[pltpu.VMEM((rows, width), BF16)],
        compiler_params=limit,
        cost_estimate=cost(2 * rows * width * 8 * width, 2**23),
    )(grad_query, head, w_query)
    half = rows // 2
    cross = reduce_blocks(cross_own, cross_away, lambda x: (x[:half], x[half:]))
    grad_states = cotangent.astype(F32) + cross

    block = R // peers
    spread = slots.reshape(CAP, peers, block, DE).transpose(1, 0, 2, 3)
    parts = lax.all_to_all(spread, "ctx", 0, 0, tiled=True).reshape(peers * CAP, block, DE)
    grad_database = pl.pallas_call(
        functools.partial(scatter_kernel, requests),
        name="scatter",
        out_shape=shape((database.shape[0], block, DE), F32),
        in_specs=[SMEM, VMEM],
        out_specs=VMEM,
        compiler_params=limit,
    )(ids, parts)
    return grad_states, grad_database


def solution(mesh):
    in_specs = (
        P("ctx", "db"),
        P("ctx", "db"),
        P(None, "db"),
        P(None, "db"),
        P(None, "db"),
        P("db", None),
        P("db", None, None),
        P("ctx", None),
        P("ctx", None),
    )
    out_specs = (P("ctx", "db"), P("db", "ctx", None))
    return jax.shard_map(
        per_device, mesh=mesh, in_specs=in_specs, out_specs=out_specs, check_vma=False
    )
```

time: 375 us -> 131 us (0.35)
  waiting for transfers between devices: 246 us -> 43.1 us
  matrix products: 47.4 us -> 0 us
  starting transfers between devices: 15.1 us -> 50.2 us
  local copies, waits for them, and re-layouts: 38.3 us -> 4.03 us
  Pallas kernels: 0 us -> 25.5 us
  between operations: 14.4 us -> 1.02 us
  other arithmetic: 12 us -> 5.26 us
    reduce_scatter x3 -> x0, waiting for transfers between devices: 183 us -> none  [the longest x1 129 us: per_device(): lax.psum_scatter(dense.astype(jnp.bfloat16), 'ctx', scatter_dimension=1,...]
    all_gather x3 -> x0, waiting for transfers between devices: 57 us -> none  [the longest x1 28 us: per_device(): piece = lax.all_gather(outgoing, 'db', axis=0, tiled=True)]
    dot_general x11 -> x0, matrix products: 47.4 us -> none  [the longest x1 11.6 us: per_device(): jnp.einsum('bs,srd->brd', table, slot_grads, precision=lax.Precision.HIGH...]
    pallas_call x0 -> x9, Pallas kernels: none -> 25.5 us  [the longest x2 6.9 us: term(): pl.pallas_call(functools.partial(term_kernel, core), name=name, out_shape...]
    ppermute x3 -> x31, waiting for transfers between devices: 5.71 us -> 30.4 us  [the longest x8 17 us: up(): return lax.ppermute(x, 'db', [(s, (s + 2) % 8) for s in range(8)])]
    ppermute x3 -> x31, starting transfers between devices: 14.6 us -> 36.5 us  [the longest x8 24.8 us: down(): return lax.ppermute(x, 'db', [(s, (s - 2) % 8) for s in range(8)])]
    gather x3 -> x0, local copies, waits for them, and re-layouts: 13.8 us -> none  [the longest x1 8.19 us: per_device(): jnp.take(database, owned_row, axis=0)]
    all_to_all x0 -> x2, starting transfers between devices: none -> 13.7 us  [the longest x1 7.48 us: per_device(): lax.all_to_all(jnp.broadcast_to(ids, (peers, 1, 128)), 'ctx', 0, 0, tiled...]
  transfers between devices with their start and end apart: 9 -> 33, of which waited for: 9 -> 11; matrix products, arithmetic and copies ran while one was open for 12% -> 5% of each run, Pallas kernels for 0% -> 7%
where the time goes in v1:
time: 131 us; the launch traced here: 129 us
  starting transfers between devices  50.2 us (38%)
  waiting for transfers between devices  43.1 us (33%)
  Pallas kernels  25.5 us (19%)
  other arithmetic  5.26 us (4%)
  local copies, waits for them, and re-layouts  4.03 us (3%)
    ppermute x8, starting transfers between devices, down(): return lax.ppermute(x, 'db', [(s, (s - 2) % 8) for s in range(8)])  24.8 us
    ppermute x8, waiting for transfers between devices, up(): return lax.ppermute(x, 'db', [(s, (s + 2) % 8) for s in range(8)])  17 us
    ppermute x3, waiting for transfers between devices, along_ctx(): lax.ppermute(x, 'ctx', [(i, i + by) for i in range(peers) if 0 <= i + by...  10 us
    ppermute x3, starting transfers between devices, along_ctx(): lax.ppermute(x, 'ctx', [(i, i + by) for i in range(peers) if 0 <= i + by...  9.47 us
    all_to_all x1, starting transfers between devices, per_device(): lax.all_to_all(jnp.broadcast_to(ids, (peers, 1, 128)), 'ctx', 0, 0, tiled...  7.48 us
    pallas_call x2, Pallas kernels, term(): pl.pallas_call(functools.partial(term_kernel, core), name=name, out_shape...  6.9 us
    all_to_all x1, waiting for transfers between devices, per_device(): lax.all_to_all(spread, 'ctx', 0, 0, tiled=True)  6.71 us
    pallas_call x1, Pallas kernels, per_device(): pl.pallas_call(attend_kernel, name='attend', out_shape=(shape((rows, widt...  6.24 us
  transfers between devices with their start and end apart: 33, of which 11 were waited for; matrix products, arithmetic and copies ran while one was open for 5% of the time, Pallas kernels for 7%

profile of v1, /device:TPU:2, one launch (start us, length us, event | category | flops | bytes accessed | tf_op | source)
XLA Modules:
  0.0 129.1 jit_solution(10276876638054582206)
XLA Ops:
  0.7 2.7 %fetch.1.refs_5_ = bf16[2,128,896]{2,1,0:T(8,128)(2,1)} custom-call(s32[2,4]{1,0:T(2,128)} %bitcast.66, s32[2,4]{1,0:T(2,128)} %bitcast.70, bf16[96,128,896]{2,1,0:T(8,128)(2,1)} %database_ref.1), custom_call_target="tpu_custom_call" | custom-call | tf_op jit(solution)/shard_map/fetch/pallas_call | solution.py:278
  3.4 4.1 %collective-permute-start.11 = (bf16[2,128,896]{2,1,0:T(8,128)(2,1)}, bf16[2,128,896]{2,1,0:T(8,128)(2,1)S(1)}, u32[]{:S(2)}, u32[]{:S(2)}) collective-permute-start(bf16[2,128,896]{2,1,0:T(8,128)(2,1)} %fetch.1.refs_5_), channel_id=1, source_target_pairs={{0,6},{1,7},{2,0},{3,1},{4,2},{5,3},{6,4},{7,5},{8,14},{9,15},{10,... | collective-permute-start | bytes 1376264 | tf_op jit(solution)/shard_map/ppermute | solution.py:32
  9.3 3.3 %collective-permute-start = (bf16[2,256,512]{2,1,0:T(8,128)(2,1)}, bf16[2,256,512]{2,1,0:T(8,128)(2,1)S(1)}, u32[]{:S(2)}, u32[]{:S(2)}) collective-permute-start(bf16[2,256,512]{2,1,0:T(8,128)(2,1)} %pack.1.refs_0_), channel_id=1, source_target_pairs={{0,6},{1,7},{2,0},{3,1},{4,2},{5,3},{6,4},{7,5},{8,14},{9,15},{10,... | collective-permute-start | bytes 1572872 | tf_op jit(solution)/shard_map/ppermute | solution.py:32
  13.7 7.5 %all-to-all-start = ((s32[16,1,128]{2,1,0:T(1,128)}), s32[16,1,128]{2,1,0:T(1,128)S(1)}, u32[]{:S(2)}, u32[]{:S(2)}) async-start(s32[16,1,128]{2,1,0:T(1,128)} %broadcast_in_dim.3), calls=%async_computation | async-start | bytes 16384 | tf_op jit(solution)/shard_map/all_to_all | solution.py:288
  21.2 6.0 %all-to-all-done.ids_ref = s32[16,1,128]{2,1,0:T(1,128)S(1)} async-done(((s32[16,1,128]{2,1,0:T(1,128)}), s32[16,1,128]{2,1,0:T(1,128)S(1)}, u32[]{:S(2)}, u32[]{:S(2)}) %all-to-all-start) | async-done | bytes 8224 | tf_op jit(solution)/shard_map/all_to_all | solution.py:288
  28.8 3.7 %collective-permute-start.8 = (bf16[256,512]{1,0:T(8,128)(2,1)S(1)}, bf16[256,512]{1,0:T(8,128)(2,1)S(1)}, u32[]{:S(2)}, u32[]{:S(2)}) collective-permute-start(bf16[256,512]{1,0:T(8,128)(2,1)S(1)} %slice_bitcast_fusion), channel_id=1, source_target_pairs={{0,6},{1,7},{2,0},{3,1},{4,2},{5,3},{6,4},{7,5},{8,14},{9,15},{10,... | collective-permute-start | bytes 786440 | tf_op jit(solution)/shard_map/ppermute | solution.py:32
  34.3 4.2 %collective-permute-done.13.refs_8_ = bf16[128,896]{1,0:T(8,128)(2,1)S(1)} collective-permute-done((bf16[128,896]{1,0:T(8,128)(2,1)S(1)}, bf16[128,896]{1,0:T(8,128)(2,1)S(1)}, u32[]{:S(2)}, u32[]{:S(2)}) %collective-permute-start.13) | collective-permute-done | bytes 229408 | tf_op jit(solution)/shard_map/ppermute | solution.py:28
  39.0 3.7 %collective-permute-done.2.refs_3_ = bf16[256,512]{1,0:T(8,128)(2,1)S(1)} collective-permute-done((bf16[256,512]{1,0:T(8,128)(2,1)S(1)}, bf16[256,512]{1,0:T(8,128)(2,1)S(1)}, u32[]{:S(2)}, u32[]{:S(2)}) %collective-permute-start.2) | collective-permute-done | bytes 262176 | tf_op jit(solution)/shard_map/ppermute | solution.py:28
  45.6 2.2 %copy-done.2 = bf16[512,4096]{1,0:T(8,128)(2,1)S(1)} copy-done((bf16[512,4096]{1,0:T(8,128)(2,1)S(1)}, bf16[512,4096]{1,0:T(8,128)(2,1)}, u32[]{:S(2)}) %copy-start.2) | copy-done | bytes 4194328
  51.5 4.9 %collective-permute-start.10 = (bf16[64,512]{1,0:T(8,128)(2,1)S(1)}, bf16[64,512]{1,0:T(8,128)(2,1)S(1)}, u32[]{:S(2)}, u32[]{:S(2)}) collective-permute-start(bf16[64,512]{1,0:T(8,128)(2,1)S(1)} %slice.203), channel_id=1, source_target_pairs={{8,0},{16,8},{24,16},{32,24},{40,32},{48,40},{56,48},{64,56},{72,6... | collective-permute-start | bytes 196616 | tf_op jit(solution)/shard_map/ppermute | solution.py:41
  56.4 2.7 %collective-permute-start.7 = (bf16[64,512]{1,0:T(8,128)(2,1)S(1)}, bf16[64,512]{1,0:T(8,128)(2,1)S(1)}, u32[]{:S(2)}, u32[]{:S(2)}) collective-permute-start(bf16[64,512]{1,0:T(8,128)(2,1)S(1)} %slice.201), channel_id=1, source_target_pairs={{8,0},{16,8},{24,16},{32,24},{40,32},{48,40},{56,48},{64,56},{72,6... | collective-permute-start | bytes 196616 | tf_op jit(solution)/shard_map/ppermute | solution.py:41
  59.1 3.5 %collective-permute-done.7.refs_2_ = bf16[64,512]{1,0:T(8,128)(2,1)S(1)} collective-permute-done((bf16[64,512]{1,0:T(8,128)(2,1)S(1)}, bf16[64,512]{1,0:T(8,128)(2,1)S(1)}, u32[]{:S(2)}, u32[]{:S(2)}) %collective-permute-start.7) | collective-permute-done | bytes 65568 | tf_op jit(solution)/shard_map/ppermute | solution.py:41
  62.5 6.2 %attend.1 = (bf16[256,512]{1,0:T(8,128)(2,1)S(1)}, bf16[1024,512]{1,0:T(8,128)(2,1)S(1)}, bf16[1024,512]{1,0:T(8,128)(2,1)S(1)}) custom-call(s32[2,4]{1,0:T(2,128)S(1)} %bitcast.67, bf16[256,512]{1,0:T(8,128)(2,1)S(1)} %query.1.refs_1_, bf16[64,512]{1,0:T(8,128)(2,1)S(1)} %collective-permute-done.7.refs_2_, bf16[256,512]{1,0:T(8,128)(2,1)S(1)} %grad_out.1.refs_3_, ...), custom_call_target="tpu_custom_call" | custom-call | flops 3758096384 | bytes 8388608 | tf_op jit(solution)/shard_map/attend/pallas_call | solution.py:310
  68.8 4.1 %term_away.1 = bf16[4,2,128,896]{3,2,1,0:T(8,128)(2,1)S(1)} custom-call(s32[2,4]{1,0:T(2,128)S(1)} %bitcast.68, bf16[1024,512]{1,0:T(8,128)(2,1)S(1)} %get-tuple-element.14.gk_ref, bf16[1024,512]{1,0:T(8,128)(2,1)S(1)} %get-tuple-element.15.gv_ref, bf16[896,512]{1,0:T(8,128)(2,1)S(1)} %copy-done.3, bf16[896,512]{1,0:T(8,128)(2,1)S(1)} %copy-done.4), custom_call_target="tpu_custom_call" | custom-call | flops 939524096 | bytes 4194304 | tf_op jit(solution)/shard_map/term_away/pallas_call | solution.py:330
  75.0 6.5 %collective-permute-done.20.head_ref = bf16[64,512]{1,0:T(8,128)(2,1)S(1)} collective-permute-done((bf16[64,512]{1,0:T(8,128)(2,1)S(1)}, bf16[64,512]{1,0:T(8,128)(2,1)S(1)}, u32[]{:S(2)}, u32[]{:S(2)}) %collective-permute-start.20) | collective-permute-done | bytes 65568 | tf_op jit(solution)/shard_map/ppermute | solution.py:41
  82.9 2.8 %term_own.1 = bf16[4,2,128,896]{3,2,1,0:T(8,128)(2,1)S(1)} custom-call(s32[2,4]{1,0:T(2,128)S(1)} %bitcast.69, bf16[1024,512]{1,0:T(8,128)(2,1)S(1)} %get-tuple-element.14.gk_ref, bf16[1024,512]{1,0:T(8,128)(2,1)S(1)} %get-tuple-element.15.gv_ref, bf16[896,512]{1,0:T(8,128)(2,1)S(1)} %copy-done.3, bf16[896,512]{1,0:T(8,128)(2,1)S(1)} %copy-done.4), custom_call_target="tpu_custom_call" | custom-call | flops 939524096 | bytes 4194304 | tf_op jit(solution)/shard_map/term_own/pallas_call | solution.py:330
  86.0 3.2 %collective-permute-start.29 = (bf16[1,128,896]{2,1,0:T(8,128)(2,1)S(1)}, bf16[1,128,896]{2,1,0:T(8,128)(2,1)S(1)}, u32[]{:S(2)}, u32[]{:S(2)}) collective-permute-start(bf16[1,128,896]{2,1,0:T(8,128)(2,1)S(1)} %get-tuple-element.19), channel_id=1, source_target_pairs={{0,6},{1,7},{2,0},{3,1},{4,2},{5,3},{6,4},{7,5},{8,14},{9,15},{10,... | collective-permute-start | bytes 688136 | tf_op jit(solution)/shard_map/ppermute | solution.py:32
  89.5 3.2 %collective-permute-start.24 = (bf16[128,512]{1,0:T(8,128)(2,1)S(1)}, bf16[128,512]{1,0:T(8,128)(2,1)S(1)}, u32[]{:S(2)}, u32[]{:S(2)}) collective-permute-start(bf16[128,512]{1,0:T(8,128)(2,1)S(1)} %get-tuple-element.25), channel_id=1, source_target_pairs={{0,6},{1,7},{2,0},{3,1},{4,2},{5,3},{6,4},{7,5},{8,14},{9,15},{10,... | collective-permute-start | bytes 393224 | tf_op jit(solution)/shard_map/ppermute | solution.py:32
  95.2 3.6 %collective-permute-start.30 = (bf16[2,128,896]{2,1,0:T(8,128)(2,1)S(1)}, bf16[2,128,896]{2,1,0:T(8,128)(2,1)S(1)}, u32[]{:S(2)}, u32[]{:S(2)}) collective-permute-start(bf16[2,128,896]{2,1,0:T(8,128)(2,1)S(1)} %pad_maximum_fusion.1), channel_id=1, source_target_pairs={{0,6},{1,7},{2,0},{3,1},{4,2},{5,3},{6,4},{7,5},{8,14},{9,15},{10,... | collective-permute-start | bytes 1376264 | tf_op jit(solution)/shard_map/ppermute | solution.py:32
  100.4 3.2 %collective-permute-start.25 = (bf16[256,512]{1,0:T(8,128)(2,1)}, bf16[256,512]{1,0:T(8,128)(2,1)}, u32[]{:S(2)}, u32[]{:S(2)}) collective-permute-start(bf16[256,512]{1,0:T(8,128)(2,1)} %pad_maximum_fusion.3), channel_id=1, source_target_pairs={{0,6},{1,7},{2,0},{3,1},{4,2},{5,3},{6,4},{7,5},{8,14},{9,15},{10,... | collective-permute-start | bytes 786440 | tf_op jit(solution)/shard_map/ppermute | solution.py:32
  103.6 5.9 %collective-permute-done.28 = bf16[2,128,896]{2,1,0:T(8,128)(2,1)S(1)} collective-permute-done((bf16[2,128,896]{2,1,0:T(8,128)(2,1)S(1)}, bf16[2,128,896]{2,1,0:T(8,128)(2,1)S(1)}, u32[]{:S(2)}, u32[]{:S(2)}) %collective-permute-start.28) | collective-permute-done | bytes 458784 | tf_op jit(solution)/shard_map/ppermute | solution.py:28
  110.5 6.2 %all-to-all-start.1 = ((bf16[16,2,8,896]{3,2,1,0:T(8,128)(2,1)}), bf16[16,2,8,896]{3,2,1,0:T(8,128)(2,1)S(1)}, u32[]{:S(2)}, u32[]{:S(2)}) async-start(bf16[16,2,8,896]{3,2,1,0:T(8,128)(2,1)} %copy_bitcast_fusion), calls=%async_computation.1 | async-start | bytes 917504 | tf_op jit(solution)/shard_map/all_to_all | solution.py:358
  118.7 6.7 %all-to-all-done.1 = bf16[16,2,8,896]{3,2,1,0:T(8,128)(2,1)S(1)} async-done(((bf16[16,2,8,896]{3,2,1,0:T(8,128)(2,1)}), bf16[16,2,8,896]{3,2,1,0:T(8,128)(2,1)S(1)}, u32[]{:S(2)}, u32[]{:S(2)}) %all-to-all-start.1) | async-done | bytes 458784 | tf_op jit(solution)/shard_map/all_to_all | solution.py:358
  125.4 3.7 %scatter.1 = f32[96,8,896]{2,1,0:T(8,128)} custom-call(s32[16,1,128]{2,1,0:T(1,128)S(1)} %all-to-all-done.ids_ref, bf16[32,8,896]{2,1,0:T(8,128)(2,1)S(1)} %bitcast.65), custom_call_target="tpu_custom_call" | custom-call | tf_op jit(solution)/shard_map/scatter/pallas_call | solution.py:359
  (93 shorter events, 24.3 us)
Async XLA Ops:
  3.4 23.8 %collective-permute-start.11 = (bf16[2,128,896]{2,1,0:T(8,128)(2,1)}, bf16[2,128,896]{2,1,0:T(8,128)(2,1)S(1)}, u32[]{:S(2)}, u32[]{:S(2)}) collective-permute-start(bf16[2,128,896]{2,1,0:T(8,128)(2,1)} %fetch.1.refs_5_), channel_id=1, source_target_pairs={{0,6},{1,7},{2,0},{3,1},{4,2},{5,3},{6,4},{7,5},{8,14},{9,15},{10,... | collective-permute-start | bytes 1376264 | tf_op jit(solution)/shard_map/ppermute | solution.py:32
  7.5 19.7 %collective-permute-start.12 = (bf16[2,128,896]{2,1,0:T(8,128)(2,1)}, bf16[2,128,896]{2,1,0:T(8,128)(2,1)S(1)}, u32[]{:S(2)}, u32[]{:S(2)}) collective-permute-start(bf16[2,128,896]{2,1,0:T(8,128)(2,1)} %fetch.1.refs_5_), channel_id=1, source_target_pairs={{0,2},{1,3},{2,4},{3,5},{4,6},{5,7},{6,0},{7,1},{8,10},{9,11},{10,... | collective-permute-start | bytes 1376264 | tf_op jit(solution)/shard_map/ppermute | solution.py:28
  9.3 19.5 %collective-permute-start = (bf16[2,256,512]{2,1,0:T(8,128)(2,1)}, bf16[2,256,512]{2,1,0:T(8,128)(2,1)S(1)}, u32[]{:S(2)}, u32[]{:S(2)}) collective-permute-start(bf16[2,256,512]{2,1,0:T(8,128)(2,1)} %pack.1.refs_0_), channel_id=1, source_target_pairs={{0,6},{1,7},{2,0},{3,1},{4,2},{5,3},{6,4},{7,5},{8,14},{9,15},{10,... | collective-permute-start | bytes 1572872 | tf_op jit(solution)/shard_map/ppermute | solution.py:32
  12.6 20.9 %collective-permute-start.1 = (bf16[2,256,512]{2,1,0:T(8,128)(2,1)}, bf16[2,256,512]{2,1,0:T(8,128)(2,1)S(1)}, u32[]{:S(2)}, u32[]{:S(2)}) collective-permute-start(bf16[2,256,512]{2,1,0:T(8,128)(2,1)} %pack.1.refs_0_), channel_id=1, source_target_pairs={{0,2},{1,3},{2,4},{3,5},{4,6},{5,7},{6,0},{7,1},{8,10},{9,11},{10,... | collective-permute-start | bytes 1572872 | tf_op jit(solution)/shard_map/ppermute | solution.py:28
  13.7 13.5 %all-to-all-start = ((s32[16,1,128]{2,1,0:T(1,128)}), s32[16,1,128]{2,1,0:T(1,128)S(1)}, u32[]{:S(2)}, u32[]{:S(2)}) async-start(s32[16,1,128]{2,1,0:T(1,128)} %broadcast_in_dim.3), calls=%async_computation | async-start | bytes 16384 | tf_op jit(solution)/shard_map/all_to_all | solution.py:288
  21.2 12.6 %collective-permute-start.3 = (bf16[2,256,512]{2,1,0:T(8,128)(2,1)}, bf16[2,256,512]{2,1,0:T(8,128)(2,1)S(1)}, u32[]{:S(2)}, u32[]{:S(2)}) collective-permute-start(bf16[2,256,512]{2,1,0:T(8,128)(2,1)} %pack.1.refs_0_), channel_id=1, source_target_pairs={{0,1},{1,0},{2,3},{3,2},{4,5},{5,4},{6,7},{7,6},{8,9},{9,8},{10,11... | collective-permute-start | bytes 1572872 | tf_op jit(solution)/shard_map/ppermute | solution.py:36
  27.2 11.2 %collective-permute-start.13 = (bf16[128,896]{1,0:T(8,128)(2,1)S(1)}, bf16[128,896]{1,0:T(8,128)(2,1)S(1)}, u32[]{:S(2)}, u32[]{:S(2)}) collective-permute-start(bf16[128,896]{1,0:T(8,128)(2,1)S(1)} %slice_bitcast_fusion.3), channel_id=1, source_target_pairs={{0,2},{1,3},{2,4},{3,5},{4,6},{5,7},{6,0},{7,1},{8,10},{9,11},{10,... | collective-permute-start | bytes 688136 | tf_op jit(solution)/shard_map/ppermute | solution.py:28
  28.8 10.1 %collective-permute-start.8 = (bf16[256,512]{1,0:T(8,128)(2,1)S(1)}, bf16[256,512]{1,0:T(8,128)(2,1)S(1)}, u32[]{:S(2)}, u32[]{:S(2)}) collective-permute-start(bf16[256,512]{1,0:T(8,128)(2,1)S(1)} %slice_bitcast_fusion), channel_id=1, source_target_pairs={{0,6},{1,7},{2,0},{3,1},{4,2},{5,3},{6,4},{7,5},{8,14},{9,15},{10,... | collective-permute-start | bytes 786440 | tf_op jit(solution)/shard_map/ppermute | solution.py:32
  33.6 9.0 %collective-permute-start.2 = (bf16[256,512]{1,0:T(8,128)(2,1)S(1)}, bf16[256,512]{1,0:T(8,128)(2,1)S(1)}, u32[]{:S(2)}, u32[]{:S(2)}) collective-permute-start(bf16[256,512]{1,0:T(8,128)(2,1)S(1)} %slice_bitcast_fusion.1), channel_id=1, source_target_pairs={{0,2},{1,3},{2,4},{3,5},{4,6},{5,7},{6,0},{7,1},{8,10},{9,11},{10,... | collective-permute-start | bytes 786440 | tf_op jit(solution)/shard_map/ppermute | solution.py:28
  33.7 11.4 %collective-permute-start.4 = (bf16[2,256,512]{2,1,0:T(8,128)(2,1)S(1)}, bf16[2,256,512]{2,1,0:T(8,128)(2,1)S(1)}, u32[]{:S(2)}, u32[]{:S(2)}) collective-permute-start(bf16[2,256,512]{2,1,0:T(8,128)(2,1)S(1)} %collective-permute-done.refs_1_), channel_id=1, source_target_pairs={{0,1},{1,0},{2,3},{3,2},{4,5},{5,4},{6,7},{7,6},{8,9},{9,8},{10,11... | collective-permute-start | bytes 1572872 | tf_op jit(solution)/shard_map/ppermute | solution.py:36
  33.8 11.3 %collective-permute-start.5 = (bf16[2,256,512]{2,1,0:T(8,128)(2,1)S(1)}, bf16[2,256,512]{2,1,0:T(8,128)(2,1)S(1)}, u32[]{:S(2)}, u32[]{:S(2)}) collective-permute-start(bf16[2,256,512]{2,1,0:T(8,128)(2,1)S(1)} %collective-permute-done.1.refs_2_), channel_id=1, source_target_pairs={{0,1},{1,0},{2,3},{3,2},{4,5},{5,4},{6,7},{7,6},{8,9},{9,8},{10,11... | collective-permute-start | bytes 1572872 | tf_op jit(solution)/shard_map/ppermute | solution.py:36
  44.5 14.5 %collective-permute-start.16 = (bf16[2,128,896]{2,1,0:T(8,128)(2,1)S(1)}, bf16[2,128,896]{2,1,0:T(8,128)(2,1)S(1)}, u32[]{:S(2)}, u32[]{:S(2)}) collective-permute-start(bf16[2,128,896]{2,1,0:T(8,128)(2,1)S(1)} %collective-permute-done.11.refs_6_), channel_id=1, source_target_pairs={{0,1},{1,0},{2,3},{3,2},{4,5},{5,4},{6,7},{7,6},{8,9},{9,8},{10,11... | collective-permute-start | bytes 1376264 | tf_op jit(solution)/shard_map/ppermute | solution.py:36
  45.0 14.0 %collective-permute-start.17 = (bf16[2,128,896]{2,1,0:T(8,128)(2,1)S(1)}, bf16[2,128,896]{2,1,0:T(8,128)(2,1)S(1)}, u32[]{:S(2)}, u32[]{:S(2)}) collective-permute-start(bf16[2,128,896]{2,1,0:T(8,128)(2,1)S(1)} %collective-permute-done.12.refs_7_), channel_id=1, source_target_pairs={{0,1},{1,0},{2,3},{3,2},{4,5},{5,4},{6,7},{7,6},{8,9},{9,8},{10,11... | collective-permute-start | bytes 1376264 | tf_op jit(solution)/shard_map/ppermute | solution.py:36
  45.1 11.2 %collective-permute-start.18 = (bf16[128,896]{1,0:T(8,128)(2,1)S(1)}, bf16[128,896]{1,0:T(8,128)(2,1)S(1)}, u32[]{:S(2)}, u32[]{:S(2)}) collective-permute-start(bf16[128,896]{1,0:T(8,128)(2,1)S(1)} %collective-permute-done.13.refs_8_), channel_id=1, source_target_pairs={{0,1},{1,0},{2,3},{3,2},{4,5},{5,4},{6,7},{7,6},{8,9},{9,8},{10,11... | collective-permute-start | bytes 688136 | tf_op jit(solution)/shard_map/ppermute | solution.py:36
  45.6 13.5 %collective-permute-start.19 = (bf16[128,896]{1,0:T(8,128)(2,1)S(1)}, bf16[128,896]{1,0:T(8,128)(2,1)S(1)}, u32[]{:S(2)}, u32[]{:S(2)}) collective-permute-start(bf16[128,896]{1,0:T(8,128)(2,1)S(1)} %collective-permute-done.14.refs_9_), channel_id=1, source_target_pairs={{0,1},{1,0},{2,3},{3,2},{4,5},{5,4},{6,7},{7,6},{8,9},{9,8},{10,11... | collective-permute-start | bytes 688136 | tf_op jit(solution)/shard_map/ppermute | solution.py:36
  72.9 12.7 %collective-permute-start.26 = (bf16[4,2,128,896]{3,2,1,0:T(8,128)(2,1)S(1)}, bf16[4,2,128,896]{3,2,1,0:T(8,128)(2,1)S(1)}, u32[]{:S(2)}, u32[]{:S(2)}) collective-permute-start(bf16[4,2,128,896]{3,2,1,0:T(8,128)(2,1)S(1)} %term_away.1), channel_id=1, source_target_pairs={{0,1},{1,0},{2,3},{3,2},{4,5},{5,4},{6,7},{7,6},{8,9},{9,8},{10,11... | collective-permute-start | bytes 5505032 | tf_op jit(solution)/shard_map/ppermute | solution.py:36
  85.9 8.9 %collective-permute-start.27 = (bf16[1,128,896]{2,1,0:T(8,128)(2,1)S(1)}, bf16[1,128,896]{2,1,0:T(8,128)(2,1)S(1)}, u32[]{:S(2)}, u32[]{:S(2)}) collective-permute-start(bf16[1,128,896]{2,1,0:T(8,128)(2,1)S(1)} %get-tuple-element.18), channel_id=1, source_target_pairs={{0,2},{1,3},{2,4},{3,5},{4,6},{5,7},{6,0},{7,1},{8,10},{9,11},{10,... | collective-permute-start | bytes 688136 | tf_op jit(solution)/shard_map/ppermute | solution.py:28
  89.4 9.4 %collective-permute-start.22 = (bf16[128,512]{1,0:T(8,128)(2,1)S(1)}, bf16[128,512]{1,0:T(8,128)(2,1)S(1)}, u32[]{:S(2)}, u32[]{:S(2)}) collective-permute-start(bf16[128,512]{1,0:T(8,128)(2,1)S(1)} %get-tuple-element.24), channel_id=1, source_target_pairs={{0,2},{1,3},{2,4},{3,5},{4,6},{5,7},{6,0},{7,1},{8,10},{9,11},{10,... | collective-permute-start | bytes 393224 | tf_op jit(solution)/shard_map/ppermute | solution.py:28
  89.5 9.3 %collective-permute-start.24 = (bf16[128,512]{1,0:T(8,128)(2,1)S(1)}, bf16[128,512]{1,0:T(8,128)(2,1)S(1)}, u32[]{:S(2)}, u32[]{:S(2)}) collective-permute-start(bf16[128,512]{1,0:T(8,128)(2,1)S(1)} %get-tuple-element.25), channel_id=1, source_target_pairs={{0,6},{1,7},{2,0},{3,1},{4,2},{5,3},{6,4},{7,5},{8,14},{9,15},{10,... | collective-permute-start | bytes 393224 | tf_op jit(solution)/shard_map/ppermute | solution.py:32
  95.0 14.5 %collective-permute-start.28 = (bf16[2,128,896]{2,1,0:T(8,128)(2,1)S(1)}, bf16[2,128,896]{2,1,0:T(8,128)(2,1)S(1)}, u32[]{:S(2)}, u32[]{:S(2)}) collective-permute-start(bf16[2,128,896]{2,1,0:T(8,128)(2,1)S(1)} %pad_maximum_fusion), channel_id=1, source_target_pairs={{0,2},{1,3},{2,4},{3,5},{4,6},{5,7},{6,0},{7,1},{8,10},{9,11},{10,... | collective-permute-start | bytes 1376264 | tf_op jit(solution)/shard_map/ppermute | solution.py:28
  95.2 14.3 %collective-permute-start.30 = (bf16[2,128,896]{2,1,0:T(8,128)(2,1)S(1)}, bf16[2,128,896]{2,1,0:T(8,128)(2,1)S(1)}, u32[]{:S(2)}, u32[]{:S(2)}) collective-permute-start(bf16[2,128,896]{2,1,0:T(8,128)(2,1)S(1)} %pad_maximum_fusion.1), channel_id=1, source_target_pairs={{0,6},{1,7},{2,0},{3,1},{4,2},{5,3},{6,4},{7,5},{8,14},{9,15},{10,... | collective-permute-start | bytes 1376264 | tf_op jit(solution)/shard_map/ppermute | solution.py:32
  99.6 17.0 %collective-permute-start.23 = (bf16[256,512]{1,0:T(8,128)(2,1)}, bf16[256,512]{1,0:T(8,128)(2,1)}, u32[]{:S(2)}, u32[]{:S(2)}) collective-permute-start(bf16[256,512]{1,0:T(8,128)(2,1)} %pad_maximum_fusion.2), channel_id=1, source_target_pairs={{0,2},{1,3},{2,4},{3,5},{4,6},{5,7},{6,0},{7,1},{8,10},{9,11},{10,... | collective-permute-start | bytes 786440 | tf_op jit(solution)/shard_map/ppermute | solution.py:28
  100.4 16.3 %collective-permute-start.25 = (bf16[256,512]{1,0:T(8,128)(2,1)}, bf16[256,512]{1,0:T(8,128)(2,1)}, u32[]{:S(2)}, u32[]{:S(2)}) collective-permute-start(bf16[256,512]{1,0:T(8,128)(2,1)} %pad_maximum_fusion.3), channel_id=1, source_target_pairs={{0,6},{1,7},{2,0},{3,1},{4,2},{5,3},{6,4},{7,5},{8,14},{9,15},{10,... | collective-permute-start | bytes 786440 | tf_op jit(solution)/shard_map/ppermute | solution.py:32
  110.5 14.9 %all-to-all-start.1 = ((bf16[16,2,8,896]{3,2,1,0:T(8,128)(2,1)}), bf16[16,2,8,896]{3,2,1,0:T(8,128)(2,1)S(1)}, u32[]{:S(2)}, u32[]{:S(2)}) async-start(bf16[16,2,8,896]{3,2,1,0:T(8,128)(2,1)} %copy_bitcast_fusion), calls=%async_computation.1 | async-start | bytes 917504 | tf_op jit(solution)/shard_map/all_to_all | solution.py:358
  (18 other events, 206.9 us)

commit v2 on v0

v2 whole, which is shorter than its diff:
```python
import functools

import jax
import jax.numpy as jnp
from jax import lax
from jax.experimental import pallas as pl
from jax.experimental.pallas import tpu as pltpu
from jax.sharding import PartitionSpec as P

HDIM = 128
DE = 896
CH = 64
R = 128
K = 2
CAP = 2
BORDER = CH - 1
SCALE = HDIM ** (-0.5)
BF16, F32 = jnp.bfloat16, jnp.float32
NT = (((1,), (1,)), ((), ()))
TN = (((0,), (0,)), ((), ()))
VMEM = pl.BlockSpec(memory_space=pltpu.VMEM)
SMEM = pl.BlockSpec(memory_space=pltpu.SMEM)
ANY = pl.BlockSpec(memory_space=pl.ANY)
HBM = pl.BlockSpec(memory_space=pltpu.HBM)


def up(x):
    return lax.ppermute(x, "db", [(s, (s + 2) % 8) for s in range(8)])


def down(x):
    return lax.ppermute(x, "db", [(s, (s - 2) % 8) for s in range(8)])


def across(x):
    return lax.ppermute(x, "db", [(s, s ^ 1) for s in range(8)])


def along_ctx(x, by):
    peers = lax.axis_size("ctx")
    return lax.ppermute(x, "ctx", [(i, i + by) for i in range(peers) if 0 <= i + by < peers])


def shape(dims, dtype=BF16):
    return jax.ShapeDtypeStruct(dims, dtype)


def cost(flops, size):
    return pl.CostEstimate(flops=flops, bytes_accessed=size, transcendentals=0)


def source_of(me, core, place):
    return lax.rem(me // 2 + place, 4) * 2 + (lax.rem(me, 2) + core) % 2


def named(shards, shard):
    count, found = jnp.int32(0), [jnp.int32(0)] * CAP
    for c in range(shards.shape[1]):
        for k in range(K):
            mine = shards[k, c] == shard
            for at in range(CAP):
                found[at] = jnp.where(mine & (count == at), c * K + k, found[at])
            count = count + mine.astype(jnp.int32)
    return found, count


def load_kernel(
    shard_ref, row_ref, states_ref, cotangent_ref, database_ref, out_ref, label_ref, sems
):
    rows, width = states_ref.shape
    copies = []

    def copy(source, at, item, start, size):
        count = source.shape[-1] // HDIM
        for j in range(count):
            copies.append(
                pltpu.make_async_copy(
                    source.at[:, pl.ds(j * HDIM, HDIM)],
                    out_ref.at[item, pl.ds(start + j * size, size)],
                    sems.at[at + j],
                )
            )
            copies[-1].start()

    copy(states_ref, 0, 0, 0, rows)
    copy(cotangent_ref, 4, 1, 0, rows)
    found, count = named(shard_ref, lax.axis_index("db"))
    named_rows = [row_ref[lax.rem(request, K), request // K] for request in found]
    for slot, row in enumerate(named_rows):
        copy(database_ref.at[row], 8 + 7 * slot, slot, rows * width // HDIM, R)
    for slot, row in enumerate(named_rows):
        label = jnp.where(count > slot, row, -1).astype(F32)
        label_ref[slot] = jnp.full(label_ref.shape[1:], label, F32)
    for each in copies:
        each.wait()


def hold_kernel(label_ref, a_ref, b_ref, a_out, b_out, done_ref, sems):
    copies = [
        pltpu.make_async_copy(src, dst, sems.at[at])
        for at, (src, dst) in enumerate(((a_ref, a_out), (b_ref, b_out)))
    ]
    for copy in copies:
        copy.start()
    for copy in copies:
        copy.wait()
    done_ref[...] = label_ref[...]


def project_kernel(*refs):
    blocks, weights, outs, tail_ref, full = refs[:10], refs[10:12], refs[12:14], *refs[14:]
    me = lax.axis_index("db")
    rows, width = outs[0].shape
    for item in range(2):
        for core in range(2):
            own, nxt, prv, *far = blocks[core * 5 : core * 5 + 5]
            for place, block in ((0, own), (1, nxt), (3, prv), (2, far[item])):
                spot = pl.multiple_of(source_of(me, core, place) * width, width)
                for j in range(width // HDIM):
                    part = pl.ds(j * rows, rows)
                    full[item, :, pl.ds(spot + j * HDIM, HDIM)] = (
                        block[part] if place == 2 else block[item, part]
                    )
    for item in range(2):
        w = weights[item][...]
        if item:
            total = lax.dot_general(full[item], w, NT, preferred_element_type=F32)
        else:
            total = jnp.dot(full[item], w, preferred_element_type=F32)
        total = pltpu.roll(total, rows - BORDER, 0).astype(BF16)
        outs[item][...] = total
        tail_ref[item] = total[rows - CH :]


def places_of(shard_ref):
    me = lax.axis_index("db")
    found = []
    for request in range(shard_ref.shape[1] * K):
        shard = shard_ref[request % K, request // K]
        rank = jnp.int32(0)
        for earlier in range(request):
            same = shard_ref[earlier % K, earlier // K] == shard
            rank = rank + same.astype(jnp.int32)
        core = (lax.rem(shard, 2) + lax.rem(me, 2)) % 2
        place = lax.rem(shard // 2 - me // 2 + 4, 4)
        found.append((core, place, jnp.minimum(rank, CAP - 1)))
    return found


def span_gradients(q, g, k_ref, v_ref, memory, gk_ref, gv_ref):
    some = range(len(q))
    at = [pl.ds(h * HDIM, HDIM) for h in some]
    k, v = [k_ref[memory, x] for x in at], [v_ref[memory, x] for x in at]
    scores = [lax.dot_general(q[h], k[h], NT, preferred_element_type=F32) * SCALE for h in some]
    dattention = [lax.dot_general(g[h], v[h], NT, preferred_element_type=F32) for h in some]
    raised = [jnp.exp(x - jnp.max(x, -1, keepdims=True)) for x in scores]
    attention = [x / jnp.sum(x, -1, keepdims=True) for x in raised]
    mean = [jnp.sum(attention[h] * dattention[h], -1, keepdims=True) for h in some]
    dscores = [(attention[h] * (dattention[h] - mean[h])).astype(BF16) for h in some]
    gq = [jnp.dot(dscores[h], k[h], preferred_element_type=F32) * SCALE for h in some]
    for h in some:
        gk = lax.dot_general(dscores[h], q[h], TN, preferred_element_type=F32) * SCALE
        gk_ref[memory, at[h]] = gk.astype(BF16)
    for h in some:
        gv = lax.dot_general(attention[h].astype(BF16), g[h], TN, preferred_element_type=F32)
        gv_ref[memory, at[h]] = gv.astype(BF16)
    return gq


def neighbour_terms(gk_ref, gv_ref, wk_ref, wv_ref, found, term_s, away_ref, own_ref):
    term = lax.dot_general(gk_ref[...], wk_ref[...], NT, preferred_element_type=F32)
    term = term + lax.dot_general(gv_ref[...], wv_ref[...], NT, preferred_element_type=F32)
    term_s[...] = term.astype(BF16)
    for at, (core, place, rank) in enumerate(found):
        spot = pl.ds(at * R, R)
        for which, ref in ((0, own_ref), (1, away_ref)):

            @pl.when(core == which)
            def _(spot=spot, place=place, rank=rank, ref=ref):
                ref[place, rank] = term_s[spot]


def attend_kernel(*refs):
    shard_ref, mems, wk_ref, wv_ref, q_ref, g_ref = refs[0], refs[1:11], *refs[11:15]
    k_ref, v_ref, gq_ref, away_ref, own_ref = refs[15:20]
    mem_s, k_s, v_s, gk_s, gv_s, term_s = refs[20:]
    rows, width = q_ref.shape
    spans = rows // CH
    found = places_of(shard_ref)
    base = rows * width // HDIM

    def take(request, read):
        for j in range(DE // HDIM):
            part = read(pl.ds(base + j * R, R))
            mem_s[pl.ds(request * R, R), pl.ds(j * HDIM, HDIM)] = part

    for request, (core, place, rank) in enumerate(found):
        for which in range(2):
            own, nxt, prv, far0, far1 = mems[which * 5 : which * 5 + 5]
            here = core == which
            for at, ref in ((0, own), (1, nxt), (3, prv)):

                @pl.when(here & (place == at))
                def _(ref=ref, rank=rank, request=request):
                    take(request, lambda part: ref[rank, part])

            for at, ref in ((0, far0), (1, far1)):

                @pl.when(here & (place == 2) & (rank == at))
                def _(ref=ref, request=request):
                    take(request, lambda part: ref[part])

    k_s[...] = jnp.dot(mem_s[...], wk_ref[...], preferred_element_type=F32).astype(BF16)
    v_s[...] = jnp.dot(mem_s[...], wv_ref[...], preferred_element_type=F32).astype(BF16)
    heads = [pl.ds(h * HDIM, HDIM) for h in range(width // HDIM)]
    for c in range(spans - 1):
        span, memory = pl.ds(c * CH, CH), pl.ds(c * K * R, K * R)
        q, g = [q_ref[span, x] for x in heads], [g_ref[span, x] for x in heads]
        gq = span_gradients(q, g, k_s, v_s, memory, gk_s, gv_s)
        for x, value in zip(heads, gq):
            gq_ref[span, x] = value
    memory = pl.ds((spans - 1) * K * R, K * R)
    k_ref[...], v_ref[...] = k_s[memory], v_s[memory]
    first = found[: (spans - 1) * K]
    neighbour_terms(gk_s, gv_s, wk_ref, wv_ref, first, term_s, away_ref, own_ref)


def last_kernel(*refs):
    shard_ref, q_ref, g_ref, tail_ref, k_ref, v_ref, wk_ref, wv_ref, gq_in = refs[:9]
    gq_ref, away_ref, own_ref = refs[11:14]
    gk_s, gv_s, term_s = refs[14:]
    rows, width = q_ref.shape
    last = rows - CH
    heads = [pl.ds(h * HDIM, HDIM) for h in range(width // HDIM)]
    first_row = lax.broadcasted_iota(jnp.int32, (CH, HDIM), 0) == 0
    q, g = (
        [jnp.where(first_row, ref[last:, x], tail_ref[item, :, x]) for x in heads]
        for item, ref in enumerate((q_ref, g_ref))
    )
    gq = span_gradients(q, g, k_ref, v_ref, pl.ds(0, K * R), gk_s, gv_s)
    gq_ref[:last] = gq_in[...].astype(BF16)
    for x, value in zip(heads, gq):
        gq_ref[last:, x] = value.astype(BF16)
    found = places_of(shard_ref)[-K:]
    neighbour_terms(gk_s, gv_s, wk_ref, wv_ref, found, term_s, away_ref, own_ref)


def cross_kernel(gq_ref, w_ref, away_ref, own_ref):
    me = lax.axis_index("db")
    width = gq_ref.shape[1]
    for core, out in ((1, away_ref), (0, own_ref)):
        for place in range(4):
            spot = pl.multiple_of(source_of(me, core, place) * width, width)
            out[place] = lax.dot_general(
                gq_ref[...], w_ref[pl.ds(spot, width), :], NT, preferred_element_type=F32
            ).astype(BF16)


def scatter_kernel(label_ref, parts_ref, out_ref):
    out_ref[...] = jnp.zeros_like(out_ref)
    width = out_ref.shape[2]

    def item(i, carry):
        row = label_ref[i]

        @pl.when(row >= 0)
        def _():
            out_ref[row] += parts_ref[i][:, :width].astype(F32)

        return carry

    lax.fori_loop(0, parts_ref.shape[0], item, 0)


def after(x, token):
    return x + jnp.where(token > 0, -0.0, 0.0).astype(x.dtype)


def gather_two(own, token):
    nxt, prv = down(own), up(own)
    return own, nxt, prv, up(after(prv[0], token)), down(after(nxt[1], token))


def with_other_core(blocks):
    return tuple(blocks) + tuple(across(x) for x in blocks)


def add(*parts):
    return functools.reduce(lambda a, b: a + b, [x.astype(F32) for x in parts])


def far_sums(own, got, half):
    return add(own[2][:half], got[2][:half]), add(own[2][half:], got[2][half:])


def near_sums(own, got, half, far_up, far_down):
    nxt = [add(own[1][:half], got[1][:half], far_up), add(own[1][half:], got[1][half:])]
    prv = [add(own[3][:half], got[3][:half]), add(own[3][half:], got[3][half:], far_down)]
    return jnp.concatenate(nxt, 0), jnp.concatenate(prv, 0)


def per_device(
    states, cotangent, w_query, w_key, w_value, w_out, database, neighbour_shard, neighbour_row
):
    rows, width = states.shape
    spans = rows // CH
    limit = pltpu.CompilerParams(vmem_limit_bytes=20 * 2**20)
    shards, named_rows = neighbour_shard.T, neighbour_row.T
    peers = lax.axis_size("ctx")

    given_rows = rows * width // HDIM + R * DE // HDIM
    given, label = pl.pallas_call(
        load_kernel,
        name="load",
        out_shape=(shape((2, given_rows, HDIM)), shape((CAP, 8, 128), F32)),
        in_specs=[SMEM, SMEM, ANY, ANY, ANY],
        out_specs=(VMEM, VMEM),
        scratch_shapes=[pltpu.SemaphoreType.DMA((2 * (width + DE) // HDIM,))],
    )(shards, named_rows, states, cotangent, database)
    *held, done = pl.pallas_call(
        hold_kernel,
        name="hold",
        out_shape=(shape(w_query.shape), shape(w_out.shape), shape(label.shape, F32)),
        in_specs=[VMEM, HBM, HBM],
        out_specs=(VMEM,) * 3,
        scratch_shapes=[pltpu.SemaphoreType.DMA((2,))],
        compiler_params=limit,
    )(label, w_query, w_out)
    gathered = with_other_core(gather_two(given, done[0, :1]))

    query, grad_out, tails = pl.pallas_call(
        project_kernel,
        name="project",
        out_shape=(shape((rows, width)), shape((rows, width)), shape((2, CH, width))),
        in_specs=[VMEM] * 12,
        out_specs=(VMEM,) * 3,
        scratch_shapes=[pltpu.VMEM((2, rows, 8 * width), BF16)],
        compiler_params=limit,
        cost_estimate=cost(32 * rows * width * width, 2**23),
    )(*gathered, *held)
    tails = along_ctx(tails, -1)
    positions, slots_of = spans * K * R, shape((4, CAP, R, DE))
    most = positions - K * R
    *last, away, own = pl.pallas_call(
        attend_kernel,
        name="attend",
        out_shape=(shape((K * R, width)), shape((K * R, width)), shape((rows - CH, width), F32))
        + (slots_of, slots_of),
        in_specs=[SMEM] + [VMEM] * 14,
        out_specs=(VMEM,) * 5,
        scratch_shapes=[
            pltpu.VMEM((positions, DE), BF16),
            pltpu.VMEM((positions, width), BF16),
            pltpu.VMEM((positions, width), BF16),
            pltpu.VMEM((most, width), BF16),
            pltpu.VMEM((most, width), BF16),
            pltpu.VMEM((most, DE), BF16),
        ],
        compiler_params=limit,
        cost_estimate=cost(8 * positions * DE * width, 2**23),
    )(shards, *gathered, w_key, w_value, query, grad_out)
    grad_query, away, own = pl.pallas_call(
        last_kernel,
        name="last",
        out_shape=(shape((rows, width)), slots_of, slots_of),
        in_specs=[SMEM] + [VMEM] * 8 + [VMEM] * 2,
        out_specs=(VMEM,) * 3,
        scratch_shapes=[
            pltpu.VMEM((K * R, width), BF16),
            pltpu.VMEM((K * R, width), BF16),
            pltpu.VMEM((K * R, DE), BF16),
        ],
        input_output_aliases={9: 1, 10: 2},
        compiler_params=limit,
        cost_estimate=cost(2 * positions * DE * width, 2**22),
    )(shards, query, grad_out, tails, last[0], last[1], w_key, w_value, last[2], away, own)
    got, half = across(away), CAP // 2
    far_up, far_down = far_sums(own, got, half)
    far_up, far_down = up(far_up.astype(BF16)), down(far_down.astype(BF16))
    nxt, prv = (x.astype(BF16) for x in near_sums(own, got, half, far_up, far_down))
    slots = add(own[0], got[0], up(nxt), down(prv)).astype(BF16)
    block = R // peers
    spread = slots.reshape(CAP, peers, block, DE).transpose(1, 0, 2, 3)
    labels = jnp.broadcast_to(label.astype(BF16), (peers,) + label.shape)
    spread = jnp.concatenate([spread, labels], -1)
    parts = lax.all_to_all(spread, "ctx", 0, 0, tiled=True)
    parts = parts.reshape(peers * CAP, block, DE + label.shape[-1])
    labels = parts[:, 0, DE].astype(jnp.int32)
    cross_away, cross_own = pl.pallas_call(
        cross_kernel,
        name="cross",
        out_shape=(shape((4, rows, width)), shape((4, rows, width))),
        in_specs=[VMEM] * 2,
        out_specs=(VMEM, VMEM),
        compiler_params=limit,
        cost_estimate=cost(2 * rows * width * 8 * width, 2**23),
    )(grad_query, held[0])
    cross_got, half = across(cross_away), rows // 2
    far_up, far_down = far_sums(cross_own, cross_got, half)
    far_up, far_down = up(far_up.astype(BF16)), down(far_down.astype(BF16))
    nxt, prv = near_sums(cross_own, cross_got, half, far_up, far_down)
    nxt, prv = nxt.astype(BF16), prv.astype(BF16)
    cross = add(cross_own[0], cross_got[0], up(nxt), down(prv))
    keep = rows - BORDER
    carried = along_ctx(cross[keep:].astype(BF16), 1).astype(F32)
    grad_states = cotangent.astype(F32) + jnp.concatenate([carried, cross[:keep]], 0)
    grad_database = pl.pallas_call(
        scatter_kernel,
        name="scatter",
        out_shape=shape((database.shape[0], block, DE), F32),
        in_specs=[SMEM, VMEM],
        out_specs=VMEM,
        compiler_params=limit,
        cost_estimate=cost(2**38, 2**32),
    )(labels, parts)
    return grad_states, grad_database


def solution(mesh):
    in_specs = (
        P("ctx", "db"),
        P("ctx", "db"),
        P(None, "db"),
        P(None, "db"),
        P(None, "db"),
        P("db", None),
        P("db", None, None),
        P("ctx", None),
        P("ctx", None),
    )
    out_specs = (P("ctx", "db"), P("db", "ctx", None))
    return jax.shard_map(
        per_device, mesh=mesh, in_specs=in_specs, out_specs=out_specs, check_vma=False
    )
```

time: 375 us -> 120 us (0.32)
  waiting for transfers between devices: 246 us -> 52.1 us
  matrix products: 47.4 us -> 0 us
  local copies, waits for them, and re-layouts: 38.3 us -> 5.15 us
  Pallas kernels: 0 us -> 21 us
  starting transfers between devices: 15.1 us -> 36 us
  between operations: 14.4 us -> 0.97 us
  other arithmetic: 12 us -> 4.7 us
    reduce_scatter x3 -> x0, waiting for transfers between devices: 183 us -> none  [the longest x1 129 us: per_device(): lax.psum_scatter(dense.astype(jnp.bfloat16), 'ctx', scatter_dimension=1,...]
    all_gather x3 -> x0, waiting for transfers between devices: 57 us -> none  [the longest x1 28 us: per_device(): piece = lax.all_gather(outgoing, 'db', axis=0, tiled=True)]
    dot_general x11 -> x0, matrix products: 47.4 us -> none  [the longest x1 11.6 us: per_device(): jnp.einsum('bs,srd->brd', table, slot_grads, precision=lax.Precision.HIGH...]
    ppermute x3 -> x21, waiting for transfers between devices: 5.71 us -> 52.1 us  [the longest x6 24.4 us: down(): return lax.ppermute(x, 'db', [(s, (s - 2) % 8) for s in range(8)])]
    pallas_call x0 -> x7, Pallas kernels: none -> 21 us  [the longest x1 7.82 us: per_device(): pl.pallas_call(attend_kernel, name='attend', out_shape=(shape((K * R, wid...]
    ppermute x3 -> x21, starting transfers between devices: 14.6 us -> 30.8 us  [the longest x6 20.9 us: down(): return lax.ppermute(x, 'db', [(s, (s - 2) % 8) for s in range(8)])]
    gather x3 -> x0, local copies, waits for them, and re-layouts: 13.8 us -> none  [the longest x1 8.19 us: per_device(): jnp.take(database, owned_row, axis=0)]
    slice x9 -> x2, local copies, waits for them, and re-layouts: 7.6 us -> 0.04 us  [the longest x1 0.03 us: per_device(): cross[:keep]]
  transfers between devices with their start and end apart: 9 -> 22, of which waited for: 9 -> 11; matrix products, arithmetic and copies ran while one was open for 12% -> 3% of each run, Pallas kernels for 0% -> 8%
where the time goes in v2:
time: 120 us
  waiting for transfers between devices  52.1 us (43%)
  starting transfers between devices  36 us (30%)
  Pallas kernels  21 us (18%)
  local copies, waits for them, and re-layouts  5.15 us (4%)
  other arithmetic  4.7 us (4%)
    ppermute x6, waiting for transfers between devices, down(): return lax.ppermute(x, 'db', [(s, (s - 2) % 8) for s in range(8)])  24.4 us
    ppermute x6, starting transfers between devices, down(): return lax.ppermute(x, 'db', [(s, (s - 2) % 8) for s in range(8)])  20.9 us
    ppermute x6, waiting for transfers between devices, up(): return lax.ppermute(x, 'db', [(s, (s + 2) % 8) for s in range(8)])  19.2 us
    ppermute x2, starting transfers between devices, along_ctx(): lax.ppermute(x, 'ctx', [(i, i + by) for i in range(peers) if 0 <= i + by...  8.26 us
    pallas_call x1, Pallas kernels, per_device(): pl.pallas_call(attend_kernel, name='attend', out_shape=(shape((K * R, wid...  7.82 us
    all_to_all x1, starting transfers between devices, per_device(): parts = lax.all_to_all(spread, 'ctx', 0, 0, tiled=True)  5.18 us
    unnamed x18, local copies, waits for them, and re-layouts  5.1 us
    ppermute x2, waiting for transfers between devices, along_ctx(): lax.ppermute(x, 'ctx', [(i, i + by) for i in range(peers) if 0 <= i + by...  4.86 us
  transfers between devices with their start and end apart: 22, of which 11 were waited for; matrix products, arithmetic and copies ran while one was open for 3% of the time, Pallas kernels for 8%

profile of v2, /device:TPU:2, one launch (start us, length us, event | category | flops | bytes accessed | tf_op | source)
XLA Modules:
  0.0 119.9 jit_solution(16249965288658062987)
XLA Ops:
  0.6 3.0 %load.1 = (bf16[2,1920,128]{2,1,0:T(8,128)(2,1)}, f32[2,8,128]{2,1,0:T(8,128)}) custom-call(s32[2,4]{1,0:T(2,128)} %bitcast.65, s32[2,4]{1,0:T(2,128)} %bitcast.68, bf16[256,512]{1,0:T(8,128)(2,1)} %states_ref.1, bf16[256,512]{1,0:T(8,128)(2,1)} %cotangent_ref.1, bf16[96,128,896]{2,1,0:T(8,128)(2,1)} %database_ref.1), custom_call_target="tpu_custom_call" | custom-call | tf_op jit(solution)/shard_map/load/pallas_call | solution.py:312
  3.7 4.1 %collective-permute-start = (bf16[2,1920,128]{2,1,0:T(8,128)(2,1)}, bf16[2,1920,128]{2,1,0:T(8,128)(2,1)S(1)}, u32[]{:S(2)}, u32[]{:S(2)}) collective-permute-start(bf16[2,1920,128]{2,1,0:T(8,128)(2,1)} %get-tuple-element.20.refs_0_.refs_1_), channel_id=1, source_target_pairs={{0,6},{1,7},{2,0},{3,1},{4,2},{5,3},{6,4},{7,5},{8,14},{9,15},{10,... | collective-permute-start | bytes 2949128 | tf_op jit(solution)/shard_map/ppermute | solution.py:32
  7.8 2.2 %copy-done = bf16[4096,512]{1,0:T(8,128)(2,1)S(1)} copy-done((bf16[4096,512]{1,0:T(8,128)(2,1)S(1)}, bf16[4096,512]{1,0:T(8,128)(2,1)}, u32[]{:S(2)}) %copy-start) | copy-done | bytes 4194328
  10.0 2.2 %copy-done.1 = bf16[512,4096]{1,0:T(8,128)(2,1)S(1)} copy-done((bf16[512,4096]{1,0:T(8,128)(2,1)S(1)}, bf16[512,4096]{1,0:T(8,128)(2,1)}, u32[]{:S(2)}) %copy-start.1) | copy-done | bytes 4194328
  13.5 15.6 %collective-permute-done.refs_1_.refs_2_ = bf16[2,1920,128]{2,1,0:T(8,128)(2,1)S(1)} collective-permute-done((bf16[2,1920,128]{2,1,0:T(8,128)(2,1)}, bf16[2,1920,128]{2,1,0:T(8,128)(2,1)S(1)}, u32[]{:S(2)}, u32[]{:S(2)}) %collective-permute-start) | collective-permute-done | bytes 983072 | tf_op jit(solution)/shard_map/ppermute | solution.py:32
  29.1 3.3 %collective-permute-done.1.refs_2_.refs_3_ = bf16[2,1920,128]{2,1,0:T(8,128)(2,1)S(1)} collective-permute-done((bf16[2,1920,128]{2,1,0:T(8,128)(2,1)}, bf16[2,1920,128]{2,1,0:T(8,128)(2,1)S(1)}, u32[]{:S(2)}, u32[]{:S(2)}) %collective-permute-start.1) | collective-permute-done | bytes 983072 | tf_op jit(solution)/shard_map/ppermute | solution.py:28
  33.1 3.1 %collective-permute-start.3 = (bf16[1920,128]{1,0:T(8,128)(2,1)S(1)}, bf16[1920,128]{1,0:T(8,128)(2,1)S(1)}, u32[]{:S(2)}, u32[]{:S(2)}) collective-permute-start(bf16[1920,128]{1,0:T(8,128)(2,1)S(1)} %get-tuple-element.50), channel_id=1, source_target_pairs={{0,6},{1,7},{2,0},{3,1},{4,2},{5,3},{6,4},{7,5},{8,14},{9,15},{10,... | collective-permute-start | bytes 1474568 | tf_op jit(solution)/shard_map/ppermute | solution.py:32
  36.3 9.2 %collective-permute-done.2.refs_3_.refs_4_ = bf16[1920,128]{1,0:T(8,128)(2,1)S(1)} collective-permute-done((bf16[1920,128]{1,0:T(8,128)(2,1)S(1)}, bf16[1920,128]{1,0:T(8,128)(2,1)S(1)}, u32[]{:S(2)}, u32[]{:S(2)}) %collective-permute-start.2) | collective-permute-done | bytes 491552 | tf_op jit(solution)/shard_map/ppermute | solution.py:28
  48.8 3.5 %project.1 = (bf16[256,512]{1,0:T(8,128)(2,1)S(1)}, bf16[256,512]{1,0:T(8,128)(2,1)S(1)}, bf16[2,64,512]{2,1,0:T(8,128)(2,1)S(1)}) custom-call(bf16[2,1920,128]{2,1,0:T(8,128)(2,1)S(1)} %copy-done.2, bf16[2,1920,128]{2,1,0:T(8,128)(2,1)S(1)} %collective-permute-done.refs_1_.refs_2_, bf16[2,1920,128]{2,1,0:T(8,128)(2,1)S(1)} %collective-permute-done.1.refs_2_.refs_3_, ...), custom_call_target="tpu_custom_call" | custom-call | flops 2147483648 | bytes 8388608 | tf_op jit(solution)/shard_map/project/pallas_call | solution.py:331
  52.3 4.9 %collective-permute-start.9 = (bf16[2,64,512]{2,1,0:T(8,128)(2,1)S(1)}, bf16[2,64,512]{2,1,0:T(8,128)(2,1)S(1)}, u32[]{:S(2)}, u32[]{:S(2)}) collective-permute-start(bf16[2,64,512]{2,1,0:T(8,128)(2,1)S(1)} %get-tuple-element.27), channel_id=1, source_target_pairs={{8,0},{16,8},{24,16},{32,24},{40,32},{48,40},{56,48},{64,56},{72,6... | collective-permute-start | bytes 393224 | tf_op jit(solution)/shard_map/ppermute | solution.py:41
  57.2 7.8 %attend.1 = (bf16[256,512]{1,0:T(8,128)(2,1)S(1)}, bf16[256,512]{1,0:T(8,128)(2,1)S(1)}, f32[192,512]{1,0:T(8,128)S(1)}, bf16[4,2,128,896]{3,2,1,0:T(8,128)(2,1)S(1)}, bf16[4,2,128,896]{3,2,1,0:T(8,128)(2,1)S(1)}) custom-call(s32[2,4]{1,0:T(2,128)S(1)} %bitcast.66, bf16[2,1920,128]{2,1,0:T(8,128)(2,1)S(1)} %copy-done.2, ...), custom_call_target="tpu_custom_call" | custom-call | flops 3758096384 | bytes 8388608 | tf_op jit(solution)/shard_map/attend/pallas_call | solution.py:344
  65.1 2.0 %last.1 = (bf16[256,512]{1,0:T(8,128)(2,1)S(1)}, bf16[4,2,128,896]{3,2,1,0:T(8,128)(2,1)S(1)}, bf16[4,2,128,896]{3,2,1,0:T(8,128)(2,1)S(1)}) custom-call(s32[2,4]{1,0:T(2,128)S(1)} %bitcast.67, bf16[256,512]{1,0:T(8,128)(2,1)S(1)} %get-tuple-element.25.refs_13_.refs_1_, ...), custom_call_target="tpu_custom_call", output_to_operand_aliasing={{1}: (9, {}), {2}: (10, {})} | custom-call | flops 939524096 | bytes 4194304 | tf_op jit(solution)/shard_map/last/pallas_call | solution.py:362
  69.1 1.8 %collective-permute-done.16 = bf16[4,2,128,896]{3,2,1,0:T(8,128)(2,1)S(1)} collective-permute-done((bf16[4,2,128,896]{3,2,1,0:T(8,128)(2,1)S(1)}, bf16[4,2,128,896]{3,2,1,0:T(8,128)(2,1)S(1)}, u32[]{:S(2)}, u32[]{:S(2)}) %collective-permute-start.16) | collective-permute-done | bytes 1835040 | tf_op jit(solution)/shard_map/ppermute | solution.py:36
  71.3 3.8 %collective-permute-start.19 = (bf16[1,128,896]{2,1,0:T(8,128)(2,1)S(1)}, bf16[1,128,896]{2,1,0:T(8,128)(2,1)S(1)}, u32[]{:S(2)}, u32[]{:S(2)}) collective-permute-start(bf16[1,128,896]{2,1,0:T(8,128)(2,1)S(1)} %get-tuple-element.41), channel_id=1, source_target_pairs={{0,6},{1,7},{2,0},{3,1},{4,2},{5,3},{6,4},{7,5},{8,14},{9,15},{10,... | collective-permute-start | bytes 688136 | tf_op jit(solution)/shard_map/ppermute | solution.py:32
  75.3 3.2 %collective-permute-start.13 = (bf16[128,512]{1,0:T(8,128)(2,1)S(1)}, bf16[128,512]{1,0:T(8,128)(2,1)S(1)}, u32[]{:S(2)}, u32[]{:S(2)}) collective-permute-start(bf16[128,512]{1,0:T(8,128)(2,1)S(1)} %get-tuple-element.47), channel_id=1, source_target_pairs={{0,6},{1,7},{2,0},{3,1},{4,2},{5,3},{6,4},{7,5},{8,14},{9,15},{10,... | collective-permute-start | bytes 393224 | tf_op jit(solution)/shard_map/ppermute | solution.py:32
  78.5 2.8 %collective-permute-done.17 = bf16[1,128,896]{2,1,0:T(8,128)(2,1)S(1)} collective-permute-done((bf16[1,128,896]{2,1,0:T(8,128)(2,1)S(1)}, bf16[1,128,896]{2,1,0:T(8,128)(2,1)S(1)}, u32[]{:S(2)}, u32[]{:S(2)}) %collective-permute-start.17) | collective-permute-done | bytes 229408 | tf_op jit(solution)/shard_map/ppermute | solution.py:28
  81.6 3.4 %collective-permute-start.20 = (bf16[2,128,896]{2,1,0:T(8,128)(2,1)S(1)}, bf16[2,128,896]{2,1,0:T(8,128)(2,1)S(1)}, u32[]{:S(2)}, u32[]{:S(2)}) collective-permute-start(bf16[2,128,896]{2,1,0:T(8,128)(2,1)S(1)} %pad_maximum_fusion.2), channel_id=1, source_target_pairs={{0,6},{1,7},{2,0},{3,1},{4,2},{5,3},{6,4},{7,5},{8,14},{9,15},{10,... | collective-permute-start | bytes 1376264 | tf_op jit(solution)/shard_map/ppermute | solution.py:32
  85.3 3.3 %collective-permute-start.14 = (bf16[256,512]{1,0:T(8,128)(2,1)S(1)}, bf16[256,512]{1,0:T(8,128)(2,1)}, u32[]{:S(2)}, u32[]{:S(2)}) collective-permute-start(bf16[256,512]{1,0:T(8,128)(2,1)S(1)} %pad_maximum_fusion.4), channel_id=1, source_target_pairs={{0,6},{1,7},{2,0},{3,1},{4,2},{5,3},{6,4},{7,5},{8,14},{9,15},{10,... | collective-permute-start | bytes 786440 | tf_op jit(solution)/shard_map/ppermute | solution.py:32
  88.7 7.3 %collective-permute-done.20 = bf16[2,128,896]{2,1,0:T(8,128)(2,1)S(1)} collective-permute-done((bf16[2,128,896]{2,1,0:T(8,128)(2,1)S(1)}, bf16[2,128,896]{2,1,0:T(8,128)(2,1)S(1)}, u32[]{:S(2)}, u32[]{:S(2)}) %collective-permute-start.20) | collective-permute-done | bytes 458784 | tf_op jit(solution)/shard_map/ppermute | solution.py:32
  96.0 3.8 %collective-permute-done.18 = bf16[2,128,896]{2,1,0:T(8,128)(2,1)S(1)} collective-permute-done((bf16[2,128,896]{2,1,0:T(8,128)(2,1)S(1)}, bf16[2,128,896]{2,1,0:T(8,128)(2,1)S(1)}, u32[]{:S(2)}, u32[]{:S(2)}) %collective-permute-start.18) | collective-permute-done | bytes 458784 | tf_op jit(solution)/shard_map/ppermute | solution.py:28
  100.9 5.2 %all-to-all-start = ((bf16[16,2,8,1024]{3,2,1,0:T(8,128)(2,1)}), bf16[16,2,8,1024]{3,2,1,0:T(8,128)(2,1)S(1)}, u32[]{:S(2)}, u32[]{:S(2)}) async-start(bf16[16,2,8,1024]{3,2,1,0:T(8,128)(2,1)} %pad_maximum_fusion), calls=%async_computation | async-start | bytes 1048576 | tf_op jit(solution)/shard_map/all_to_all | solution.py:386
  107.3 3.4 %collective-permute-start.15 = (bf16[63,512]{1,0:T(8,128)(2,1)S(1)}, bf16[63,512]{1,0:T(8,128)(2,1)S(1)}, u32[]{:S(2)}, u32[]{:S(2)}) collective-permute-start(bf16[63,512]{1,0:T(8,128)(2,1)S(1)} %slice.267), channel_id=1, source_target_pairs={{0,8},{8,16},{16,24},{24,32},{32,40},{40,48},{48,56},{56,64},{64,7... | collective-permute-start | bytes 193544 | tf_op jit(solution)/shard_map/ppermute | solution.py:41
  110.7 4.9 %collective-permute-done.15 = bf16[63,512]{1,0:T(8,128)(2,1)S(1)} collective-permute-done((bf16[63,512]{1,0:T(8,128)(2,1)S(1)}, bf16[63,512]{1,0:T(8,128)(2,1)S(1)}, u32[]{:S(2)}, u32[]{:S(2)}) %collective-permute-start.15) | collective-permute-done | bytes 64544 | tf_op jit(solution)/shard_map/ppermute | solution.py:41
  117.2 2.8 %scatter.1 = f32[96,8,896]{2,1,0:T(8,128)} custom-call(s32[32]{0:T(128)S(1)} %fusion.18.label_ref, bf16[32,8,1024]{2,1,0:T(8,128)(2,1)S(1)} %bitcast.64), custom_call_target="tpu_custom_call" | custom-call | flops 274877906944 | bytes 4294967296 | tf_op jit(solution)/shard_map/scatter/pallas_call | solution.py:407
  (65 shorter events, 12.3 us)
Async XLA Ops:
  3.7 25.4 %collective-permute-start = (bf16[2,1920,128]{2,1,0:T(8,128)(2,1)}, bf16[2,1920,128]{2,1,0:T(8,128)(2,1)S(1)}, u32[]{:S(2)}, u32[]{:S(2)}) collective-permute-start(bf16[2,1920,128]{2,1,0:T(8,128)(2,1)} %get-tuple-element.20.refs_0_.refs_1_), channel_id=1, source_target_pairs={{0,6},{1,7},{2,0},{3,1},{4,2},{5,3},{6,4},{7,5},{8,14},{9,15},{10,... | collective-permute-start | bytes 2949128 | tf_op jit(solution)/shard_map/ppermute | solution.py:32
  7.8 24.6 %collective-permute-start.1 = (bf16[2,1920,128]{2,1,0:T(8,128)(2,1)}, bf16[2,1920,128]{2,1,0:T(8,128)(2,1)S(1)}, u32[]{:S(2)}, u32[]{:S(2)}) collective-permute-start(bf16[2,1920,128]{2,1,0:T(8,128)(2,1)} %get-tuple-element.20.refs_0_.refs_1_), channel_id=1, source_target_pairs={{0,2},{1,3},{2,4},{3,5},{4,6},{5,7},{6,0},{7,1},{8,10},{9,11},{10,... | collective-permute-start | bytes 2949128 | tf_op jit(solution)/shard_map/ppermute | solution.py:28
  7.8 39.2 %collective-permute-start.4 = (bf16[2,1920,128]{2,1,0:T(8,128)(2,1)}, bf16[2,1920,128]{2,1,0:T(8,128)(2,1)S(1)}, u32[]{:S(2)}, u32[]{:S(2)}) collective-permute-start(bf16[2,1920,128]{2,1,0:T(8,128)(2,1)} %get-tuple-element.20.refs_0_.refs_1_), channel_id=1, source_target_pairs={{0,1},{1,0},{2,3},{3,2},{4,5},{5,4},{6,7},{7,6},{8,9},{9,8},{10,11... | collective-permute-start | bytes 2949128 | tf_op jit(solution)/shard_map/ppermute | solution.py:36
  13.4 35.4 %copy-start.2 = (bf16[2,1920,128]{2,1,0:T(8,128)(2,1)S(1)}, bf16[2,1920,128]{2,1,0:T(8,128)(2,1)}, u32[]{:S(2)}) copy-start(bf16[2,1920,128]{2,1,0:T(8,128)(2,1)} %get-tuple-element.20.refs_0_.refs_1_) | copy-start | bytes 2949124
  32.5 13.1 %collective-permute-start.2 = (bf16[1920,128]{1,0:T(8,128)(2,1)S(1)}, bf16[1920,128]{1,0:T(8,128)(2,1)S(1)}, u32[]{:S(2)}, u32[]{:S(2)}) collective-permute-start(bf16[1920,128]{1,0:T(8,128)(2,1)S(1)} %get-tuple-element.51), channel_id=1, source_target_pairs={{0,2},{1,3},{2,4},{3,5},{4,6},{5,7},{6,0},{7,1},{8,10},{9,11},{10,... | collective-permute-start | bytes 1474568 | tf_op jit(solution)/shard_map/ppermute | solution.py:28
  32.6 14.4 %collective-permute-start.5 = (bf16[2,1920,128]{2,1,0:T(8,128)(2,1)S(1)}, bf16[2,1920,128]{2,1,0:T(8,128)(2,1)S(1)}, u32[]{:S(2)}, u32[]{:S(2)}) collective-permute-start(bf16[2,1920,128]{2,1,0:T(8,128)(2,1)S(1)} %collective-permute-done.refs_1_.refs_2_), channel_id=1, source_target_pairs={{0,1},{1,0},{2,3},{3,2},{4,5},{5,4},{6,7},{7,6},{8,9},{9,8},{10,11... | collective-permute-start | bytes 2949128 | tf_op jit(solution)/shard_map/ppermute | solution.py:36
  32.6 14.3 %collective-permute-start.6 = (bf16[2,1920,128]{2,1,0:T(8,128)(2,1)S(1)}, bf16[2,1920,128]{2,1,0:T(8,128)(2,1)S(1)}, u32[]{:S(2)}, u32[]{:S(2)}) collective-permute-start(bf16[2,1920,128]{2,1,0:T(8,128)(2,1)S(1)} %collective-permute-done.1.refs_2_.refs_3_), channel_id=1, source_target_pairs={{0,1},{1,0},{2,3},{3,2},{4,5},{5,4},{6,7},{7,6},{8,9},{9,8},{10,11... | collective-permute-start | bytes 2949128 | tf_op jit(solution)/shard_map/ppermute | solution.py:36
  33.1 13.8 %collective-permute-start.3 = (bf16[1920,128]{1,0:T(8,128)(2,1)S(1)}, bf16[1920,128]{1,0:T(8,128)(2,1)S(1)}, u32[]{:S(2)}, u32[]{:S(2)}) collective-permute-start(bf16[1920,128]{1,0:T(8,128)(2,1)S(1)} %get-tuple-element.50), channel_id=1, source_target_pairs={{0,6},{1,7},{2,0},{3,1},{4,2},{5,3},{6,4},{7,5},{8,14},{9,15},{10,... | collective-permute-start | bytes 1474568 | tf_op jit(solution)/shard_map/ppermute | solution.py:32
  45.5 1.9 %collective-permute-start.7 = (bf16[1920,128]{1,0:T(8,128)(2,1)S(1)}, bf16[1920,128]{1,0:T(8,128)(2,1)S(1)}, u32[]{:S(2)}, u32[]{:S(2)}) collective-permute-start(bf16[1920,128]{1,0:T(8,128)(2,1)S(1)} %collective-permute-done.2.refs_3_.refs_4_), channel_id=1, source_target_pairs={{0,1},{1,0},{2,3},{3,2},{4,5},{5,4},{6,7},{7,6},{8,9},{9,8},{10,11... | collective-permute-start | bytes 1474568 | tf_op jit(solution)/shard_map/ppermute | solution.py:36
  46.9 1.9 %collective-permute-start.8 = (bf16[1920,128]{1,0:T(8,128)(2,1)S(1)}, bf16[1920,128]{1,0:T(8,128)(2,1)S(1)}, u32[]{:S(2)}, u32[]{:S(2)}) collective-permute-start(bf16[1920,128]{1,0:T(8,128)(2,1)S(1)} %collective-permute-done.3.refs_4_.refs_5_), channel_id=1, source_target_pairs={{0,1},{1,0},{2,3},{3,2},{4,5},{5,4},{6,7},{7,6},{8,9},{9,8},{10,11... | collective-permute-start | bytes 1474568 | tf_op jit(solution)/shard_map/ppermute | solution.py:36
  52.3 12.8 %collective-permute-start.9 = (bf16[2,64,512]{2,1,0:T(8,128)(2,1)S(1)}, bf16[2,64,512]{2,1,0:T(8,128)(2,1)S(1)}, u32[]{:S(2)}, u32[]{:S(2)}) collective-permute-start(bf16[2,64,512]{2,1,0:T(8,128)(2,1)S(1)} %get-tuple-element.27), channel_id=1, source_target_pairs={{8,0},{16,8},{24,16},{32,24},{40,32},{48,40},{56,48},{64,56},{72,6... | collective-permute-start | bytes 393224 | tf_op jit(solution)/shard_map/ppermute | solution.py:41
  67.1 3.9 %collective-permute-start.16 = (bf16[4,2,128,896]{3,2,1,0:T(8,128)(2,1)S(1)}, bf16[4,2,128,896]{3,2,1,0:T(8,128)(2,1)S(1)}, u32[]{:S(2)}, u32[]{:S(2)}) collective-permute-start(bf16[4,2,128,896]{3,2,1,0:T(8,128)(2,1)S(1)} %get-tuple-element.37), channel_id=1, source_target_pairs={{0,1},{1,0},{2,3},{3,2},{4,5},{5,4},{6,7},{7,6},{8,9},{9,8},{10,11... | collective-permute-start | bytes 5505032 | tf_op jit(solution)/shard_map/ppermute | solution.py:36
  68.6 6.5 %collective-permute-start.10 = (bf16[4,256,512]{2,1,0:T(8,128)(2,1)S(1)}, bf16[4,256,512]{2,1,0:T(8,128)(2,1)S(1)}, u32[]{:S(2)}, u32[]{:S(2)}) collective-permute-start(bf16[4,256,512]{2,1,0:T(8,128)(2,1)S(1)} %get-tuple-element.35), channel_id=1, source_target_pairs={{0,1},{1,0},{2,3},{3,2},{4,5},{5,4},{6,7},{7,6},{8,9},{9,8},{10,11... | collective-permute-start | bytes 3145736 | tf_op jit(solution)/shard_map/ppermute | solution.py:36
  71.2 10.1 %collective-permute-start.17 = (bf16[1,128,896]{2,1,0:T(8,128)(2,1)S(1)}, bf16[1,128,896]{2,1,0:T(8,128)(2,1)S(1)}, u32[]{:S(2)}, u32[]{:S(2)}) collective-permute-start(bf16[1,128,896]{2,1,0:T(8,128)(2,1)S(1)} %get-tuple-element.40), channel_id=1, source_target_pairs={{0,2},{1,3},{2,4},{3,5},{4,6},{5,7},{6,0},{7,1},{8,10},{9,11},{10,... | collective-permute-start | bytes 688136 | tf_op jit(solution)/shard_map/ppermute | solution.py:28
  71.3 10.1 %collective-permute-start.19 = (bf16[1,128,896]{2,1,0:T(8,128)(2,1)S(1)}, bf16[1,128,896]{2,1,0:T(8,128)(2,1)S(1)}, u32[]{:S(2)}, u32[]{:S(2)}) collective-permute-start(bf16[1,128,896]{2,1,0:T(8,128)(2,1)S(1)} %get-tuple-element.41), channel_id=1, source_target_pairs={{0,6},{1,7},{2,0},{3,1},{4,2},{5,3},{6,4},{7,5},{8,14},{9,15},{10,... | collective-permute-start | bytes 688136 | tf_op jit(solution)/shard_map/ppermute | solution.py:32
  75.2 10.0 %collective-permute-start.11 = (bf16[128,512]{1,0:T(8,128)(2,1)S(1)}, bf16[128,512]{1,0:T(8,128)(2,1)S(1)}, u32[]{:S(2)}, u32[]{:S(2)}) collective-permute-start(bf16[128,512]{1,0:T(8,128)(2,1)S(1)} %get-tuple-element.46), channel_id=1, source_target_pairs={{0,2},{1,3},{2,4},{3,5},{4,6},{5,7},{6,0},{7,1},{8,10},{9,11},{10,... | collective-permute-start | bytes 393224 | tf_op jit(solution)/shard_map/ppermute | solution.py:28
  75.3 9.9 %collective-permute-start.13 = (bf16[128,512]{1,0:T(8,128)(2,1)S(1)}, bf16[128,512]{1,0:T(8,128)(2,1)S(1)}, u32[]{:S(2)}, u32[]{:S(2)}) collective-permute-start(bf16[128,512]{1,0:T(8,128)(2,1)S(1)} %get-tuple-element.47), channel_id=1, source_target_pairs={{0,6},{1,7},{2,0},{3,1},{4,2},{5,3},{6,4},{7,5},{8,14},{9,15},{10,... | collective-permute-start | bytes 393224 | tf_op jit(solution)/shard_map/ppermute | solution.py:32
  81.6 14.4 %collective-permute-start.20 = (bf16[2,128,896]{2,1,0:T(8,128)(2,1)S(1)}, bf16[2,128,896]{2,1,0:T(8,128)(2,1)S(1)}, u32[]{:S(2)}, u32[]{:S(2)}) collective-permute-start(bf16[2,128,896]{2,1,0:T(8,128)(2,1)S(1)} %pad_maximum_fusion.2), channel_id=1, source_target_pairs={{0,6},{1,7},{2,0},{3,1},{4,2},{5,3},{6,4},{7,5},{8,14},{9,15},{10,... | collective-permute-start | bytes 1376264 | tf_op jit(solution)/shard_map/ppermute | solution.py:32
  85.1 14.7 %collective-permute-start.18 = (bf16[2,128,896]{2,1,0:T(8,128)(2,1)S(1)}, bf16[2,128,896]{2,1,0:T(8,128)(2,1)S(1)}, u32[]{:S(2)}, u32[]{:S(2)}) collective-permute-start(bf16[2,128,896]{2,1,0:T(8,128)(2,1)S(1)} %pad_maximum_fusion.1), channel_id=1, source_target_pairs={{0,2},{1,3},{2,4},{3,5},{4,6},{5,7},{6,0},{7,1},{8,10},{9,11},{10,... | collective-permute-start | bytes 1376264 | tf_op jit(solution)/shard_map/ppermute | solution.py:28
  85.3 20.8 %collective-permute-start.14 = (bf16[256,512]{1,0:T(8,128)(2,1)S(1)}, bf16[256,512]{1,0:T(8,128)(2,1)}, u32[]{:S(2)}, u32[]{:S(2)}) collective-permute-start(bf16[256,512]{1,0:T(8,128)(2,1)S(1)} %pad_maximum_fusion.4), channel_id=1, source_target_pairs={{0,6},{1,7},{2,0},{3,1},{4,2},{5,3},{6,4},{7,5},{8,14},{9,15},{10,... | collective-permute-start | bytes 786440 | tf_op jit(solution)/shard_map/ppermute | solution.py:32
  88.6 17.5 %collective-permute-start.12 = (bf16[256,512]{1,0:T(8,128)(2,1)S(1)}, bf16[256,512]{1,0:T(8,128)(2,1)}, u32[]{:S(2)}, u32[]{:S(2)}) collective-permute-start(bf16[256,512]{1,0:T(8,128)(2,1)S(1)} %pad_maximum_fusion.3), channel_id=1, source_target_pairs={{0,2},{1,3},{2,4},{3,5},{4,6},{5,7},{6,0},{7,1},{8,10},{9,11},{10,... | collective-permute-start | bytes 786440 | tf_op jit(solution)/shard_map/ppermute | solution.py:28
  100.9 14.7 %copy-start.8 = (bf16[256,512]{1,0:T(8,128)(2,1)S(1)}, bf16[256,512]{1,0:T(8,128)(2,1)}, u32[]{:S(2)}) copy-start(bf16[256,512]{1,0:T(8,128)(2,1)} %cotangent_ref.1) | copy-start | bytes 786436
  100.9 15.6 %all-to-all-start = ((bf16[16,2,8,1024]{3,2,1,0:T(8,128)(2,1)}), bf16[16,2,8,1024]{3,2,1,0:T(8,128)(2,1)S(1)}, u32[]{:S(2)}, u32[]{:S(2)}) async-start(bf16[16,2,8,1024]{3,2,1,0:T(8,128)(2,1)} %pad_maximum_fusion), calls=%async_computation | async-start | bytes 1048576 | tf_op jit(solution)/shard_map/all_to_all | solution.py:386
  107.3 8.3 %collective-permute-start.15 = (bf16[63,512]{1,0:T(8,128)(2,1)S(1)}, bf16[63,512]{1,0:T(8,128)(2,1)S(1)}, u32[]{:S(2)}, u32[]{:S(2)}) collective-permute-start(bf16[63,512]{1,0:T(8,128)(2,1)S(1)} %slice.267), channel_id=1, source_target_pairs={{0,8},{8,16},{16,24},{24,32},{32,40},{40,48},{48,56},{56,64},{64,7... | collective-permute-start | bytes 193544 | tf_op jit(solution)/shard_map/ppermute | solution.py:41
  (7 other events, 32.3 us)

commit v3 on v2

--- a/solution.py
+++ b/solution.py
@@ -21,7 +21,6 @@
 VMEM = pl.BlockSpec(memory_space=pltpu.VMEM)
 SMEM = pl.BlockSpec(memory_space=pltpu.SMEM)
 ANY = pl.BlockSpec(memory_space=pl.ANY)
-HBM = pl.BlockSpec(memory_space=pltpu.HBM)
 
 
 def up(x):
@@ -95,38 +94,48 @@
         each.wait()
 
 
-def hold_kernel(label_ref, a_ref, b_ref, a_out, b_out, done_ref, sems):
-    copies = [
-        pltpu.make_async_copy(src, dst, sems.at[at])
-        for at, (src, dst) in enumerate(((a_ref, a_out), (b_ref, b_out)))
-    ]
-    for copy in copies:
-        copy.start()
-    for copy in copies:
-        copy.wait()
-    done_ref[...] = label_ref[...]
+def near_kernel(*refs):
+    blocks, weights, (wk_ref, wv_ref) = refs[:6], refs[6:8], refs[8:10]
+    (sum_ref, k_ref, v_ref), (full, mem_s) = refs[10:13], refs[13:]
+    me = lax.axis_index("db")
+    rows, width = sum_ref.shape[1:]
+    base = rows * width // HDIM
+    for core in range(2):
+        far = pl.multiple_of(source_of(me, core, 2) * width, width)
+        full[:, :, pl.ds(far, width)] = jnp.zeros((2, rows, width), BF16)
+        for at, place in enumerate((0, 1, 3)):
+            block = blocks[core * 3 + at]
+            spot = pl.multiple_of(source_of(me, core, place) * width, width)
+            for item in range(2):
+                for j in range(width // HDIM):
+                    full[item, :, pl.ds(spot + j * HDIM, HDIM)] = block[item, pl.ds(j * rows, rows)]
+                slot = ((core * 3 + at) * 2 + item) * R
+                for j in range(DE // HDIM):
+                    part = block[item, pl.ds(base + j * R, R)]
+                    mem_s[pl.ds(slot, R), pl.ds(j * HDIM, HDIM)] = part
+    sum_ref[0] = jnp.dot(full[0], weights[0][...], preferred_element_type=F32)
+    sum_ref[1] = lax.dot_general(full[1], weights[1][...], NT, preferred_element_type=F32)
+    k_ref[...] = jnp.dot(mem_s[...], wk_ref[...], preferred_element_type=F32).astype(BF16)
+    v_ref[...] = jnp.dot(mem_s[...], wv_ref[...], preferred_element_type=F32).astype(BF16)
 
 
 def project_kernel(*refs):
-    blocks, weights, outs, tail_ref, full = refs[:10], refs[10:12], refs[12:14], *refs[14:]
+    fars, weights, sum_ref, outs, tail_ref, x_s = refs[:4], refs[4:6], refs[6], refs[7:9], *refs[9:]
     me = lax.axis_index("db")
     rows, width = outs[0].shape
     for item in range(2):
+        total = sum_ref[item]
         for core in range(2):
-            own, nxt, prv, *far = blocks[core * 5 : core * 5 + 5]
-            for place, block in ((0, own), (1, nxt), (3, prv), (2, far[item])):
-                spot = pl.multiple_of(source_of(me, core, place) * width, width)
-                for j in range(width // HDIM):
-                    part = pl.ds(j * rows, rows)
-                    full[item, :, pl.ds(spot + j * HDIM, HDIM)] = (
-                        block[part] if place == 2 else block[item, part]
-                    )
-    for item in range(2):
-        w = weights[item][...]
-        if item:
-            total = lax.dot_general(full[item], w, NT, preferred_element_type=F32)
-        else:
-            total = jnp.dot(full[item], w, preferred_element_type=F32)
+            for j in range(width // HDIM):
+                x_s[:, pl.ds(j * HDIM, HDIM)] = fars[core * 2 + item][pl.ds(j * rows, rows)]
+            spot = pl.ds(pl.multiple_of(source_of(me, core, 2) * width, width), width)
+            if item:
+                part = lax.dot_general(
+                    x_s[...], weights[1][:, spot], NT, preferred_element_type=F32
+                )
+            else:
+                part = jnp.dot(x_s[...], weights[0][spot, :], preferred_element_type=F32)
+            total = total + part
         total = pltpu.roll(total, rows - BORDER, 0).astype(BF16)
         outs[item][...] = total
         tail_ref[item] = total[rows - CH :]
@@ -181,37 +190,32 @@
 
 
 def attend_kernel(*refs):
-    shard_ref, mems, wk_ref, wv_ref, q_ref, g_ref = refs[0], refs[1:11], *refs[11:15]
-    k_ref, v_ref, gq_ref, away_ref, own_ref = refs[15:20]
-    mem_s, k_s, v_s, gk_s, gv_s, term_s = refs[20:]
+    shard_ref, fars, k_near, v_near, wk_ref, wv_ref, q_ref, g_ref = refs[0], refs[1:5], *refs[5:11]
+    k_ref, v_ref, gq_ref, away_ref, own_ref = refs[11:16]
+    mem_s, k_far, v_far, k_s, v_s, gk_s, gv_s, term_s = refs[16:]
     rows, width = q_ref.shape
     spans = rows // CH
+    base = rows * width // HDIM
+    for slot, far in enumerate(fars):
+        for j in range(DE // HDIM):
+            part = far[pl.ds(base + j * R, R)]
+            mem_s[pl.ds(slot * R, R), pl.ds(j * HDIM, HDIM)] = part
+    k_far[...] = jnp.dot(mem_s[...], wk_ref[...], preferred_element_type=F32).astype(BF16)
+    v_far[...] = jnp.dot(mem_s[...], wv_ref[...], preferred_element_type=F32).astype(BF16)
     found = places_of(shard_ref)
-    base = rows * width // HDIM
-
-    def take(request, read):
-        for j in range(DE // HDIM):
-            part = read(pl.ds(base + j * R, R))
-            mem_s[pl.ds(request * R, R), pl.ds(j * HDIM, HDIM)] = part
-
     for request, (core, place, rank) in enumerate(found):
-        for which in range(2):
-            own, nxt, prv, far0, far1 = mems[which * 5 : which * 5 + 5]
-            here = core == which
-            for at, ref in ((0, own), (1, nxt), (3, prv)):
-
-                @pl.when(here & (place == at))
-                def _(ref=ref, rank=rank, request=request):
-                    take(request, lambda part: ref[rank, part])
-
-            for at, ref in ((0, far0), (1, far1)):
-
-                @pl.when(here & (place == 2) & (rank == at))
-                def _(ref=ref, request=request):
-                    take(request, lambda part: ref[part])
-
-    k_s[...] = jnp.dot(mem_s[...], wk_ref[...], preferred_element_type=F32).astype(BF16)
-    v_s[...] = jnp.dot(mem_s[...], wv_ref[...], preferred_element_type=F32).astype(BF16)
+        spot = pl.ds(request * R, R)
+
+        @pl.when(place == 2)
+        def _(spot=spot, slot=core * 2 + rank):
+            source = pl.ds(pl.multiple_of(slot * R, R), R)
+            k_s[spot], v_s[spot] = k_far[source], v_far[source]
+
+        @pl.when(place != 2)
+        def _(spot=spot, slot=(core * 3 + jnp.minimum(place, 2)) * 2 + rank):
+            source = pl.ds(pl.multiple_of(slot * R, R), R)
+            k_s[spot], v_s[spot] = k_near[source], v_near[source]
+
     heads = [pl.ds(h * HDIM, HDIM) for h in range(width // HDIM)]
     for c in range(spans - 1):
         span, memory = pl.ds(c * CH, CH), pl.ds(c * K * R, K * R)
@@ -276,15 +280,6 @@
     return x + jnp.where(token > 0, -0.0, 0.0).astype(x.dtype)
 
 
-def gather_two(own, token):
-    nxt, prv = down(own), up(own)
-    return own, nxt, prv, up(after(prv[0], token)), down(after(nxt[1], token))
-
-
-def with_other_core(blocks):
-    return tuple(blocks) + tuple(across(x) for x in blocks)
-
-
 def add(*parts):
     return functools.reduce(lambda a, b: a + b, [x.astype(F32) for x in parts])
 
@@ -317,27 +312,32 @@
         out_specs=(VMEM, VMEM),
         scratch_shapes=[pltpu.SemaphoreType.DMA((2 * (width + DE) // HDIM,))],
     )(shards, named_rows, states, cotangent, database)
-    *held, done = pl.pallas_call(
-        hold_kernel,
-        name="hold",
-        out_shape=(shape(w_query.shape), shape(w_out.shape), shape(label.shape, F32)),
-        in_specs=[VMEM, HBM, HBM],
+    nxt, prv = down(given), up(given)
+    far_a, far_b = up(prv[0]), down(nxt[1])
+    near = (given, nxt, prv, across(given), across(nxt), across(prv))
+    partial, *near_states = pl.pallas_call(
+        near_kernel,
+        name="near",
+        out_shape=(shape((2, rows, width), F32),) + (shape((12 * R, width)),) * 2,
+        in_specs=[VMEM] * 10,
         out_specs=(VMEM,) * 3,
-        scratch_shapes=[pltpu.SemaphoreType.DMA((2,))],
-        compiler_params=limit,
-    )(label, w_query, w_out)
-    gathered = with_other_core(gather_two(given, done[0, :1]))
-
+        scratch_shapes=[pltpu.VMEM((2, rows, 8 * width), BF16), pltpu.VMEM((12 * R, DE), BF16)],
+        compiler_params=limit,
+        cost_estimate=cost(32 * rows * width * width, 2**23),
+    )(*near, w_query, w_out, w_key, w_value)
+    token = partial[0, :1, :HDIM]
+    far_a, far_b = after(far_a, token), after(far_b, token)
+    fars = (far_a, far_b, across(far_a), across(far_b))
     query, grad_out, tails = pl.pallas_call(
         project_kernel,
         name="project",
         out_shape=(shape((rows, width)), shape((rows, width)), shape((2, CH, width))),
-        in_specs=[VMEM] * 12,
+        in_specs=[VMEM] * 7,
         out_specs=(VMEM,) * 3,
-        scratch_shapes=[pltpu.VMEM((2, rows, 8 * width), BF16)],
-        compiler_params=limit,
-        cost_estimate=cost(32 * rows * width * width, 2**23),
-    )(*gathered, *held)
+        scratch_shapes=[pltpu.VMEM((rows, width), BF16)],
+        compiler_params=limit,
+        cost_estimate=cost(8 * rows * width * width, 2**23),
+    )(*fars, w_query, w_out, partial)
     tails = along_ctx(tails, -1)
     positions, slots_of = spans * K * R, shape((4, CAP, R, DE))
     most = positions - K * R
@@ -346,10 +346,12 @@
         name="attend",
         out_shape=(shape((K * R, width)), shape((K * R, width)), shape((rows - CH, width), F32))
         + (slots_of, slots_of),
-        in_specs=[SMEM] + [VMEM] * 14,
+        in_specs=[SMEM] + [VMEM] * 10,
         out_specs=(VMEM,) * 5,
         scratch_shapes=[
-            pltpu.VMEM((positions, DE), BF16),
+            pltpu.VMEM((4 * R, DE), BF16),
+            pltpu.VMEM((4 * R, width), BF16),
+            pltpu.VMEM((4 * R, width), BF16),
             pltpu.VMEM((positions, width), BF16),
             pltpu.VMEM((positions, width), BF16),
             pltpu.VMEM((most, width), BF16),
@@ -358,7 +360,7 @@
         ],
         compiler_params=limit,
         cost_estimate=cost(8 * positions * DE * width, 2**23),
-    )(shards, *gathered, w_key, w_value, query, grad_out)
+    )(shards, *fars, *near_states, w_key, w_value, query, grad_out)
     grad_query, away, own = pl.pallas_call(
         last_kernel,
         name="last",
@@ -394,7 +396,7 @@
         out_specs=(VMEM, VMEM),
         compiler_params=limit,
         cost_estimate=cost(2 * rows * width * 8 * width, 2**23),
-    )(grad_query, held[0])
+    )(grad_query, w_query)
     cross_got, half = across(cross_away), rows // 2
     far_up, far_down = far_sums(cross_own, cross_got, half)
     far_up, far_down = up(far_up.astype(BF16)), down(far_down.astype(BF16))

time: 120 us -> 115 us (0.958)
  waiting for transfers between devices: 52.1 us -> 44.1 us
  Pallas kernels: 21 us -> 22.6 us
    pallas_call x1, Pallas kernels: 0.58 us -> 6.52 us  [per_device(): pl.pallas_call(near_kernel, name='near', out_shape=(shape((2, rows, width...]
    ppermute x6, waiting for transfers between devices: 19.2 us -> 14 us  [up(): return lax.ppermute(x, 'db', [(s, (s + 2) % 8) for s in range(8)])]
    ppermute x6, waiting for transfers between devices: 24.4 us -> 21.3 us  [down(): return lax.ppermute(x, 'db', [(s, (s - 2) % 8) for s in range(8)])]
    pallas_call x1, Pallas kernels: 3.5 us -> 0.85 us  [per_device(): pl.pallas_call(project_kernel, name='project', out_shape=(shape((rows, wi...]
    pallas_call x1, Pallas kernels: 7.82 us -> 6.17 us  [per_device(): pl.pallas_call(attend_kernel, name='attend', out_shape=(shape((K * R, wid...]
    unnamed x18 -> x20, local copies, waits for them, and re-layouts: 5.1 us -> 5.61 us
  transfers between devices with their start and end apart: 22 -> 22, of which waited for: 11 -> 8; matrix products, arithmetic and copies ran while one was open for 3% -> 4% of each run, Pallas kernels for 8% -> 12%
where the time goes in v3:
time: 115 us; the launch traced here: 114 us
  waiting for transfers between devices  44.1 us (38%)
  starting transfers between devices  36.2 us (31%)
  Pallas kernels  22.6 us (20%)
  local copies, waits for them, and re-layouts  5.73 us (5%)
  other arithmetic  4.69 us (4%)
    ppermute x6, waiting for transfers between devices, down(): return lax.ppermute(x, 'db', [(s, (s - 2) % 8) for s in range(8)])  21.3 us
    ppermute x6, starting transfers between devices, down(): return lax.ppermute(x, 'db', [(s, (s - 2) % 8) for s in range(8)])  19.9 us
    ppermute x6, waiting for transfers between devices, up(): return lax.ppermute(x, 'db', [(s, (s + 2) % 8) for s in range(8)])  14 us
    ppermute x2, starting transfers between devices, along_ctx(): lax.ppermute(x, 'ctx', [(i, i + by) for i in range(peers) if 0 <= i + by...  8.26 us
    pallas_call x1, Pallas kernels, per_device(): pl.pallas_call(near_kernel, name='near', out_shape=(shape((2, rows, width...  6.52 us
    pallas_call x1, Pallas kernels, per_device(): pl.pallas_call(attend_kernel, name='attend', out_shape=(shape((K * R, wid...  6.17 us
    all_to_all x1, starting transfers between devices, per_device(): parts = lax.all_to_all(spread, 'ctx', 0, 0, tiled=True)  5.89 us
    unnamed x20, local copies, waits for them, and re-layouts  5.61 us
  transfers between devices with their start and end apart: 22, of which 8 were waited for; matrix products, arithmetic and copies ran while one was open for 4% of the time, Pallas kernels for 12%

profile of v3, /device:TPU:2, one launch (start us, length us, event | category | flops | bytes accessed | tf_op | source)
XLA Modules:
  0.0 114.4 jit_solution(9009589679679657453)
XLA Ops:
  0.6 3.0 %load.1 = (bf16[2,1920,128]{2,1,0:T(8,128)(2,1)}, f32[2,8,128]{2,1,0:T(8,128)}) custom-call(s32[2,4]{1,0:T(2,128)} %bitcast.61, s32[2,4]{1,0:T(2,128)} %bitcast.64, bf16[256,512]{1,0:T(8,128)(2,1)} %states_ref.1, bf16[256,512]{1,0:T(8,128)(2,1)} %cotangent_ref.1, bf16[96,128,896]{2,1,0:T(8,128)(2,1)} %database_ref.1), custom_call_target="tpu_custom_call" | custom-call | tf_op jit(solution)/shard_map/load/pallas_call | solution.py:307
  3.7 4.1 %collective-permute-start.2 = (bf16[2,1920,128]{2,1,0:T(8,128)(2,1)}, bf16[2,1920,128]{2,1,0:T(8,128)(2,1)S(1)}, u32[]{:S(2)}, u32[]{:S(2)}) collective-permute-start(bf16[2,1920,128]{2,1,0:T(8,128)(2,1)} %get-tuple-element.20.refs_0_), channel_id=1, source_target_pairs={{0,6},{1,7},{2,0},{3,1},{4,2},{5,3},{6,4},{7,5},{8,14},{9,15},{10,... | collective-permute-start | bytes 2949128 | tf_op jit(solution)/shard_map/ppermute | solution.py:31
  7.8 21.3 %collective-permute-done.2.refs_1_ = bf16[2,1920,128]{2,1,0:T(8,128)(2,1)S(1)} collective-permute-done((bf16[2,1920,128]{2,1,0:T(8,128)(2,1)}, bf16[2,1920,128]{2,1,0:T(8,128)(2,1)S(1)}, u32[]{:S(2)}, u32[]{:S(2)}) %collective-permute-start.2) | collective-permute-done | bytes 983072 | tf_op jit(solution)/shard_map/ppermute | solution.py:31
  29.1 3.3 %collective-permute-done.refs_2_ = bf16[2,1920,128]{2,1,0:T(8,128)(2,1)S(1)} collective-permute-done((bf16[2,1920,128]{2,1,0:T(8,128)(2,1)}, bf16[2,1920,128]{2,1,0:T(8,128)(2,1)S(1)}, u32[]{:S(2)}, u32[]{:S(2)}) %collective-permute-start) | collective-permute-done | bytes 983072 | tf_op jit(solution)/shard_map/ppermute | solution.py:27
  32.6 3.3 %collective-permute-start.6 = (bf16[1920,128]{1,0:T(8,128)(2,1)S(1)}, bf16[1920,128]{1,0:T(8,128)(2,1)S(1)}, u32[]{:S(2)}, u32[]{:S(2)}) collective-permute-start(bf16[1920,128]{1,0:T(8,128)(2,1)S(1)} %slice_bitcast_fusion), channel_id=1, source_target_pairs={{0,6},{1,7},{2,0},{3,1},{4,2},{5,3},{6,4},{7,5},{8,14},{9,15},{10,... | collective-permute-start | bytes 1474568 | tf_op jit(solution)/shard_map/ppermute | solution.py:31
  35.9 2.2 %copy-done = bf16[4096,512]{1,0:T(8,128)(2,1)S(1)} copy-done((bf16[4096,512]{1,0:T(8,128)(2,1)S(1)}, bf16[4096,512]{1,0:T(8,128)(2,1)}, u32[]{:S(2)}) %copy-start) | copy-done | bytes 4194328
  38.1 2.2 %copy-done.2 = bf16[512,4096]{1,0:T(8,128)(2,1)S(1)} copy-done((bf16[512,4096]{1,0:T(8,128)(2,1)S(1)}, bf16[512,4096]{1,0:T(8,128)(2,1)}, u32[]{:S(2)}) %copy-start.2) | copy-done | bytes 4194328
  41.5 6.5 %near.1 = (f32[2,256,512]{2,1,0:T(8,128)S(1)}, bf16[1536,512]{1,0:T(8,128)(2,1)S(1)}, bf16[1536,512]{1,0:T(8,128)(2,1)S(1)}) custom-call(bf16[2,1920,128]{2,1,0:T(8,128)(2,1)S(1)} %copy-done.6, bf16[2,1920,128]{2,1,0:T(8,128)(2,1)S(1)} %collective-permute-done.2.refs_1_, bf16[2,1920,128]{2,1,0:T(8,128)(2,1)S(1)} %collective-permute-done.refs_2_, ...), custom_call_target="tpu_custom_call" | custom-call | flops 2147483648 | bytes 8388608 | tf_op jit(solution)/shard_map/near/pallas_call | solution.py:318
  48.7 1.4 %collective-permute-done.7.refs_2_.refs_3_ = bf16[1920,128]{1,0:T(8,128)(2,1)S(1)} collective-permute-done((bf16[1920,128]{1,0:T(8,128)(2,1)S(1)}, bf16[1920,128]{1,0:T(8,128)(2,1)S(1)}, u32[]{:S(2)}, u32[]{:S(2)}) %collective-permute-start.7) | collective-permute-done | bytes 491552 | tf_op jit(solution)/shard_map/ppermute | solution.py:35
  51.6 4.9 %collective-permute-start.9 = (bf16[2,64,512]{2,1,0:T(8,128)(2,1)S(1)}, bf16[2,64,512]{2,1,0:T(8,128)(2,1)S(1)}, u32[]{:S(2)}, u32[]{:S(2)}) collective-permute-start(bf16[2,64,512]{2,1,0:T(8,128)(2,1)S(1)} %get-tuple-element.24), channel_id=1, source_target_pairs={{8,0},{16,8},{24,16},{32,24},{40,32},{48,40},{56,48},{64,56},{72,6... | collective-permute-start | bytes 393224 | tf_op jit(solution)/shard_map/ppermute | solution.py:40
  56.5 6.2 %attend.1 = (bf16[256,512]{1,0:T(8,128)(2,1)S(1)}, bf16[256,512]{1,0:T(8,128)(2,1)S(1)}, f32[192,512]{1,0:T(8,128)S(1)}, bf16[4,2,128,896]{3,2,1,0:T(8,128)(2,1)S(1)}, bf16[4,2,128,896]{3,2,1,0:T(8,128)(2,1)S(1)}) custom-call(s32[2,4]{1,0:T(2,128)S(1)} %bitcast.62, bf16[1920,128]{1,0:T(8,128)(2,1)S(1)} %get-tuple-element.51.refs_0_.refs_1_, ...), custom_call_target="tpu_custom_call" | custom-call | flops 3758096384 | bytes 8388608 | tf_op jit(solution)/shard_map/attend/pallas_call | solution.py:344
  62.7 2.0 %last.1 = (bf16[256,512]{1,0:T(8,128)(2,1)S(1)}, bf16[4,2,128,896]{3,2,1,0:T(8,128)(2,1)S(1)}, bf16[4,2,128,896]{3,2,1,0:T(8,128)(2,1)S(1)}) custom-call(s32[2,4]{1,0:T(2,128)S(1)} %bitcast.63, bf16[256,512]{1,0:T(8,128)(2,1)S(1)} %get-tuple-element.22.refs_9_.refs_1_, ...), custom_call_target="tpu_custom_call", output_to_operand_aliasing={{1}: (9, {}), {2}: (10, {})} | custom-call | flops 939524096 | bytes 4194304 | tf_op jit(solution)/shard_map/last/pallas_call | solution.py:364
  64.8 1.4 %cross.1 = (bf16[4,256,512]{2,1,0:T(8,128)(2,1)S(1)}, bf16[4,256,512]{2,1,0:T(8,128)(2,1)S(1)}) custom-call(bf16[256,512]{1,0:T(8,128)(2,1)S(1)} %get-tuple-element.32.gq_ref, bf16[4096,512]{1,0:T(8,128)(2,1)S(1)} %copy-done.1), custom_call_target="tpu_custom_call" | custom-call | flops 1073741824 | bytes 8388608 | tf_op jit(solution)/shard_map/cross/pallas_call | solution.py:391
  66.7 1.8 %collective-permute-done.16 = bf16[4,2,128,896]{3,2,1,0:T(8,128)(2,1)S(1)} collective-permute-done((bf16[4,2,128,896]{3,2,1,0:T(8,128)(2,1)S(1)}, bf16[4,2,128,896]{3,2,1,0:T(8,128)(2,1)S(1)}, u32[]{:S(2)}, u32[]{:S(2)}) %collective-permute-start.16) | collective-permute-done | bytes 1835040 | tf_op jit(solution)/shard_map/ppermute | solution.py:35
  68.9 3.2 %collective-permute-start.19 = (bf16[1,128,896]{2,1,0:T(8,128)(2,1)S(1)}, bf16[1,128,896]{2,1,0:T(8,128)(2,1)S(1)}, u32[]{:S(2)}, u32[]{:S(2)}) collective-permute-start(bf16[1,128,896]{2,1,0:T(8,128)(2,1)S(1)} %get-tuple-element.41), channel_id=1, source_target_pairs={{0,6},{1,7},{2,0},{3,1},{4,2},{5,3},{6,4},{7,5},{8,14},{9,15},{10,... | collective-permute-start | bytes 688136 | tf_op jit(solution)/shard_map/ppermute | solution.py:31
  72.3 3.2 %collective-permute-start.13 = (bf16[128,512]{1,0:T(8,128)(2,1)S(1)}, bf16[128,512]{1,0:T(8,128)(2,1)S(1)}, u32[]{:S(2)}, u32[]{:S(2)}) collective-permute-start(bf16[128,512]{1,0:T(8,128)(2,1)S(1)} %get-tuple-element.47), channel_id=1, source_target_pairs={{0,6},{1,7},{2,0},{3,1},{4,2},{5,3},{6,4},{7,5},{8,14},{9,15},{10,... | collective-permute-start | bytes 393224 | tf_op jit(solution)/shard_map/ppermute | solution.py:31
  75.6 3.0 %collective-permute-done.17 = bf16[1,128,896]{2,1,0:T(8,128)(2,1)S(1)} collective-permute-done((bf16[1,128,896]{2,1,0:T(8,128)(2,1)S(1)}, bf16[1,128,896]{2,1,0:T(8,128)(2,1)S(1)}, u32[]{:S(2)}, u32[]{:S(2)}) %collective-permute-start.17) | collective-permute-done | bytes 229408 | tf_op jit(solution)/shard_map/ppermute | solution.py:27
  79.5 2.8 %collective-permute-start.20 = (bf16[2,128,896]{2,1,0:T(8,128)(2,1)S(1)}, bf16[2,128,896]{2,1,0:T(8,128)(2,1)S(1)}, u32[]{:S(2)}, u32[]{:S(2)}) collective-permute-start(bf16[2,128,896]{2,1,0:T(8,128)(2,1)S(1)} %pad_maximum_fusion.2), channel_id=1, source_target_pairs={{0,6},{1,7},{2,0},{3,1},{4,2},{5,3},{6,4},{7,5},{8,14},{9,15},{10,... | collective-permute-start | bytes 1376264 | tf_op jit(solution)/shard_map/ppermute | solution.py:31
  82.5 3.3 %collective-permute-start.14 = (bf16[256,512]{1,0:T(8,128)(2,1)S(1)}, bf16[256,512]{1,0:T(8,128)(2,1)}, u32[]{:S(2)}, u32[]{:S(2)}) collective-permute-start(bf16[256,512]{1,0:T(8,128)(2,1)S(1)} %pad_maximum_fusion.4), channel_id=1, source_target_pairs={{0,6},{1,7},{2,0},{3,1},{4,2},{5,3},{6,4},{7,5},{8,14},{9,15},{10,... | collective-permute-start | bytes 786440 | tf_op jit(solution)/shard_map/ppermute | solution.py:31
  85.8 7.8 %collective-permute-done.18 = bf16[2,128,896]{2,1,0:T(8,128)(2,1)S(1)} collective-permute-done((bf16[2,128,896]{2,1,0:T(8,128)(2,1)S(1)}, bf16[2,128,896]{2,1,0:T(8,128)(2,1)S(1)}, u32[]{:S(2)}, u32[]{:S(2)}) %collective-permute-start.18) | collective-permute-done | bytes 458784 | tf_op jit(solution)/shard_map/ppermute | solution.py:27
  94.7 5.9 %all-to-all-start = ((bf16[16,2,8,1024]{3,2,1,0:T(8,128)(2,1)}), bf16[16,2,8,1024]{3,2,1,0:T(8,128)(2,1)S(1)}, u32[]{:S(2)}, u32[]{:S(2)}) async-start(bf16[16,2,8,1024]{3,2,1,0:T(8,128)(2,1)} %pad_maximum_fusion), calls=%async_computation | async-start | bytes 1048576 | tf_op jit(solution)/shard_map/all_to_all | solution.py:388
  101.8 3.4 %collective-permute-start.15 = (bf16[63,512]{1,0:T(8,128)(2,1)S(1)}, bf16[63,512]{1,0:T(8,128)(2,1)S(1)}, u32[]{:S(2)}, u32[]{:S(2)}) collective-permute-start(bf16[63,512]{1,0:T(8,128)(2,1)S(1)} %slice.263), channel_id=1, source_target_pairs={{0,8},{8,16},{16,24},{24,32},{32,40},{40,48},{48,56},{56,64},{64,7... | collective-permute-start | bytes 193544 | tf_op jit(solution)/shard_map/ppermute | solution.py:40
  105.2 4.9 %collective-permute-done.15 = bf16[63,512]{1,0:T(8,128)(2,1)S(1)} collective-permute-done((bf16[63,512]{1,0:T(8,128)(2,1)S(1)}, bf16[63,512]{1,0:T(8,128)(2,1)S(1)}, u32[]{:S(2)}, u32[]{:S(2)}) %collective-permute-start.15) | collective-permute-done | bytes 64544 | tf_op jit(solution)/shard_map/ppermute | solution.py:40
  111.6 2.7 %scatter.1 = f32[96,8,896]{2,1,0:T(8,128)} custom-call(s32[32]{0:T(128)S(1)} %fusion.16.label_ref, bf16[32,8,1024]{2,1,0:T(8,128)(2,1)S(1)} %bitcast.60), custom_call_target="tpu_custom_call" | custom-call | flops 274877906944 | bytes 4294967296 | tf_op jit(solution)/shard_map/scatter/pallas_call | solution.py:409
  (69 shorter events, 9.8 us)
Async XLA Ops:
  3.7 32.2 %copy-start.4 = (bf16[896,512]{1,0:T(8,128)(2,1)S(1)}, bf16[896,512]{1,0:T(8,128)(2,1)}, u32[]{:S(2)}) copy-start(bf16[896,512]{1,0:T(8,128)(2,1)} %refs_6_.3) | copy-start | bytes 2752516
  3.7 32.2 %copy-start.5 = (bf16[896,512]{1,0:T(8,128)(2,1)S(1)}, bf16[896,512]{1,0:T(8,128)(2,1)}, u32[]{:S(2)}) copy-start(bf16[896,512]{1,0:T(8,128)(2,1)} %refs_7_.5) | copy-start | bytes 2752516
  3.7 25.4 %collective-permute-start.2 = (bf16[2,1920,128]{2,1,0:T(8,128)(2,1)}, bf16[2,1920,128]{2,1,0:T(8,128)(2,1)S(1)}, u32[]{:S(2)}, u32[]{:S(2)}) collective-permute-start(bf16[2,1920,128]{2,1,0:T(8,128)(2,1)} %get-tuple-element.20.refs_0_), channel_id=1, source_target_pairs={{0,6},{1,7},{2,0},{3,1},{4,2},{5,3},{6,4},{7,5},{8,14},{9,15},{10,... | collective-permute-start | bytes 2949128 | tf_op jit(solution)/shard_map/ppermute | solution.py:31
  7.8 24.6 %collective-permute-start = (bf16[2,1920,128]{2,1,0:T(8,128)(2,1)}, bf16[2,1920,128]{2,1,0:T(8,128)(2,1)S(1)}, u32[]{:S(2)}, u32[]{:S(2)}) collective-permute-start(bf16[2,1920,128]{2,1,0:T(8,128)(2,1)} %get-tuple-element.20.refs_0_), channel_id=1, source_target_pairs={{0,2},{1,3},{2,4},{3,5},{4,6},{5,7},{6,0},{7,1},{8,10},{9,11},{10,... | collective-permute-start | bytes 2949128 | tf_op jit(solution)/shard_map/ppermute | solution.py:27
  7.8 28.1 %collective-permute-start.3 = (bf16[2,1920,128]{2,1,0:T(8,128)(2,1)}, bf16[2,1920,128]{2,1,0:T(8,128)(2,1)S(1)}, u32[]{:S(2)}, u32[]{:S(2)}) collective-permute-start(bf16[2,1920,128]{2,1,0:T(8,128)(2,1)} %get-tuple-element.20.refs_0_), channel_id=1, source_target_pairs={{0,1},{1,0},{2,3},{3,2},{4,5},{5,4},{6,7},{7,6},{8,9},{9,8},{10,11... | collective-permute-start | bytes 2949128 | tf_op jit(solution)/shard_map/ppermute | solution.py:35
  29.1 6.8 %collective-permute-start.4 = (bf16[2,1920,128]{2,1,0:T(8,128)(2,1)S(1)}, bf16[2,1920,128]{2,1,0:T(8,128)(2,1)S(1)}, u32[]{:S(2)}, u32[]{:S(2)}) collective-permute-start(bf16[2,1920,128]{2,1,0:T(8,128)(2,1)S(1)} %collective-permute-done.2.refs_1_), channel_id=1, source_target_pairs={{0,1},{1,0},{2,3},{3,2},{4,5},{5,4},{6,7},{7,6},{8,9},{9,8},{10,11... | collective-permute-start | bytes 2949128 | tf_op jit(solution)/shard_map/ppermute | solution.py:35
  32.4 3.5 %collective-permute-start.5 = (bf16[2,1920,128]{2,1,0:T(8,128)(2,1)S(1)}, bf16[2,1920,128]{2,1,0:T(8,128)(2,1)S(1)}, u32[]{:S(2)}, u32[]{:S(2)}) collective-permute-start(bf16[2,1920,128]{2,1,0:T(8,128)(2,1)S(1)} %collective-permute-done.refs_2_), channel_id=1, source_target_pairs={{0,1},{1,0},{2,3},{3,2},{4,5},{5,4},{6,7},{7,6},{8,9},{9,8},{10,11... | collective-permute-start | bytes 2949128 | tf_op jit(solution)/shard_map/ppermute | solution.py:35
  32.5 15.6 %collective-permute-start.1 = (bf16[1920,128]{1,0:T(8,128)(2,1)S(1)}, bf16[1920,128]{1,0:T(8,128)(2,1)S(1)}, u32[]{:S(2)}, u32[]{:S(2)}) collective-permute-start(bf16[1920,128]{1,0:T(8,128)(2,1)S(1)} %slice_bitcast_fusion.1), channel_id=1, source_target_pairs={{0,2},{1,3},{2,4},{3,5},{4,6},{5,7},{6,0},{7,1},{8,10},{9,11},{10,... | collective-permute-start | bytes 1474568 | tf_op jit(solution)/shard_map/ppermute | solution.py:27
  32.6 15.5 %collective-permute-start.6 = (bf16[1920,128]{1,0:T(8,128)(2,1)S(1)}, bf16[1920,128]{1,0:T(8,128)(2,1)S(1)}, u32[]{:S(2)}, u32[]{:S(2)}) collective-permute-start(bf16[1920,128]{1,0:T(8,128)(2,1)S(1)} %slice_bitcast_fusion), channel_id=1, source_target_pairs={{0,6},{1,7},{2,0},{3,1},{4,2},{5,3},{6,4},{7,5},{8,14},{9,15},{10,... | collective-permute-start | bytes 1474568 | tf_op jit(solution)/shard_map/ppermute | solution.py:31
  48.1 1.9 %collective-permute-start.7 = (bf16[1920,128]{1,0:T(8,128)(2,1)S(1)}, bf16[1920,128]{1,0:T(8,128)(2,1)S(1)}, u32[]{:S(2)}, u32[]{:S(2)}) collective-permute-start(bf16[1920,128]{1,0:T(8,128)(2,1)S(1)} %get-tuple-element.51.refs_0_.refs_1_), channel_id=1, source_target_pairs={{0,1},{1,0},{2,3},{3,2},{4,5},{5,4},{6,7},{7,6},{8,9},{9,8},{10,11... | collective-permute-start | bytes 1474568 | tf_op jit(solution)/shard_map/ppermute | solution.py:35
  48.2 2.5 %collective-permute-start.8 = (bf16[1920,128]{1,0:T(8,128)(2,1)S(1)}, bf16[1920,128]{1,0:T(8,128)(2,1)S(1)}, u32[]{:S(2)}, u32[]{:S(2)}) collective-permute-start(bf16[1920,128]{1,0:T(8,128)(2,1)S(1)} %get-tuple-element.50.refs_1_.refs_2_), channel_id=1, source_target_pairs={{0,1},{1,0},{2,3},{3,2},{4,5},{5,4},{6,7},{7,6},{8,9},{9,8},{10,11... | collective-permute-start | bytes 1474568 | tf_op jit(solution)/shard_map/ppermute | solution.py:35
  51.6 11.1 %collective-permute-start.9 = (bf16[2,64,512]{2,1,0:T(8,128)(2,1)S(1)}, bf16[2,64,512]{2,1,0:T(8,128)(2,1)S(1)}, u32[]{:S(2)}, u32[]{:S(2)}) collective-permute-start(bf16[2,64,512]{2,1,0:T(8,128)(2,1)S(1)} %get-tuple-element.24), channel_id=1, source_target_pairs={{8,0},{16,8},{24,16},{32,24},{40,32},{48,40},{56,48},{64,56},{72,6... | collective-permute-start | bytes 393224 | tf_op jit(solution)/shard_map/ppermute | solution.py:40
  64.7 3.9 %collective-permute-start.16 = (bf16[4,2,128,896]{3,2,1,0:T(8,128)(2,1)S(1)}, bf16[4,2,128,896]{3,2,1,0:T(8,128)(2,1)S(1)}, u32[]{:S(2)}, u32[]{:S(2)}) collective-permute-start(bf16[4,2,128,896]{3,2,1,0:T(8,128)(2,1)S(1)} %get-tuple-element.36), channel_id=1, source_target_pairs={{0,1},{1,0},{2,3},{3,2},{4,5},{5,4},{6,7},{7,6},{8,9},{9,8},{10,11... | collective-permute-start | bytes 5505032 | tf_op jit(solution)/shard_map/ppermute | solution.py:35
  66.2 5.9 %collective-permute-start.10 = (bf16[4,256,512]{2,1,0:T(8,128)(2,1)S(1)}, bf16[4,256,512]{2,1,0:T(8,128)(2,1)S(1)}, u32[]{:S(2)}, u32[]{:S(2)}) collective-permute-start(bf16[4,256,512]{2,1,0:T(8,128)(2,1)S(1)} %get-tuple-element.34), channel_id=1, source_target_pairs={{0,1},{1,0},{2,3},{3,2},{4,5},{5,4},{6,7},{7,6},{8,9},{9,8},{10,11... | collective-permute-start | bytes 3145736 | tf_op jit(solution)/shard_map/ppermute | solution.py:35
  68.8 9.7 %collective-permute-start.17 = (bf16[1,128,896]{2,1,0:T(8,128)(2,1)S(1)}, bf16[1,128,896]{2,1,0:T(8,128)(2,1)S(1)}, u32[]{:S(2)}, u32[]{:S(2)}) collective-permute-start(bf16[1,128,896]{2,1,0:T(8,128)(2,1)S(1)} %get-tuple-element.40), channel_id=1, source_target_pairs={{0,2},{1,3},{2,4},{3,5},{4,6},{5,7},{6,0},{7,1},{8,10},{9,11},{10,... | collective-permute-start | bytes 688136 | tf_op jit(solution)/shard_map/ppermute | solution.py:27
  68.9 9.6 %collective-permute-start.19 = (bf16[1,128,896]{2,1,0:T(8,128)(2,1)S(1)}, bf16[1,128,896]{2,1,0:T(8,128)(2,1)S(1)}, u32[]{:S(2)}, u32[]{:S(2)}) collective-permute-start(bf16[1,128,896]{2,1,0:T(8,128)(2,1)S(1)} %get-tuple-element.41), channel_id=1, source_target_pairs={{0,6},{1,7},{2,0},{3,1},{4,2},{5,3},{6,4},{7,5},{8,14},{9,15},{10,... | collective-permute-start | bytes 688136 | tf_op jit(solution)/shard_map/ppermute | solution.py:31
  72.3 10.0 %collective-permute-start.11 = (bf16[128,512]{1,0:T(8,128)(2,1)S(1)}, bf16[128,512]{1,0:T(8,128)(2,1)S(1)}, u32[]{:S(2)}, u32[]{:S(2)}) collective-permute-start(bf16[128,512]{1,0:T(8,128)(2,1)S(1)} %get-tuple-element.46), channel_id=1, source_target_pairs={{0,2},{1,3},{2,4},{3,5},{4,6},{5,7},{6,0},{7,1},{8,10},{9,11},{10,... | collective-permute-start | bytes 393224 | tf_op jit(solution)/shard_map/ppermute | solution.py:27
  72.3 9.9 %collective-permute-start.13 = (bf16[128,512]{1,0:T(8,128)(2,1)S(1)}, bf16[128,512]{1,0:T(8,128)(2,1)S(1)}, u32[]{:S(2)}, u32[]{:S(2)}) collective-permute-start(bf16[128,512]{1,0:T(8,128)(2,1)S(1)} %get-tuple-element.47), channel_id=1, source_target_pairs={{0,6},{1,7},{2,0},{3,1},{4,2},{5,3},{6,4},{7,5},{8,14},{9,15},{10,... | collective-permute-start | bytes 393224 | tf_op jit(solution)/shard_map/ppermute | solution.py:31
  78.8 14.8 %collective-permute-start.18 = (bf16[2,128,896]{2,1,0:T(8,128)(2,1)S(1)}, bf16[2,128,896]{2,1,0:T(8,128)(2,1)S(1)}, u32[]{:S(2)}, u32[]{:S(2)}) collective-permute-start(bf16[2,128,896]{2,1,0:T(8,128)(2,1)S(1)} %pad_maximum_fusion.1), channel_id=1, source_target_pairs={{0,2},{1,3},{2,4},{3,5},{4,6},{5,7},{6,0},{7,1},{8,10},{9,11},{10,... | collective-permute-start | bytes 1376264 | tf_op jit(solution)/shard_map/ppermute | solution.py:27
  79.5 14.1 %collective-permute-start.20 = (bf16[2,128,896]{2,1,0:T(8,128)(2,1)S(1)}, bf16[2,128,896]{2,1,0:T(8,128)(2,1)S(1)}, u32[]{:S(2)}, u32[]{:S(2)}) collective-permute-start(bf16[2,128,896]{2,1,0:T(8,128)(2,1)S(1)} %pad_maximum_fusion.2), channel_id=1, source_target_pairs={{0,6},{1,7},{2,0},{3,1},{4,2},{5,3},{6,4},{7,5},{8,14},{9,15},{10,... | collective-permute-start | bytes 1376264 | tf_op jit(solution)/shard_map/ppermute | solution.py:31
  82.4 18.2 %collective-permute-start.12 = (bf16[256,512]{1,0:T(8,128)(2,1)S(1)}, bf16[256,512]{1,0:T(8,128)(2,1)}, u32[]{:S(2)}, u32[]{:S(2)}) collective-permute-start(bf16[256,512]{1,0:T(8,128)(2,1)S(1)} %pad_maximum_fusion.3), channel_id=1, source_target_pairs={{0,2},{1,3},{2,4},{3,5},{4,6},{5,7},{6,0},{7,1},{8,10},{9,11},{10,... | collective-permute-start | bytes 786440 | tf_op jit(solution)/shard_map/ppermute | solution.py:27
  82.5 18.1 %collective-permute-start.14 = (bf16[256,512]{1,0:T(8,128)(2,1)S(1)}, bf16[256,512]{1,0:T(8,128)(2,1)}, u32[]{:S(2)}, u32[]{:S(2)}) collective-permute-start(bf16[256,512]{1,0:T(8,128)(2,1)S(1)} %pad_maximum_fusion.4), channel_id=1, source_target_pairs={{0,6},{1,7},{2,0},{3,1},{4,2},{5,3},{6,4},{7,5},{8,14},{9,15},{10,... | collective-permute-start | bytes 786440 | tf_op jit(solution)/shard_map/ppermute | solution.py:31
  94.7 16.3 %all-to-all-start = ((bf16[16,2,8,1024]{3,2,1,0:T(8,128)(2,1)}), bf16[16,2,8,1024]{3,2,1,0:T(8,128)(2,1)S(1)}, u32[]{:S(2)}, u32[]{:S(2)}) async-start(bf16[16,2,8,1024]{3,2,1,0:T(8,128)(2,1)} %pad_maximum_fusion), calls=%async_computation | async-start | bytes 1048576 | tf_op jit(solution)/shard_map/all_to_all | solution.py:388
  101.8 8.3 %collective-permute-start.15 = (bf16[63,512]{1,0:T(8,128)(2,1)S(1)}, bf16[63,512]{1,0:T(8,128)(2,1)S(1)}, u32[]{:S(2)}, u32[]{:S(2)}) collective-permute-start(bf16[63,512]{1,0:T(8,128)(2,1)S(1)} %slice.263), channel_id=1, source_target_pairs={{0,8},{8,16},{16,24},{24,32},{32,40},{40,48},{48,56},{56,64},{64,7... | collective-permute-start | bytes 193544 | tf_op jit(solution)/shard_map/ppermute | solution.py:40
  (8 other events, 49.8 us)

commit v4 on v3

--- a/solution.py
+++ b/solution.py
@@ -21,6 +21,7 @@
 VMEM = pl.BlockSpec(memory_space=pltpu.VMEM)
 SMEM = pl.BlockSpec(memory_space=pltpu.SMEM)
 ANY = pl.BlockSpec(memory_space=pl.ANY)
+HBM = pl.BlockSpec(memory_space=pltpu.HBM)
 
 
 def up(x):
@@ -64,7 +65,7 @@
 
 
 def load_kernel(
-    shard_ref, row_ref, states_ref, cotangent_ref, database_ref, out_ref, label_ref, sems
+    shard_ref, row_ref, states_ref, cotangent_ref, database_ref, a_ref, b_ref, label_ref, sems
 ):
     rows, width = states_ref.shape
     copies = []
@@ -75,7 +76,7 @@
             copies.append(
                 pltpu.make_async_copy(
                     source.at[:, pl.ds(j * HDIM, HDIM)],
-                    out_ref.at[item, pl.ds(start + j * size, size)],
+                    (a_ref, b_ref)[item].at[pl.ds(start + j * size, size)],
                     sems.at[at + j],
                 )
             )
@@ -94,9 +95,21 @@
         each.wait()
 
 
+def hold_kernel(label_ref, a_ref, b_ref, a_out, b_out, done_ref, sems):
+    copies = [
+        pltpu.make_async_copy(src, dst, sems.at[at])
+        for at, (src, dst) in enumerate(((a_ref, a_out), (b_ref, b_out)))
+    ]
+    for copy in copies:
+        copy.start()
+    for copy in copies:
+        copy.wait()
+    done_ref[...] = label_ref[...]
+
+
 def near_kernel(*refs):
-    blocks, weights, (wk_ref, wv_ref) = refs[:6], refs[6:8], refs[8:10]
-    (sum_ref, k_ref, v_ref), (full, mem_s) = refs[10:13], refs[13:]
+    blocks, weights, (wk_ref, wv_ref) = refs[:12], refs[12:14], refs[14:16]
+    (sum_ref, k_ref, v_ref), (full, mem_s) = refs[16:19], refs[19:]
     me = lax.axis_index("db")
     rows, width = sum_ref.shape[1:]
     base = rows * width // HDIM
@@ -104,14 +117,14 @@
         far = pl.multiple_of(source_of(me, core, 2) * width, width)
         full[:, :, pl.ds(far, width)] = jnp.zeros((2, rows, width), BF16)
         for at, place in enumerate((0, 1, 3)):
-            block = blocks[core * 3 + at]
             spot = pl.multiple_of(source_of(me, core, place) * width, width)
             for item in range(2):
+                block = blocks[core * 6 + at * 2 + item]
                 for j in range(width // HDIM):
-                    full[item, :, pl.ds(spot + j * HDIM, HDIM)] = block[item, pl.ds(j * rows, rows)]
+                    full[item, :, pl.ds(spot + j * HDIM, HDIM)] = block[pl.ds(j * rows, rows)]
                 slot = ((core * 3 + at) * 2 + item) * R
                 for j in range(DE // HDIM):
-                    part = block[item, pl.ds(base + j * R, R)]
+                    part = block[pl.ds(base + j * R, R)]
                     mem_s[pl.ds(slot, R), pl.ds(j * HDIM, HDIM)] = part
     sum_ref[0] = jnp.dot(full[0], weights[0][...], preferred_element_type=F32)
     sum_ref[1] = lax.dot_general(full[1], weights[1][...], NT, preferred_element_type=F32)
@@ -304,27 +317,41 @@
     peers = lax.axis_size("ctx")
 
     given_rows = rows * width // HDIM + R * DE // HDIM
-    given, label = pl.pallas_call(
+    *given, label = pl.pallas_call(
         load_kernel,
         name="load",
-        out_shape=(shape((2, given_rows, HDIM)), shape((CAP, 8, 128), F32)),
+        out_shape=(shape((given_rows, HDIM)),) * 2 + (shape((CAP, 8, 128), F32),),
         in_specs=[SMEM, SMEM, ANY, ANY, ANY],
-        out_specs=(VMEM, VMEM),
+        out_specs=(VMEM,) * 3,
         scratch_shapes=[pltpu.SemaphoreType.DMA((2 * (width + DE) // HDIM,))],
     )(shards, named_rows, states, cotangent, database)
-    nxt, prv = down(given), up(given)
-    far_a, far_b = up(prv[0]), down(nxt[1])
-    near = (given, nxt, prv, across(given), across(nxt), across(prv))
+    *held, done = pl.pallas_call(
+        hold_kernel,
+        name="hold",
+        out_shape=(shape(w_query.shape), shape(w_out.shape), shape(label.shape, F32)),
+        in_specs=[VMEM, HBM, HBM],
+        out_specs=(VMEM,) * 3,
+        scratch_shapes=[pltpu.SemaphoreType.DMA((2,))],
+        compiler_params=limit,
+    )(label, w_query, w_out)
+    prv_a, nxt_b = up(given[0]), down(given[1])
+    prv_b, nxt_a = up(given[1]), down(given[0])
+    token = done[0, :1]
+    far_a, far_b = up(after(prv_a, token)), down(after(nxt_b, token))
+    near = (*given, nxt_a, nxt_b, prv_a, prv_b)
+    near = near + tuple(across(x) for x in given)
+    near = near + (across(after(nxt_a, token)), across(after(nxt_b, prv_b[:1])))
+    near = near + (across(after(prv_a, nxt_a[:1])), across(after(prv_b, token)))
     partial, *near_states = pl.pallas_call(
         near_kernel,
         name="near",
         out_shape=(shape((2, rows, width), F32),) + (shape((12 * R, width)),) * 2,
-        in_specs=[VMEM] * 10,
+        in_specs=[VMEM] * 16,
         out_specs=(VMEM,) * 3,
         scratch_shapes=[pltpu.VMEM((2, rows, 8 * width), BF16), pltpu.VMEM((12 * R, DE), BF16)],
         compiler_params=limit,
-        cost_estimate=cost(32 * rows * width * width, 2**23),
-    )(*near, w_query, w_out, w_key, w_value)
+        cost_estimate=cost(1, 1),
+    )(*near, *held, w_key, w_value)
     token = partial[0, :1, :HDIM]
     far_a, far_b = after(far_a, token), after(far_b, token)
     fars = (far_a, far_b, across(far_a), across(far_b))
@@ -337,7 +364,7 @@
         scratch_shapes=[pltpu.VMEM((rows, width), BF16)],
         compiler_params=limit,
         cost_estimate=cost(8 * rows * width * width, 2**23),
-    )(*fars, w_query, w_out, partial)
+    )(*fars, *held, partial)
     tails = along_ctx(tails, -1)
     positions, slots_of = spans * K * R, shape((4, CAP, R, DE))
     most = positions - K * R
@@ -396,7 +423,7 @@
         out_specs=(VMEM, VMEM),
         compiler_params=limit,
         cost_estimate=cost(2 * rows * width * 8 * width, 2**23),
-    )(grad_query, w_query)
+    )(grad_query, held[0])
     cross_got, half = across(cross_away), rows // 2
     far_up, far_down = far_sums(cross_own, cross_got, half)
     far_up, far_down = up(far_up.astype(BF16)), down(far_down.astype(BF16))

time: 115 us -> 113 us (0.983)
  waiting for transfers between devices: 44.1 us -> 36.7 us
  starting transfers between devices: 36.2 us -> 41.8 us
    ppermute x6 -> x7, waiting for transfers between devices: 21.3 us -> 0.41 us  [down(): return lax.ppermute(x, 'db', [(s, (s - 2) % 8) for s in range(8)])]
    ppermute x6 -> x7, waiting for transfers between devices: 14 us -> 27.6 us  [up(): return lax.ppermute(x, 'db', [(s, (s + 2) % 8) for s in range(8)])]
    ppermute x6 -> x7, starting transfers between devices: 0.94 us -> 6.34 us  [up(): return lax.ppermute(x, 'db', [(s, (s + 2) % 8) for s in range(8)])]
    ppermute x7 -> x10, starting transfers between devices: 1.21 us -> 2.3 us  [across(): return lax.ppermute(x, 'db', [(s, s ^ 1) for s in range(8)])]
    ppermute x6 -> x7, starting transfers between devices: 19.9 us -> 19 us  [down(): return lax.ppermute(x, 'db', [(s, (s - 2) % 8) for s in range(8)])]
    pallas_call x1 -> x2, Pallas kernels: 3.02 us -> 3.59 us  [the longest x1 3.01 us: per_device(): pl.pallas_call(load_kernel, name='load', out_shape=(shape((given_rows, HD...]
    ppermute x7 -> x10, waiting for transfers between devices: 3.91 us -> 3.92 us  [across(): return lax.ppermute(x, 'db', [(s, s ^ 1) for s in range(8)])]
  transfers between devices with their start and end apart: 22 -> 27, of which waited for: 8 -> 11; matrix products, arithmetic and copies ran while one was open for 4% -> 4% of each run, Pallas kernels for 12% -> 13%
where the time goes in v4:
time: 113 us
  starting transfers between devices  41.8 us (37%)
  waiting for transfers between devices  36.7 us (32%)
  Pallas kernels  23.2 us (21%)
  local copies, waits for them, and re-layouts  5.16 us (5%)
  other arithmetic  4.92 us (4%)
    ppermute x7, waiting for transfers between devices, up(): return lax.ppermute(x, 'db', [(s, (s + 2) % 8) for s in range(8)])  27.6 us
    ppermute x7, starting transfers between devices, down(): return lax.ppermute(x, 'db', [(s, (s - 2) % 8) for s in range(8)])  19 us
    ppermute x2, starting transfers between devices, along_ctx(): lax.ppermute(x, 'ctx', [(i, i + by) for i in range(peers) if 0 <= i + by...  8.27 us
    pallas_call x1, Pallas kernels, per_device(): pl.pallas_call(near_kernel, name='near', out_shape=(shape((2, rows, width...  6.53 us
    ppermute x7, starting transfers between devices, up(): return lax.ppermute(x, 'db', [(s, (s + 2) % 8) for s in range(8)])  6.34 us
    pallas_call x1, Pallas kernels, per_device(): pl.pallas_call(attend_kernel, name='attend', out_shape=(shape((K * R, wid...  6.17 us
    all_to_all x1, starting transfers between devices, per_device(): parts = lax.all_to_all(spread, 'ctx', 0, 0, tiled=True)  5.9 us
    unnamed x20, local copies, waits for them, and re-layouts  5.11 us
  transfers between devices with their start and end apart: 27, of which 11 were waited for; matrix products, arithmetic and copies ran while one was open for 4% of the time, Pallas kernels for 13%

profile of v4, /device:TPU:2, one launch (start us, length us, event | category | flops | bytes accessed | tf_op | source)
XLA Modules:
  0.0 112.8 jit_solution(13871710731513169445)
XLA Ops:
  0.6 3.0 %load.1 = (bf16[1920,128]{1,0:T(8,128)(2,1)}, bf16[1920,128]{1,0:T(8,128)(2,1)}, f32[2,8,128]{2,1,0:T(8,128)}) custom-call(s32[2,4]{1,0:T(2,128)} %bitcast.63, s32[2,4]{1,0:T(2,128)} %bitcast.66, bf16[256,512]{1,0:T(8,128)(2,1)} %states_ref.1, bf16[256,512]{1,0:T(8,128)(2,1)} %cotangent_ref.1, bf16[96,128,896]{2,1,0:T(8,128)(2,1)} %database_ref.1), custom_call_target="tpu_custom_call" | custom-call | tf_op jit(solution)/shard_map/load/pallas_call | solution.py:320
  3.6 2.0 %collective-permute-start.4 = (bf16[1920,128]{1,0:T(8,128)(2,1)}, bf16[1920,128]{1,0:T(8,128)(2,1)S(1)}, u32[]{:S(2)}, u32[]{:S(2)}) collective-permute-start(bf16[1920,128]{1,0:T(8,128)(2,1)} %get-tuple-element.27.refs_1_), channel_id=1, source_target_pairs={{0,2},{1,3},{2,4},{3,5},{4,6},{5,7},{6,0},{7,1},{8,10},{9,11},{10,... | collective-permute-start | bytes 1474568 | tf_op jit(solution)/shard_map/ppermute | solution.py:28
  5.6 2.2 %collective-permute-start.2 = (bf16[1920,128]{1,0:T(8,128)(2,1)}, bf16[1920,128]{1,0:T(8,128)(2,1)S(1)}, u32[]{:S(2)}, u32[]{:S(2)}) collective-permute-start(bf16[1920,128]{1,0:T(8,128)(2,1)} %get-tuple-element.24.refs_0_), channel_id=1, source_target_pairs={{0,6},{1,7},{2,0},{3,1},{4,2},{5,3},{6,4},{7,5},{8,14},{9,15},{10,... | collective-permute-start | bytes 1474568 | tf_op jit(solution)/shard_map/ppermute | solution.py:32
  7.8 3.2 %collective-permute-start.3 = (bf16[1920,128]{1,0:T(8,128)(2,1)}, bf16[1920,128]{1,0:T(8,128)(2,1)S(1)}, u32[]{:S(2)}, u32[]{:S(2)}) collective-permute-start(bf16[1920,128]{1,0:T(8,128)(2,1)} %get-tuple-element.27.refs_1_), channel_id=1, source_target_pairs={{0,6},{1,7},{2,0},{3,1},{4,2},{5,3},{6,4},{7,5},{8,14},{9,15},{10,... | collective-permute-start | bytes 1474568 | tf_op jit(solution)/shard_map/ppermute | solution.py:32
  11.1 2.2 %copy-done = bf16[4096,512]{1,0:T(8,128)(2,1)S(1)} copy-done((bf16[4096,512]{1,0:T(8,128)(2,1)S(1)}, bf16[4096,512]{1,0:T(8,128)(2,1)}, u32[]{:S(2)}) %copy-start) | copy-done | bytes 4194328
  13.3 2.2 %copy-done.1 = bf16[512,4096]{1,0:T(8,128)(2,1)S(1)} copy-done((bf16[512,4096]{1,0:T(8,128)(2,1)S(1)}, bf16[512,4096]{1,0:T(8,128)(2,1)}, u32[]{:S(2)}) %copy-start.1) | copy-done | bytes 4194328
  16.8 3.3 %collective-permute-done.4.refs_5_ = bf16[1920,128]{1,0:T(8,128)(2,1)S(1)} collective-permute-done((bf16[1920,128]{1,0:T(8,128)(2,1)}, bf16[1920,128]{1,0:T(8,128)(2,1)S(1)}, u32[]{:S(2)}, u32[]{:S(2)}) %collective-permute-start.4) | collective-permute-done | bytes 491552 | tf_op jit(solution)/shard_map/ppermute | solution.py:28
  20.1 9.6 %collective-permute-done.refs_4_ = bf16[1920,128]{1,0:T(8,128)(2,1)S(1)} collective-permute-done((bf16[1920,128]{1,0:T(8,128)(2,1)}, bf16[1920,128]{1,0:T(8,128)(2,1)S(1)}, u32[]{:S(2)}, u32[]{:S(2)}) %collective-permute-start) | collective-permute-done | bytes 491552 | tf_op jit(solution)/shard_map/ppermute | solution.py:28
  32.3 2.6 %collective-permute-start.11 = (bf16[1920,128]{1,0:T(8,128)(2,1)S(1)}, bf16[1920,128]{1,0:T(8,128)(2,1)S(1)}, u32[]{:S(2)}, u32[]{:S(2)}) collective-permute-start(bf16[1920,128]{1,0:T(8,128)(2,1)S(1)} %get-tuple-element.63), channel_id=1, source_target_pairs={{0,6},{1,7},{2,0},{3,1},{4,2},{5,3},{6,4},{7,5},{8,14},{9,15},{10,... | collective-permute-start | bytes 1474568 | tf_op jit(solution)/shard_map/ppermute | solution.py:32
  34.9 6.5 %near.1 = (f32[2,256,512]{2,1,0:T(8,128)S(1)}, bf16[1536,512]{1,0:T(8,128)(2,1)S(1)}, bf16[1536,512]{1,0:T(8,128)(2,1)S(1)}) custom-call(bf16[1920,128]{1,0:T(8,128)(2,1)S(1)} %copy-done.4, bf16[1920,128]{1,0:T(8,128)(2,1)S(1)} %copy-done.5, bf16[1920,128]{1,0:T(8,128)(2,1)S(1)} %collective-permute-done.2.refs_2_, ...), custom_call_target="tpu_custom_call" | custom-call | flops 1 | bytes 1 | tf_op jit(solution)/shard_map/near/pallas_call | solution.py:345
  41.5 4.1 %collective-permute-done.1 = bf16[1920,128]{1,0:T(8,128)(2,1)S(1)} collective-permute-done((bf16[1920,128]{1,0:T(8,128)(2,1)S(1)}, bf16[1920,128]{1,0:T(8,128)(2,1)S(1)}, u32[]{:S(2)}, u32[]{:S(2)}) %collective-permute-start.1) | collective-permute-done | bytes 491552 | tf_op jit(solution)/shard_map/ppermute | solution.py:28
  49.3 4.9 %collective-permute-start.14 = (bf16[2,64,512]{2,1,0:T(8,128)(2,1)S(1)}, bf16[2,64,512]{2,1,0:T(8,128)(2,1)S(1)}, u32[]{:S(2)}, u32[]{:S(2)}) collective-permute-start(bf16[2,64,512]{2,1,0:T(8,128)(2,1)S(1)} %get-tuple-element.33), channel_id=1, source_target_pairs={{8,0},{16,8},{24,16},{32,24},{40,32},{48,40},{56,48},{64,56},{72,6... | collective-permute-start | bytes 393224 | tf_op jit(solution)/shard_map/ppermute | solution.py:41
  54.2 6.2 %attend.1 = (bf16[256,512]{1,0:T(8,128)(2,1)S(1)}, bf16[256,512]{1,0:T(8,128)(2,1)S(1)}, f32[192,512]{1,0:T(8,128)S(1)}, bf16[4,2,128,896]{3,2,1,0:T(8,128)(2,1)S(1)}, bf16[4,2,128,896]{3,2,1,0:T(8,128)(2,1)S(1)}) custom-call(s32[2,4]{1,0:T(2,128)S(1)} %bitcast.64, bf16[1920,128]{1,0:T(8,128)(2,1)S(1)} %get-tuple-element.67.refs_0_.refs_1_, ...), custom_call_target="tpu_custom_call" | custom-call | flops 3758096384 | bytes 8388608 | tf_op jit(solution)/shard_map/attend/pallas_call | solution.py:371
  60.4 2.0 %last.1 = (bf16[256,512]{1,0:T(8,128)(2,1)S(1)}, bf16[4,2,128,896]{3,2,1,0:T(8,128)(2,1)S(1)}, bf16[4,2,128,896]{3,2,1,0:T(8,128)(2,1)S(1)}) custom-call(s32[2,4]{1,0:T(2,128)S(1)} %bitcast.65, bf16[256,512]{1,0:T(8,128)(2,1)S(1)} %get-tuple-element.31.refs_9_.refs_1_, ...), custom_call_target="tpu_custom_call", output_to_operand_aliasing={{1}: (9, {}), {2}: (10, {})} | custom-call | flops 939524096 | bytes 4194304 | tf_op jit(solution)/shard_map/last/pallas_call | solution.py:391
  67.7 2.6 %collective-permute-start.24 = (bf16[1,128,896]{2,1,0:T(8,128)(2,1)S(1)}, bf16[1,128,896]{2,1,0:T(8,128)(2,1)S(1)}, u32[]{:S(2)}, u32[]{:S(2)}) collective-permute-start(bf16[1,128,896]{2,1,0:T(8,128)(2,1)S(1)} %get-tuple-element.49), channel_id=1, source_target_pairs={{0,6},{1,7},{2,0},{3,1},{4,2},{5,3},{6,4},{7,5},{8,14},{9,15},{10,... | collective-permute-start | bytes 688136 | tf_op jit(solution)/shard_map/ppermute | solution.py:32
  70.5 3.2 %collective-permute-start.18 = (bf16[128,512]{1,0:T(8,128)(2,1)S(1)}, bf16[128,512]{1,0:T(8,128)(2,1)S(1)}, u32[]{:S(2)}, u32[]{:S(2)}) collective-permute-start(bf16[128,512]{1,0:T(8,128)(2,1)S(1)} %get-tuple-element.55), channel_id=1, source_target_pairs={{0,6},{1,7},{2,0},{3,1},{4,2},{5,3},{6,4},{7,5},{8,14},{9,15},{10,... | collective-permute-start | bytes 393224 | tf_op jit(solution)/shard_map/ppermute | solution.py:32
  73.8 2.8 %collective-permute-done.22 = bf16[1,128,896]{2,1,0:T(8,128)(2,1)S(1)} collective-permute-done((bf16[1,128,896]{2,1,0:T(8,128)(2,1)S(1)}, bf16[1,128,896]{2,1,0:T(8,128)(2,1)S(1)}, u32[]{:S(2)}, u32[]{:S(2)}) %collective-permute-start.22) | collective-permute-done | bytes 229408 | tf_op jit(solution)/shard_map/ppermute | solution.py:28
  78.4 2.0 %collective-permute-start.25 = (bf16[2,128,896]{2,1,0:T(8,128)(2,1)S(1)}, bf16[2,128,896]{2,1,0:T(8,128)(2,1)S(1)}, u32[]{:S(2)}, u32[]{:S(2)}) collective-permute-start(bf16[2,128,896]{2,1,0:T(8,128)(2,1)S(1)} %pad_maximum_fusion.2), channel_id=1, source_target_pairs={{0,6},{1,7},{2,0},{3,1},{4,2},{5,3},{6,4},{7,5},{8,14},{9,15},{10,... | collective-permute-start | bytes 1376264 | tf_op jit(solution)/shard_map/ppermute | solution.py:32
  80.8 3.1 %collective-permute-start.19 = (bf16[256,512]{1,0:T(8,128)(2,1)S(1)}, bf16[256,512]{1,0:T(8,128)(2,1)}, u32[]{:S(2)}, u32[]{:S(2)}) collective-permute-start(bf16[256,512]{1,0:T(8,128)(2,1)S(1)} %pad_maximum_fusion.4), channel_id=1, source_target_pairs={{0,6},{1,7},{2,0},{3,1},{4,2},{5,3},{6,4},{7,5},{8,14},{9,15},{10,... | collective-permute-start | bytes 786440 | tf_op jit(solution)/shard_map/ppermute | solution.py:32
  83.9 7.8 %collective-permute-done.23 = bf16[2,128,896]{2,1,0:T(8,128)(2,1)S(1)} collective-permute-done((bf16[2,128,896]{2,1,0:T(8,128)(2,1)S(1)}, bf16[2,128,896]{2,1,0:T(8,128)(2,1)S(1)}, u32[]{:S(2)}, u32[]{:S(2)}) %collective-permute-start.23) | collective-permute-done | bytes 458784 | tf_op jit(solution)/shard_map/ppermute | solution.py:28
  93.1 5.9 %all-to-all-start = ((bf16[16,2,8,1024]{3,2,1,0:T(8,128)(2,1)}), bf16[16,2,8,1024]{3,2,1,0:T(8,128)(2,1)S(1)}, u32[]{:S(2)}, u32[]{:S(2)}) async-start(bf16[16,2,8,1024]{3,2,1,0:T(8,128)(2,1)} %pad_maximum_fusion), calls=%async_computation | async-start | bytes 1048576 | tf_op jit(solution)/shard_map/all_to_all | solution.py:415
  100.2 3.4 %collective-permute-start.20 = (bf16[63,512]{1,0:T(8,128)(2,1)S(1)}, bf16[63,512]{1,0:T(8,128)(2,1)S(1)}, u32[]{:S(2)}, u32[]{:S(2)}) collective-permute-start(bf16[63,512]{1,0:T(8,128)(2,1)S(1)} %slice.268), channel_id=1, source_target_pairs={{0,8},{8,16},{16,24},{24,32},{32,40},{40,48},{48,56},{56,64},{64,7... | collective-permute-start | bytes 193544 | tf_op jit(solution)/shard_map/ppermute | solution.py:41
  103.6 4.9 %collective-permute-done.20 = bf16[63,512]{1,0:T(8,128)(2,1)S(1)} collective-permute-done((bf16[63,512]{1,0:T(8,128)(2,1)S(1)}, bf16[63,512]{1,0:T(8,128)(2,1)S(1)}, u32[]{:S(2)}, u32[]{:S(2)}) %collective-permute-start.20) | collective-permute-done | bytes 64544 | tf_op jit(solution)/shard_map/ppermute | solution.py:41
  110.0 2.7 %scatter.1 = f32[96,8,896]{2,1,0:T(8,128)} custom-call(s32[32]{0:T(128)S(1)} %fusion.16.label_ref, bf16[32,8,1024]{2,1,0:T(8,128)(2,1)S(1)} %bitcast.62), custom_call_target="tpu_custom_call" | custom-call | flops 274877906944 | bytes 4294967296 | tf_op jit(solution)/shard_map/scatter/pallas_call | solution.py:436
  (82 shorter events, 19.5 us)
Async XLA Ops:
  3.6 16.4 %collective-permute-start.4 = (bf16[1920,128]{1,0:T(8,128)(2,1)}, bf16[1920,128]{1,0:T(8,128)(2,1)S(1)}, u32[]{:S(2)}, u32[]{:S(2)}) collective-permute-start(bf16[1920,128]{1,0:T(8,128)(2,1)} %get-tuple-element.27.refs_1_), channel_id=1, source_target_pairs={{0,2},{1,3},{2,4},{3,5},{4,6},{5,7},{6,0},{7,1},{8,10},{9,11},{10,... | collective-permute-start | bytes 1474568 | tf_op jit(solution)/shard_map/ppermute | solution.py:28
  5.6 14.4 %collective-permute-start.2 = (bf16[1920,128]{1,0:T(8,128)(2,1)}, bf16[1920,128]{1,0:T(8,128)(2,1)S(1)}, u32[]{:S(2)}, u32[]{:S(2)}) collective-permute-start(bf16[1920,128]{1,0:T(8,128)(2,1)} %get-tuple-element.24.refs_0_), channel_id=1, source_target_pairs={{0,6},{1,7},{2,0},{3,1},{4,2},{5,3},{6,4},{7,5},{8,14},{9,15},{10,... | collective-permute-start | bytes 1474568 | tf_op jit(solution)/shard_map/ppermute | solution.py:32
  7.8 21.9 %collective-permute-start = (bf16[1920,128]{1,0:T(8,128)(2,1)}, bf16[1920,128]{1,0:T(8,128)(2,1)S(1)}, u32[]{:S(2)}, u32[]{:S(2)}) collective-permute-start(bf16[1920,128]{1,0:T(8,128)(2,1)} %get-tuple-element.24.refs_0_), channel_id=1, source_target_pairs={{0,2},{1,3},{2,4},{3,5},{4,6},{5,7},{6,0},{7,1},{8,10},{9,11},{10,... | collective-permute-start | bytes 1474568 | tf_op jit(solution)/shard_map/ppermute | solution.py:28
  7.8 21.9 %collective-permute-start.3 = (bf16[1920,128]{1,0:T(8,128)(2,1)}, bf16[1920,128]{1,0:T(8,128)(2,1)S(1)}, u32[]{:S(2)}, u32[]{:S(2)}) collective-permute-start(bf16[1920,128]{1,0:T(8,128)(2,1)} %get-tuple-element.27.refs_1_), channel_id=1, source_target_pairs={{0,6},{1,7},{2,0},{3,1},{4,2},{5,3},{6,4},{7,5},{8,14},{9,15},{10,... | collective-permute-start | bytes 1474568 | tf_op jit(solution)/shard_map/ppermute | solution.py:32
  11.1 19.5 %collective-permute-start.5 = (bf16[1920,128]{1,0:T(8,128)(2,1)}, bf16[1920,128]{1,0:T(8,128)(2,1)S(1)}, u32[]{:S(2)}, u32[]{:S(2)}) collective-permute-start(bf16[1920,128]{1,0:T(8,128)(2,1)} %get-tuple-element.24.refs_0_), channel_id=1, source_target_pairs={{0,1},{1,0},{2,3},{3,2},{4,5},{5,4},{6,7},{7,6},{8,9},{9,8},{10,11... | collective-permute-start | bytes 1474568 | tf_op jit(solution)/shard_map/ppermute | solution.py:36
  20.0 11.0 %collective-permute-start.6 = (bf16[1920,128]{1,0:T(8,128)(2,1)S(1)}, bf16[1920,128]{1,0:T(8,128)(2,1)S(1)}, u32[]{:S(2)}, u32[]{:S(2)}) collective-permute-start(bf16[1920,128]{1,0:T(8,128)(2,1)S(1)} %copy-done.5), channel_id=1, source_target_pairs={{0,1},{1,0},{2,3},{3,2},{4,5},{5,4},{6,7},{7,6},{8,9},{9,8},{10,11... | collective-permute-start | bytes 1474568 | tf_op jit(solution)/shard_map/ppermute | solution.py:36
  30.0 4.9 %collective-permute-start.7 = (bf16[1920,128]{1,0:T(8,128)(2,1)S(1)}, bf16[1920,128]{1,0:T(8,128)(2,1)S(1)}, u32[]{:S(2)}, u32[]{:S(2)}) collective-permute-start(bf16[1920,128]{1,0:T(8,128)(2,1)S(1)} %get-tuple-element.65), channel_id=1, source_target_pairs={{0,1},{1,0},{2,3},{3,2},{4,5},{5,4},{6,7},{7,6},{8,9},{9,8},{10,11... | collective-permute-start | bytes 1474568 | tf_op jit(solution)/shard_map/ppermute | solution.py:36
  30.5 4.4 %collective-permute-start.8 = (bf16[1920,128]{1,0:T(8,128)(2,1)S(1)}, bf16[1920,128]{1,0:T(8,128)(2,1)S(1)}, u32[]{:S(2)}, u32[]{:S(2)}) collective-permute-start(bf16[1920,128]{1,0:T(8,128)(2,1)S(1)} %get-tuple-element.62), channel_id=1, source_target_pairs={{0,1},{1,0},{2,3},{3,2},{4,5},{5,4},{6,7},{7,6},{8,9},{9,8},{10,11... | collective-permute-start | bytes 1474568 | tf_op jit(solution)/shard_map/ppermute | solution.py:36
  30.6 4.3 %collective-permute-start.9 = (bf16[1920,128]{1,0:T(8,128)(2,1)S(1)}, bf16[1920,128]{1,0:T(8,128)(2,1)S(1)}, u32[]{:S(2)}, u32[]{:S(2)}) collective-permute-start(bf16[1920,128]{1,0:T(8,128)(2,1)S(1)} %get-tuple-element.60), channel_id=1, source_target_pairs={{0,1},{1,0},{2,3},{3,2},{4,5},{5,4},{6,7},{7,6},{8,9},{9,8},{10,11... | collective-permute-start | bytes 1474568 | tf_op jit(solution)/shard_map/ppermute | solution.py:36
  31.0 14.5 %collective-permute-start.1 = (bf16[1920,128]{1,0:T(8,128)(2,1)S(1)}, bf16[1920,128]{1,0:T(8,128)(2,1)S(1)}, u32[]{:S(2)}, u32[]{:S(2)}) collective-permute-start(bf16[1920,128]{1,0:T(8,128)(2,1)S(1)} %get-tuple-element.61), channel_id=1, source_target_pairs={{0,2},{1,3},{2,4},{3,5},{4,6},{5,7},{6,0},{7,1},{8,10},{9,11},{10,... | collective-permute-start | bytes 1474568 | tf_op jit(solution)/shard_map/ppermute | solution.py:28
  32.3 13.4 %collective-permute-start.11 = (bf16[1920,128]{1,0:T(8,128)(2,1)S(1)}, bf16[1920,128]{1,0:T(8,128)(2,1)S(1)}, u32[]{:S(2)}, u32[]{:S(2)}) collective-permute-start(bf16[1920,128]{1,0:T(8,128)(2,1)S(1)} %get-tuple-element.63), channel_id=1, source_target_pairs={{0,6},{1,7},{2,0},{3,1},{4,2},{5,3},{6,4},{7,5},{8,14},{9,15},{10,... | collective-permute-start | bytes 1474568 | tf_op jit(solution)/shard_map/ppermute | solution.py:32
  49.3 11.1 %collective-permute-start.14 = (bf16[2,64,512]{2,1,0:T(8,128)(2,1)S(1)}, bf16[2,64,512]{2,1,0:T(8,128)(2,1)S(1)}, u32[]{:S(2)}, u32[]{:S(2)}) collective-permute-start(bf16[2,64,512]{2,1,0:T(8,128)(2,1)S(1)} %get-tuple-element.33), channel_id=1, source_target_pairs={{8,0},{16,8},{24,16},{32,24},{40,32},{48,40},{56,48},{64,56},{72,6... | collective-permute-start | bytes 393224 | tf_op jit(solution)/shard_map/ppermute | solution.py:41
  62.3 3.9 %collective-permute-start.21 = (bf16[4,2,128,896]{3,2,1,0:T(8,128)(2,1)S(1)}, bf16[4,2,128,896]{3,2,1,0:T(8,128)(2,1)S(1)}, u32[]{:S(2)}, u32[]{:S(2)}) collective-permute-start(bf16[4,2,128,896]{3,2,1,0:T(8,128)(2,1)S(1)} %get-tuple-element.45), channel_id=1, source_target_pairs={{0,1},{1,0},{2,3},{3,2},{4,5},{5,4},{6,7},{7,6},{8,9},{9,8},{10,11... | collective-permute-start | bytes 5505032 | tf_op jit(solution)/shard_map/ppermute | solution.py:36
  63.8 6.5 %collective-permute-start.15 = (bf16[4,256,512]{2,1,0:T(8,128)(2,1)S(1)}, bf16[4,256,512]{2,1,0:T(8,128)(2,1)S(1)}, u32[]{:S(2)}, u32[]{:S(2)}) collective-permute-start(bf16[4,256,512]{2,1,0:T(8,128)(2,1)S(1)} %get-tuple-element.43), channel_id=1, source_target_pairs={{0,1},{1,0},{2,3},{3,2},{4,5},{5,4},{6,7},{7,6},{8,9},{9,8},{10,11... | collective-permute-start | bytes 3145736 | tf_op jit(solution)/shard_map/ppermute | solution.py:36
  66.5 10.1 %collective-permute-start.22 = (bf16[1,128,896]{2,1,0:T(8,128)(2,1)S(1)}, bf16[1,128,896]{2,1,0:T(8,128)(2,1)S(1)}, u32[]{:S(2)}, u32[]{:S(2)}) collective-permute-start(bf16[1,128,896]{2,1,0:T(8,128)(2,1)S(1)} %get-tuple-element.48), channel_id=1, source_target_pairs={{0,2},{1,3},{2,4},{3,5},{4,6},{5,7},{6,0},{7,1},{8,10},{9,11},{10,... | collective-permute-start | bytes 688136 | tf_op jit(solution)/shard_map/ppermute | solution.py:28
  67.7 8.9 %collective-permute-start.24 = (bf16[1,128,896]{2,1,0:T(8,128)(2,1)S(1)}, bf16[1,128,896]{2,1,0:T(8,128)(2,1)S(1)}, u32[]{:S(2)}, u32[]{:S(2)}) collective-permute-start(bf16[1,128,896]{2,1,0:T(8,128)(2,1)S(1)} %get-tuple-element.49), channel_id=1, source_target_pairs={{0,6},{1,7},{2,0},{3,1},{4,2},{5,3},{6,4},{7,5},{8,14},{9,15},{10,... | collective-permute-start | bytes 688136 | tf_op jit(solution)/shard_map/ppermute | solution.py:32
  70.4 10.0 %collective-permute-start.16 = (bf16[128,512]{1,0:T(8,128)(2,1)S(1)}, bf16[128,512]{1,0:T(8,128)(2,1)S(1)}, u32[]{:S(2)}, u32[]{:S(2)}) collective-permute-start(bf16[128,512]{1,0:T(8,128)(2,1)S(1)} %get-tuple-element.54), channel_id=1, source_target_pairs={{0,2},{1,3},{2,4},{3,5},{4,6},{5,7},{6,0},{7,1},{8,10},{9,11},{10,... | collective-permute-start | bytes 393224 | tf_op jit(solution)/shard_map/ppermute | solution.py:28
  70.5 9.9 %collective-permute-start.18 = (bf16[128,512]{1,0:T(8,128)(2,1)S(1)}, bf16[128,512]{1,0:T(8,128)(2,1)S(1)}, u32[]{:S(2)}, u32[]{:S(2)}) collective-permute-start(bf16[128,512]{1,0:T(8,128)(2,1)S(1)} %get-tuple-element.55), channel_id=1, source_target_pairs={{0,6},{1,7},{2,0},{3,1},{4,2},{5,3},{6,4},{7,5},{8,14},{9,15},{10,... | collective-permute-start | bytes 393224 | tf_op jit(solution)/shard_map/ppermute | solution.py:32
  76.8 14.9 %collective-permute-start.23 = (bf16[2,128,896]{2,1,0:T(8,128)(2,1)S(1)}, bf16[2,128,896]{2,1,0:T(8,128)(2,1)S(1)}, u32[]{:S(2)}, u32[]{:S(2)}) collective-permute-start(bf16[2,128,896]{2,1,0:T(8,128)(2,1)S(1)} %pad_maximum_fusion.1), channel_id=1, source_target_pairs={{0,2},{1,3},{2,4},{3,5},{4,6},{5,7},{6,0},{7,1},{8,10},{9,11},{10,... | collective-permute-start | bytes 1376264 | tf_op jit(solution)/shard_map/ppermute | solution.py:28
  78.4 13.5 %collective-permute-start.25 = (bf16[2,128,896]{2,1,0:T(8,128)(2,1)S(1)}, bf16[2,128,896]{2,1,0:T(8,128)(2,1)S(1)}, u32[]{:S(2)}, u32[]{:S(2)}) collective-permute-start(bf16[2,128,896]{2,1,0:T(8,128)(2,1)S(1)} %pad_maximum_fusion.2), channel_id=1, source_target_pairs={{0,6},{1,7},{2,0},{3,1},{4,2},{5,3},{6,4},{7,5},{8,14},{9,15},{10,... | collective-permute-start | bytes 1376264 | tf_op jit(solution)/shard_map/ppermute | solution.py:32
  80.5 18.5 %collective-permute-start.17 = (bf16[256,512]{1,0:T(8,128)(2,1)S(1)}, bf16[256,512]{1,0:T(8,128)(2,1)}, u32[]{:S(2)}, u32[]{:S(2)}) collective-permute-start(bf16[256,512]{1,0:T(8,128)(2,1)S(1)} %pad_maximum_fusion.3), channel_id=1, source_target_pairs={{0,2},{1,3},{2,4},{3,5},{4,6},{5,7},{6,0},{7,1},{8,10},{9,11},{10,... | collective-permute-start | bytes 786440 | tf_op jit(solution)/shard_map/ppermute | solution.py:28
  80.8 18.2 %collective-permute-start.19 = (bf16[256,512]{1,0:T(8,128)(2,1)S(1)}, bf16[256,512]{1,0:T(8,128)(2,1)}, u32[]{:S(2)}, u32[]{:S(2)}) collective-permute-start(bf16[256,512]{1,0:T(8,128)(2,1)S(1)} %pad_maximum_fusion.4), channel_id=1, source_target_pairs={{0,6},{1,7},{2,0},{3,1},{4,2},{5,3},{6,4},{7,5},{8,14},{9,15},{10,... | collective-permute-start | bytes 786440 | tf_op jit(solution)/shard_map/ppermute | solution.py:32
  93.1 16.3 %all-to-all-start = ((bf16[16,2,8,1024]{3,2,1,0:T(8,128)(2,1)}), bf16[16,2,8,1024]{3,2,1,0:T(8,128)(2,1)S(1)}, u32[]{:S(2)}, u32[]{:S(2)}) async-start(bf16[16,2,8,1024]{3,2,1,0:T(8,128)(2,1)} %pad_maximum_fusion), calls=%async_computation | async-start | bytes 1048576 | tf_op jit(solution)/shard_map/all_to_all | solution.py:415
  100.2 8.3 %collective-permute-start.20 = (bf16[63,512]{1,0:T(8,128)(2,1)S(1)}, bf16[63,512]{1,0:T(8,128)(2,1)S(1)}, u32[]{:S(2)}, u32[]{:S(2)}) collective-permute-start(bf16[63,512]{1,0:T(8,128)(2,1)S(1)} %slice.268), channel_id=1, source_target_pairs={{0,8},{8,16},{16,24},{24,32},{32,40},{40,48},{48,56},{56,64},{64,7... | collective-permute-start | bytes 193544 | tf_op jit(solution)/shard_map/ppermute | solution.py:41
  (13 other events, 86.0 us)

commit v5 on v4

--- a/solution.py
+++ b/solution.py
@@ -277,16 +277,12 @@
     out_ref[...] = jnp.zeros_like(out_ref)
     width = out_ref.shape[2]
 
-    def item(i, carry):
+    for i in range(parts_ref.shape[0]):
         row = label_ref[i]
 
         @pl.when(row >= 0)
-        def _():
+        def _(i=i, row=row):
             out_ref[row] += parts_ref[i][:, :width].astype(F32)
-
-        return carry
-
-    lax.fori_loop(0, parts_ref.shape[0], item, 0)
 
 
 def after(x, token):

time: 113 us -> 113 us (level)
  no operation moved by 1% of the time
where the time goes in v5:
time: 113 us
  starting transfers between devices  41.7 us (37%)
  waiting for transfers between devices  36.7 us (32%)
  Pallas kernels  23 us (20%)
  local copies, waits for them, and re-layouts  5.16 us (5%)
  other arithmetic  4.92 us (4%)
    ppermute x7, waiting for transfers between devices, up(): return lax.ppermute(x, 'db', [(s, (s + 2) % 8) for s in range(8)])  27.6 us
    ppermute x7, starting transfers between devices, down(): return lax.ppermute(x, 'db', [(s, (s - 2) % 8) for s in range(8)])  19 us
    ppermute x2, starting transfers between devices, along_ctx(): lax.ppermute(x, 'ctx', [(i, i + by) for i in range(peers) if 0 <= i + by...  8.27 us
    pallas_call x1, Pallas kernels, per_device(): pl.pallas_call(near_kernel, name='near', out_shape=(shape((2, rows, width...  6.53 us
    ppermute x7, starting transfers between devices, up(): return lax.ppermute(x, 'db', [(s, (s + 2) % 8) for s in range(8)])  6.33 us
    pallas_call x1, Pallas kernels, per_device(): pl.pallas_call(attend_kernel, name='attend', out_shape=(shape((K * R, wid...  6.17 us
    all_to_all x1, starting transfers between devices, per_device(): parts = lax.all_to_all(spread, 'ctx', 0, 0, tiled=True)  5.89 us
    unnamed x20, local copies, waits for them, and re-layouts  5.11 us
  transfers between devices with their start and end apart: 27, of which 11 were waited for; matrix products, arithmetic and copies ran while one was open for 4% of the time, Pallas kernels for 13%

profile of v5, /device:TPU:2, one launch (start us, length us, event | category | flops | bytes accessed | tf_op | source)
XLA Modules:
  0.0 112.6 jit_solution(3248897871164916146)
XLA Ops:
  0.6 3.0 %load.1 = (bf16[1920,128]{1,0:T(8,128)(2,1)}, bf16[1920,128]{1,0:T(8,128)(2,1)}, f32[2,8,128]{2,1,0:T(8,128)}) custom-call(s32[2,4]{1,0:T(2,128)} %bitcast.63, s32[2,4]{1,0:T(2,128)} %bitcast.66, bf16[256,512]{1,0:T(8,128)(2,1)} %states_ref.1, bf16[256,512]{1,0:T(8,128)(2,1)} %cotangent_ref.1, bf16[96,128,896]{2,1,0:T(8,128)(2,1)} %database_ref.1), custom_call_target="tpu_custom_call" | custom-call | tf_op jit(solution)/shard_map/load/pallas_call | solution.py:316
  3.6 2.0 %collective-permute-start.4 = (bf16[1920,128]{1,0:T(8,128)(2,1)}, bf16[1920,128]{1,0:T(8,128)(2,1)S(1)}, u32[]{:S(2)}, u32[]{:S(2)}) collective-permute-start(bf16[1920,128]{1,0:T(8,128)(2,1)} %get-tuple-element.27.refs_1_), channel_id=1, source_target_pairs={{0,2},{1,3},{2,4},{3,5},{4,6},{5,7},{6,0},{7,1},{8,10},{9,11},{10,... | collective-permute-start | bytes 1474568 | tf_op jit(solution)/shard_map/ppermute | solution.py:28
  5.6 2.2 %collective-permute-start.2 = (bf16[1920,128]{1,0:T(8,128)(2,1)}, bf16[1920,128]{1,0:T(8,128)(2,1)S(1)}, u32[]{:S(2)}, u32[]{:S(2)}) collective-permute-start(bf16[1920,128]{1,0:T(8,128)(2,1)} %get-tuple-element.24.refs_0_), channel_id=1, source_target_pairs={{0,6},{1,7},{2,0},{3,1},{4,2},{5,3},{6,4},{7,5},{8,14},{9,15},{10,... | collective-permute-start | bytes 1474568 | tf_op jit(solution)/shard_map/ppermute | solution.py:32
  7.8 3.2 %collective-permute-start.3 = (bf16[1920,128]{1,0:T(8,128)(2,1)}, bf16[1920,128]{1,0:T(8,128)(2,1)S(1)}, u32[]{:S(2)}, u32[]{:S(2)}) collective-permute-start(bf16[1920,128]{1,0:T(8,128)(2,1)} %get-tuple-element.27.refs_1_), channel_id=1, source_target_pairs={{0,6},{1,7},{2,0},{3,1},{4,2},{5,3},{6,4},{7,5},{8,14},{9,15},{10,... | collective-permute-start | bytes 1474568 | tf_op jit(solution)/shard_map/ppermute | solution.py:32
  11.1 2.2 %copy-done = bf16[4096,512]{1,0:T(8,128)(2,1)S(1)} copy-done((bf16[4096,512]{1,0:T(8,128)(2,1)S(1)}, bf16[4096,512]{1,0:T(8,128)(2,1)}, u32[]{:S(2)}) %copy-start) | copy-done | bytes 4194328
  13.3 2.2 %copy-done.1 = bf16[512,4096]{1,0:T(8,128)(2,1)S(1)} copy-done((bf16[512,4096]{1,0:T(8,128)(2,1)S(1)}, bf16[512,4096]{1,0:T(8,128)(2,1)}, u32[]{:S(2)}) %copy-start.1) | copy-done | bytes 4194328
  16.8 3.3 %collective-permute-done.4.refs_5_ = bf16[1920,128]{1,0:T(8,128)(2,1)S(1)} collective-permute-done((bf16[1920,128]{1,0:T(8,128)(2,1)}, bf16[1920,128]{1,0:T(8,128)(2,1)S(1)}, u32[]{:S(2)}, u32[]{:S(2)}) %collective-permute-start.4) | collective-permute-done | bytes 491552 | tf_op jit(solution)/shard_map/ppermute | solution.py:28
  20.1 9.6 %collective-permute-done.refs_4_ = bf16[1920,128]{1,0:T(8,128)(2,1)S(1)} collective-permute-done((bf16[1920,128]{1,0:T(8,128)(2,1)}, bf16[1920,128]{1,0:T(8,128)(2,1)S(1)}, u32[]{:S(2)}, u32[]{:S(2)}) %collective-permute-start) | collective-permute-done | bytes 491552 | tf_op jit(solution)/shard_map/ppermute | solution.py:28
  32.3 2.6 %collective-permute-start.11 = (bf16[1920,128]{1,0:T(8,128)(2,1)S(1)}, bf16[1920,128]{1,0:T(8,128)(2,1)S(1)}, u32[]{:S(2)}, u32[]{:S(2)}) collective-permute-start(bf16[1920,128]{1,0:T(8,128)(2,1)S(1)} %get-tuple-element.63), channel_id=1, source_target_pairs={{0,6},{1,7},{2,0},{3,1},{4,2},{5,3},{6,4},{7,5},{8,14},{9,15},{10,... | collective-permute-start | bytes 1474568 | tf_op jit(solution)/shard_map/ppermute | solution.py:32
  34.9 6.5 %near.1 = (f32[2,256,512]{2,1,0:T(8,128)S(1)}, bf16[1536,512]{1,0:T(8,128)(2,1)S(1)}, bf16[1536,512]{1,0:T(8,128)(2,1)S(1)}) custom-call(bf16[1920,128]{1,0:T(8,128)(2,1)S(1)} %copy-done.4, bf16[1920,128]{1,0:T(8,128)(2,1)S(1)} %copy-done.5, bf16[1920,128]{1,0:T(8,128)(2,1)S(1)} %collective-permute-done.2.refs_2_, ...), custom_call_target="tpu_custom_call" | custom-call | flops 1 | bytes 1 | tf_op jit(solution)/shard_map/near/pallas_call | solution.py:341
  41.5 4.1 %collective-permute-done.1 = bf16[1920,128]{1,0:T(8,128)(2,1)S(1)} collective-permute-done((bf16[1920,128]{1,0:T(8,128)(2,1)S(1)}, bf16[1920,128]{1,0:T(8,128)(2,1)S(1)}, u32[]{:S(2)}, u32[]{:S(2)}) %collective-permute-start.1) | collective-permute-done | bytes 491552 | tf_op jit(solution)/shard_map/ppermute | solution.py:28
  49.3 4.9 %collective-permute-start.14 = (bf16[2,64,512]{2,1,0:T(8,128)(2,1)S(1)}, bf16[2,64,512]{2,1,0:T(8,128)(2,1)S(1)}, u32[]{:S(2)}, u32[]{:S(2)}) collective-permute-start(bf16[2,64,512]{2,1,0:T(8,128)(2,1)S(1)} %get-tuple-element.33), channel_id=1, source_target_pairs={{8,0},{16,8},{24,16},{32,24},{40,32},{48,40},{56,48},{64,56},{72,6... | collective-permute-start | bytes 393224 | tf_op jit(solution)/shard_map/ppermute | solution.py:41
  54.2 6.2 %attend.1 = (bf16[256,512]{1,0:T(8,128)(2,1)S(1)}, bf16[256,512]{1,0:T(8,128)(2,1)S(1)}, f32[192,512]{1,0:T(8,128)S(1)}, bf16[4,2,128,896]{3,2,1,0:T(8,128)(2,1)S(1)}, bf16[4,2,128,896]{3,2,1,0:T(8,128)(2,1)S(1)}) custom-call(s32[2,4]{1,0:T(2,128)S(1)} %bitcast.64, bf16[1920,128]{1,0:T(8,128)(2,1)S(1)} %get-tuple-element.67.refs_0_.refs_1_, ...), custom_call_target="tpu_custom_call" | custom-call | flops 3758096384 | bytes 8388608 | tf_op jit(solution)/shard_map/attend/pallas_call | solution.py:367
  60.4 2.0 %last.1 = (bf16[256,512]{1,0:T(8,128)(2,1)S(1)}, bf16[4,2,128,896]{3,2,1,0:T(8,128)(2,1)S(1)}, bf16[4,2,128,896]{3,2,1,0:T(8,128)(2,1)S(1)}) custom-call(s32[2,4]{1,0:T(2,128)S(1)} %bitcast.65, bf16[256,512]{1,0:T(8,128)(2,1)S(1)} %get-tuple-element.31.refs_9_.refs_1_, ...), custom_call_target="tpu_custom_call", output_to_operand_aliasing={{1}: (9, {}), {2}: (10, {})} | custom-call | flops 939524096 | bytes 4194304 | tf_op jit(solution)/shard_map/last/pallas_call | solution.py:387
  67.7 2.6 %collective-permute-start.24 = (bf16[1,128,896]{2,1,0:T(8,128)(2,1)S(1)}, bf16[1,128,896]{2,1,0:T(8,128)(2,1)S(1)}, u32[]{:S(2)}, u32[]{:S(2)}) collective-permute-start(bf16[1,128,896]{2,1,0:T(8,128)(2,1)S(1)} %get-tuple-element.49), channel_id=1, source_target_pairs={{0,6},{1,7},{2,0},{3,1},{4,2},{5,3},{6,4},{7,5},{8,14},{9,15},{10,... | collective-permute-start | bytes 688136 | tf_op jit(solution)/shard_map/ppermute | solution.py:32
  70.5 3.2 %collective-permute-start.18 = (bf16[128,512]{1,0:T(8,128)(2,1)S(1)}, bf16[128,512]{1,0:T(8,128)(2,1)S(1)}, u32[]{:S(2)}, u32[]{:S(2)}) collective-permute-start(bf16[128,512]{1,0:T(8,128)(2,1)S(1)} %get-tuple-element.55), channel_id=1, source_target_pairs={{0,6},{1,7},{2,0},{3,1},{4,2},{5,3},{6,4},{7,5},{8,14},{9,15},{10,... | collective-permute-start | bytes 393224 | tf_op jit(solution)/shard_map/ppermute | solution.py:32
  73.8 2.8 %collective-permute-done.22 = bf16[1,128,896]{2,1,0:T(8,128)(2,1)S(1)} collective-permute-done((bf16[1,128,896]{2,1,0:T(8,128)(2,1)S(1)}, bf16[1,128,896]{2,1,0:T(8,128)(2,1)S(1)}, u32[]{:S(2)}, u32[]{:S(2)}) %collective-permute-start.22) | collective-permute-done | bytes 229408 | tf_op jit(solution)/shard_map/ppermute | solution.py:28
  78.4 2.0 %collective-permute-start.25 = (bf16[2,128,896]{2,1,0:T(8,128)(2,1)S(1)}, bf16[2,128,896]{2,1,0:T(8,128)(2,1)S(1)}, u32[]{:S(2)}, u32[]{:S(2)}) collective-permute-start(bf16[2,128,896]{2,1,0:T(8,128)(2,1)S(1)} %pad_maximum_fusion.2), channel_id=1, source_target_pairs={{0,6},{1,7},{2,0},{3,1},{4,2},{5,3},{6,4},{7,5},{8,14},{9,15},{10,... | collective-permute-start | bytes 1376264 | tf_op jit(solution)/shard_map/ppermute | solution.py:32
  80.8 3.1 %collective-permute-start.19 = (bf16[256,512]{1,0:T(8,128)(2,1)S(1)}, bf16[256,512]{1,0:T(8,128)(2,1)}, u32[]{:S(2)}, u32[]{:S(2)}) collective-permute-start(bf16[256,512]{1,0:T(8,128)(2,1)S(1)} %pad_maximum_fusion.4), channel_id=1, source_target_pairs={{0,6},{1,7},{2,0},{3,1},{4,2},{5,3},{6,4},{7,5},{8,14},{9,15},{10,... | collective-permute-start | bytes 786440 | tf_op jit(solution)/shard_map/ppermute | solution.py:32
  84.0 7.8 %collective-permute-done.23 = bf16[2,128,896]{2,1,0:T(8,128)(2,1)S(1)} collective-permute-done((bf16[2,128,896]{2,1,0:T(8,128)(2,1)S(1)}, bf16[2,128,896]{2,1,0:T(8,128)(2,1)S(1)}, u32[]{:S(2)}, u32[]{:S(2)}) %collective-permute-start.23) | collective-permute-done | bytes 458784 | tf_op jit(solution)/shard_map/ppermute | solution.py:28
  93.1 5.9 %all-to-all-start = ((bf16[16,2,8,1024]{3,2,1,0:T(8,128)(2,1)}), bf16[16,2,8,1024]{3,2,1,0:T(8,128)(2,1)S(1)}, u32[]{:S(2)}, u32[]{:S(2)}) async-start(bf16[16,2,8,1024]{3,2,1,0:T(8,128)(2,1)} %pad_maximum_fusion), calls=%async_computation | async-start | bytes 1048576 | tf_op jit(solution)/shard_map/all_to_all | solution.py:411
  100.2 3.4 %collective-permute-start.20 = (bf16[63,512]{1,0:T(8,128)(2,1)S(1)}, bf16[63,512]{1,0:T(8,128)(2,1)S(1)}, u32[]{:S(2)}, u32[]{:S(2)}) collective-permute-start(bf16[63,512]{1,0:T(8,128)(2,1)S(1)} %slice.268), channel_id=1, source_target_pairs={{0,8},{8,16},{16,24},{24,32},{32,40},{40,48},{48,56},{56,64},{64,7... | collective-permute-start | bytes 193544 | tf_op jit(solution)/shard_map/ppermute | solution.py:41
  103.6 4.9 %collective-permute-done.20 = bf16[63,512]{1,0:T(8,128)(2,1)S(1)} collective-permute-done((bf16[63,512]{1,0:T(8,128)(2,1)S(1)}, bf16[63,512]{1,0:T(8,128)(2,1)S(1)}, u32[]{:S(2)}, u32[]{:S(2)}) %collective-permute-start.20) | collective-permute-done | bytes 64544 | tf_op jit(solution)/shard_map/ppermute | solution.py:41
  110.0 2.5 %scatter.1 = f32[96,8,896]{2,1,0:T(8,128)} custom-call(s32[32]{0:T(128)S(1)} %fusion.16.label_ref, bf16[32,8,1024]{2,1,0:T(8,128)(2,1)S(1)} %bitcast.62), custom_call_target="tpu_custom_call" | custom-call | flops 274877906944 | bytes 4294967296 | tf_op jit(solution)/shard_map/scatter/pallas_call | solution.py:432
  (82 shorter events, 19.5 us)
Async XLA Ops:
  3.6 16.4 %collective-permute-start.4 = (bf16[1920,128]{1,0:T(8,128)(2,1)}, bf16[1920,128]{1,0:T(8,128)(2,1)S(1)}, u32[]{:S(2)}, u32[]{:S(2)}) collective-permute-start(bf16[1920,128]{1,0:T(8,128)(2,1)} %get-tuple-element.27.refs_1_), channel_id=1, source_target_pairs={{0,2},{1,3},{2,4},{3,5},{4,6},{5,7},{6,0},{7,1},{8,10},{9,11},{10,... | collective-permute-start | bytes 1474568 | tf_op jit(solution)/shard_map/ppermute | solution.py:28
  5.6 14.4 %collective-permute-start.2 = (bf16[1920,128]{1,0:T(8,128)(2,1)}, bf16[1920,128]{1,0:T(8,128)(2,1)S(1)}, u32[]{:S(2)}, u32[]{:S(2)}) collective-permute-start(bf16[1920,128]{1,0:T(8,128)(2,1)} %get-tuple-element.24.refs_0_), channel_id=1, source_target_pairs={{0,6},{1,7},{2,0},{3,1},{4,2},{5,3},{6,4},{7,5},{8,14},{9,15},{10,... | collective-permute-start | bytes 1474568 | tf_op jit(solution)/shard_map/ppermute | solution.py:32
  7.8 21.9 %collective-permute-start = (bf16[1920,128]{1,0:T(8,128)(2,1)}, bf16[1920,128]{1,0:T(8,128)(2,1)S(1)}, u32[]{:S(2)}, u32[]{:S(2)}) collective-permute-start(bf16[1920,128]{1,0:T(8,128)(2,1)} %get-tuple-element.24.refs_0_), channel_id=1, source_target_pairs={{0,2},{1,3},{2,4},{3,5},{4,6},{5,7},{6,0},{7,1},{8,10},{9,11},{10,... | collective-permute-start | bytes 1474568 | tf_op jit(solution)/shard_map/ppermute | solution.py:28
  7.8 21.9 %collective-permute-start.3 = (bf16[1920,128]{1,0:T(8,128)(2,1)}, bf16[1920,128]{1,0:T(8,128)(2,1)S(1)}, u32[]{:S(2)}, u32[]{:S(2)}) collective-permute-start(bf16[1920,128]{1,0:T(8,128)(2,1)} %get-tuple-element.27.refs_1_), channel_id=1, source_target_pairs={{0,6},{1,7},{2,0},{3,1},{4,2},{5,3},{6,4},{7,5},{8,14},{9,15},{10,... | collective-permute-start | bytes 1474568 | tf_op jit(solution)/shard_map/ppermute | solution.py:32
  11.1 19.5 %collective-permute-start.5 = (bf16[1920,128]{1,0:T(8,128)(2,1)}, bf16[1920,128]{1,0:T(8,128)(2,1)S(1)}, u32[]{:S(2)}, u32[]{:S(2)}) collective-permute-start(bf16[1920,128]{1,0:T(8,128)(2,1)} %get-tuple-element.24.refs_0_), channel_id=1, source_target_pairs={{0,1},{1,0},{2,3},{3,2},{4,5},{5,4},{6,7},{7,6},{8,9},{9,8},{10,11... | collective-permute-start | bytes 1474568 | tf_op jit(solution)/shard_map/ppermute | solution.py:36
  20.0 11.0 %collective-permute-start.6 = (bf16[1920,128]{1,0:T(8,128)(2,1)S(1)}, bf16[1920,128]{1,0:T(8,128)(2,1)S(1)}, u32[]{:S(2)}, u32[]{:S(2)}) collective-permute-start(bf16[1920,128]{1,0:T(8,128)(2,1)S(1)} %copy-done.5), channel_id=1, source_target_pairs={{0,1},{1,0},{2,3},{3,2},{4,5},{5,4},{6,7},{7,6},{8,9},{9,8},{10,11... | collective-permute-start | bytes 1474568 | tf_op jit(solution)/shard_map/ppermute | solution.py:36
  30.0 4.9 %collective-permute-start.7 = (bf16[1920,128]{1,0:T(8,128)(2,1)S(1)}, bf16[1920,128]{1,0:T(8,128)(2,1)S(1)}, u32[]{:S(2)}, u32[]{:S(2)}) collective-permute-start(bf16[1920,128]{1,0:T(8,128)(2,1)S(1)} %get-tuple-element.65), channel_id=1, source_target_pairs={{0,1},{1,0},{2,3},{3,2},{4,5},{5,4},{6,7},{7,6},{8,9},{9,8},{10,11... | collective-permute-start | bytes 1474568 | tf_op jit(solution)/shard_map/ppermute | solution.py:36
  30.5 4.4 %collective-permute-start.8 = (bf16[1920,128]{1,0:T(8,128)(2,1)S(1)}, bf16[1920,128]{1,0:T(8,128)(2,1)S(1)}, u32[]{:S(2)}, u32[]{:S(2)}) collective-permute-start(bf16[1920,128]{1,0:T(8,128)(2,1)S(1)} %get-tuple-element.62), channel_id=1, source_target_pairs={{0,1},{1,0},{2,3},{3,2},{4,5},{5,4},{6,7},{7,6},{8,9},{9,8},{10,11... | collective-permute-start | bytes 1474568 | tf_op jit(solution)/shard_map/ppermute | solution.py:36
  30.6 4.3 %collective-permute-start.9 = (bf16[1920,128]{1,0:T(8,128)(2,1)S(1)}, bf16[1920,128]{1,0:T(8,128)(2,1)S(1)}, u32[]{:S(2)}, u32[]{:S(2)}) collective-permute-start(bf16[1920,128]{1,0:T(8,128)(2,1)S(1)} %get-tuple-element.60), channel_id=1, source_target_pairs={{0,1},{1,0},{2,3},{3,2},{4,5},{5,4},{6,7},{7,6},{8,9},{9,8},{10,11... | collective-permute-start | bytes 1474568 | tf_op jit(solution)/shard_map/ppermute | solution.py:36
  31.0 14.5 %collective-permute-start.1 = (bf16[1920,128]{1,0:T(8,128)(2,1)S(1)}, bf16[1920,128]{1,0:T(8,128)(2,1)S(1)}, u32[]{:S(2)}, u32[]{:S(2)}) collective-permute-start(bf16[1920,128]{1,0:T(8,128)(2,1)S(1)} %get-tuple-element.61), channel_id=1, source_target_pairs={{0,2},{1,3},{2,4},{3,5},{4,6},{5,7},{6,0},{7,1},{8,10},{9,11},{10,... | collective-permute-start | bytes 1474568 | tf_op jit(solution)/shard_map/ppermute | solution.py:28
  32.3 13.4 %collective-permute-start.11 = (bf16[1920,128]{1,0:T(8,128)(2,1)S(1)}, bf16[1920,128]{1,0:T(8,128)(2,1)S(1)}, u32[]{:S(2)}, u32[]{:S(2)}) collective-permute-start(bf16[1920,128]{1,0:T(8,128)(2,1)S(1)} %get-tuple-element.63), channel_id=1, source_target_pairs={{0,6},{1,7},{2,0},{3,1},{4,2},{5,3},{6,4},{7,5},{8,14},{9,15},{10,... | collective-permute-start | bytes 1474568 | tf_op jit(solution)/shard_map/ppermute | solution.py:32
  49.3 11.1 %collective-permute-start.14 = (bf16[2,64,512]{2,1,0:T(8,128)(2,1)S(1)}, bf16[2,64,512]{2,1,0:T(8,128)(2,1)S(1)}, u32[]{:S(2)}, u32[]{:S(2)}) collective-permute-start(bf16[2,64,512]{2,1,0:T(8,128)(2,1)S(1)} %get-tuple-element.33), channel_id=1, source_target_pairs={{8,0},{16,8},{24,16},{32,24},{40,32},{48,40},{56,48},{64,56},{72,6... | collective-permute-start | bytes 393224 | tf_op jit(solution)/shard_map/ppermute | solution.py:41
  62.4 3.9 %collective-permute-start.21 = (bf16[4,2,128,896]{3,2,1,0:T(8,128)(2,1)S(1)}, bf16[4,2,128,896]{3,2,1,0:T(8,128)(2,1)S(1)}, u32[]{:S(2)}, u32[]{:S(2)}) collective-permute-start(bf16[4,2,128,896]{3,2,1,0:T(8,128)(2,1)S(1)} %get-tuple-element.45), channel_id=1, source_target_pairs={{0,1},{1,0},{2,3},{3,2},{4,5},{5,4},{6,7},{7,6},{8,9},{9,8},{10,11... | collective-permute-start | bytes 5505032 | tf_op jit(solution)/shard_map/ppermute | solution.py:36
  63.8 6.5 %collective-permute-start.15 = (bf16[4,256,512]{2,1,0:T(8,128)(2,1)S(1)}, bf16[4,256,512]{2,1,0:T(8,128)(2,1)S(1)}, u32[]{:S(2)}, u32[]{:S(2)}) collective-permute-start(bf16[4,256,512]{2,1,0:T(8,128)(2,1)S(1)} %get-tuple-element.43), channel_id=1, source_target_pairs={{0,1},{1,0},{2,3},{3,2},{4,5},{5,4},{6,7},{7,6},{8,9},{9,8},{10,11... | collective-permute-start | bytes 3145736 | tf_op jit(solution)/shard_map/ppermute | solution.py:36
  66.5 10.1 %collective-permute-start.22 = (bf16[1,128,896]{2,1,0:T(8,128)(2,1)S(1)}, bf16[1,128,896]{2,1,0:T(8,128)(2,1)S(1)}, u32[]{:S(2)}, u32[]{:S(2)}) collective-permute-start(bf16[1,128,896]{2,1,0:T(8,128)(2,1)S(1)} %get-tuple-element.48), channel_id=1, source_target_pairs={{0,2},{1,3},{2,4},{3,5},{4,6},{5,7},{6,0},{7,1},{8,10},{9,11},{10,... | collective-permute-start | bytes 688136 | tf_op jit(solution)/shard_map/ppermute | solution.py:28
  67.7 8.9 %collective-permute-start.24 = (bf16[1,128,896]{2,1,0:T(8,128)(2,1)S(1)}, bf16[1,128,896]{2,1,0:T(8,128)(2,1)S(1)}, u32[]{:S(2)}, u32[]{:S(2)}) collective-permute-start(bf16[1,128,896]{2,1,0:T(8,128)(2,1)S(1)} %get-tuple-element.49), channel_id=1, source_target_pairs={{0,6},{1,7},{2,0},{3,1},{4,2},{5,3},{6,4},{7,5},{8,14},{9,15},{10,... | collective-permute-start | bytes 688136 | tf_op jit(solution)/shard_map/ppermute | solution.py:32
  70.5 10.0 %collective-permute-start.16 = (bf16[128,512]{1,0:T(8,128)(2,1)S(1)}, bf16[128,512]{1,0:T(8,128)(2,1)S(1)}, u32[]{:S(2)}, u32[]{:S(2)}) collective-permute-start(bf16[128,512]{1,0:T(8,128)(2,1)S(1)} %get-tuple-element.54), channel_id=1, source_target_pairs={{0,2},{1,3},{2,4},{3,5},{4,6},{5,7},{6,0},{7,1},{8,10},{9,11},{10,... | collective-permute-start | bytes 393224 | tf_op jit(solution)/shard_map/ppermute | solution.py:28
  70.5 9.9 %collective-permute-start.18 = (bf16[128,512]{1,0:T(8,128)(2,1)S(1)}, bf16[128,512]{1,0:T(8,128)(2,1)S(1)}, u32[]{:S(2)}, u32[]{:S(2)}) collective-permute-start(bf16[128,512]{1,0:T(8,128)(2,1)S(1)} %get-tuple-element.55), channel_id=1, source_target_pairs={{0,6},{1,7},{2,0},{3,1},{4,2},{5,3},{6,4},{7,5},{8,14},{9,15},{10,... | collective-permute-start | bytes 393224 | tf_op jit(solution)/shard_map/ppermute | solution.py:32
  76.9 14.9 %collective-permute-start.23 = (bf16[2,128,896]{2,1,0:T(8,128)(2,1)S(1)}, bf16[2,128,896]{2,1,0:T(8,128)(2,1)S(1)}, u32[]{:S(2)}, u32[]{:S(2)}) collective-permute-start(bf16[2,128,896]{2,1,0:T(8,128)(2,1)S(1)} %pad_maximum_fusion.1), channel_id=1, source_target_pairs={{0,2},{1,3},{2,4},{3,5},{4,6},{5,7},{6,0},{7,1},{8,10},{9,11},{10,... | collective-permute-start | bytes 1376264 | tf_op jit(solution)/shard_map/ppermute | solution.py:28
  78.4 13.5 %collective-permute-start.25 = (bf16[2,128,896]{2,1,0:T(8,128)(2,1)S(1)}, bf16[2,128,896]{2,1,0:T(8,128)(2,1)S(1)}, u32[]{:S(2)}, u32[]{:S(2)}) collective-permute-start(bf16[2,128,896]{2,1,0:T(8,128)(2,1)S(1)} %pad_maximum_fusion.2), channel_id=1, source_target_pairs={{0,6},{1,7},{2,0},{3,1},{4,2},{5,3},{6,4},{7,5},{8,14},{9,15},{10,... | collective-permute-start | bytes 1376264 | tf_op jit(solution)/shard_map/ppermute | solution.py:32
  80.6 18.4 %collective-permute-start.17 = (bf16[256,512]{1,0:T(8,128)(2,1)S(1)}, bf16[256,512]{1,0:T(8,128)(2,1)}, u32[]{:S(2)}, u32[]{:S(2)}) collective-permute-start(bf16[256,512]{1,0:T(8,128)(2,1)S(1)} %pad_maximum_fusion.3), channel_id=1, source_target_pairs={{0,2},{1,3},{2,4},{3,5},{4,6},{5,7},{6,0},{7,1},{8,10},{9,11},{10,... | collective-permute-start | bytes 786440 | tf_op jit(solution)/shard_map/ppermute | solution.py:28
  80.8 18.2 %collective-permute-start.19 = (bf16[256,512]{1,0:T(8,128)(2,1)S(1)}, bf16[256,512]{1,0:T(8,128)(2,1)}, u32[]{:S(2)}, u32[]{:S(2)}) collective-permute-start(bf16[256,512]{1,0:T(8,128)(2,1)S(1)} %pad_maximum_fusion.4), channel_id=1, source_target_pairs={{0,6},{1,7},{2,0},{3,1},{4,2},{5,3},{6,4},{7,5},{8,14},{9,15},{10,... | collective-permute-start | bytes 786440 | tf_op jit(solution)/shard_map/ppermute | solution.py:32
  93.1 16.3 %all-to-all-start = ((bf16[16,2,8,1024]{3,2,1,0:T(8,128)(2,1)}), bf16[16,2,8,1024]{3,2,1,0:T(8,128)(2,1)S(1)}, u32[]{:S(2)}, u32[]{:S(2)}) async-start(bf16[16,2,8,1024]{3,2,1,0:T(8,128)(2,1)} %pad_maximum_fusion), calls=%async_computation | async-start | bytes 1048576 | tf_op jit(solution)/shard_map/all_to_all | solution.py:411
  100.2 8.3 %collective-permute-start.20 = (bf16[63,512]{1,0:T(8,128)(2,1)S(1)}, bf16[63,512]{1,0:T(8,128)(2,1)S(1)}, u32[]{:S(2)}, u32[]{:S(2)}) collective-permute-start(bf16[63,512]{1,0:T(8,128)(2,1)S(1)} %slice.268), channel_id=1, source_target_pairs={{0,8},{8,16},{16,24},{24,32},{32,40},{40,48},{48,56},{56,64},{64,7... | collective-permute-start | bytes 193544 | tf_op jit(solution)/shard_map/ppermute | solution.py:41
  (13 other events, 86.0 us)

commit v6 on v4

--- a/solution.py
+++ b/solution.py
@@ -176,7 +176,7 @@
     scores = [lax.dot_general(q[h], k[h], NT, preferred_element_type=F32) * SCALE for h in some]
     dattention = [lax.dot_general(g[h], v[h], NT, preferred_element_type=F32) for h in some]
     raised = [jnp.exp(x - jnp.max(x, -1, keepdims=True)) for x in scores]
-    attention = [x / jnp.sum(x, -1, keepdims=True) for x in raised]
+    attention = [x * (1.0 / jnp.sum(x, -1, keepdims=True)) for x in raised]
     mean = [jnp.sum(attention[h] * dattention[h], -1, keepdims=True) for h in some]
     dscores = [(attention[h] * (dattention[h] - mean[h])).astype(BF16) for h in some]
     gq = [jnp.dot(dscores[h], k[h], preferred_element_type=F32) * SCALE for h in some]

time: 113 us -> 113 us (level)
  no operation moved by 1% of the time
where the time goes in v6:
time: 113 us
  starting transfers between devices  41.7 us (37%)
  waiting for transfers between devices  36.7 us (32%)
  Pallas kernels  23.2 us (21%)
  local copies, waits for them, and re-layouts  5.16 us (5%)
  other arithmetic  4.92 us (4%)
    ppermute x7, waiting for transfers between devices, up(): return lax.ppermute(x, 'db', [(s, (s + 2) % 8) for s in range(8)])  27.6 us
    ppermute x7, starting transfers between devices, down(): return lax.ppermute(x, 'db', [(s, (s - 2) % 8) for s in range(8)])  19 us
    ppermute x2, starting transfers between devices, along_ctx(): lax.ppermute(x, 'ctx', [(i, i + by) for i in range(peers) if 0 <= i + by...  8.27 us
    pallas_call x1, Pallas kernels, per_device(): pl.pallas_call(near_kernel, name='near', out_shape=(shape((2, rows, width...  6.53 us
    ppermute x7, starting transfers between devices, up(): return lax.ppermute(x, 'db', [(s, (s + 2) % 8) for s in range(8)])  6.34 us
    pallas_call x1, Pallas kernels, per_device(): pl.pallas_call(attend_kernel, name='attend', out_shape=(shape((K * R, wid...  6.18 us
    all_to_all x1, starting transfers between devices, per_device(): parts = lax.all_to_all(spread, 'ctx', 0, 0, tiled=True)  5.88 us
    unnamed x20, local copies, waits for them, and re-layouts  5.11 us
  transfers between devices with their start and end apart: 27, of which 11 were waited for; matrix products, arithmetic and copies ran while one was open for 4% of the time, Pallas kernels for 13%

profile of v6, /device:TPU:2, one launch (start us, length us, event | category | flops | bytes accessed | tf_op | source)
XLA Modules:
  0.0 112.8 jit_solution(13871710731513169445)
XLA Ops:
  0.6 3.0 %load.1 = (bf16[1920,128]{1,0:T(8,128)(2,1)}, bf16[1920,128]{1,0:T(8,128)(2,1)}, f32[2,8,128]{2,1,0:T(8,128)}) custom-call(s32[2,4]{1,0:T(2,128)} %bitcast.63, s32[2,4]{1,0:T(2,128)} %bitcast.66, bf16[256,512]{1,0:T(8,128)(2,1)} %states_ref.1, bf16[256,512]{1,0:T(8,128)(2,1)} %cotangent_ref.1, bf16[96,128,896]{2,1,0:T(8,128)(2,1)} %database_ref.1), custom_call_target="tpu_custom_call" | custom-call | tf_op jit(solution)/shard_map/load/pallas_call | solution.py:320
  3.6 2.0 %collective-permute-start.4 = (bf16[1920,128]{1,0:T(8,128)(2,1)}, bf16[1920,128]{1,0:T(8,128)(2,1)S(1)}, u32[]{:S(2)}, u32[]{:S(2)}) collective-permute-start(bf16[1920,128]{1,0:T(8,128)(2,1)} %get-tuple-element.27.refs_1_), channel_id=1, source_target_pairs={{0,2},{1,3},{2,4},{3,5},{4,6},{5,7},{6,0},{7,1},{8,10},{9,11},{10,... | collective-permute-start | bytes 1474568 | tf_op jit(solution)/shard_map/ppermute | solution.py:28
  5.6 2.2 %collective-permute-start.2 = (bf16[1920,128]{1,0:T(8,128)(2,1)}, bf16[1920,128]{1,0:T(8,128)(2,1)S(1)}, u32[]{:S(2)}, u32[]{:S(2)}) collective-permute-start(bf16[1920,128]{1,0:T(8,128)(2,1)} %get-tuple-element.24.refs_0_), channel_id=1, source_target_pairs={{0,6},{1,7},{2,0},{3,1},{4,2},{5,3},{6,4},{7,5},{8,14},{9,15},{10,... | collective-permute-start | bytes 1474568 | tf_op jit(solution)/shard_map/ppermute | solution.py:32
  7.8 3.2 %collective-permute-start.3 = (bf16[1920,128]{1,0:T(8,128)(2,1)}, bf16[1920,128]{1,0:T(8,128)(2,1)S(1)}, u32[]{:S(2)}, u32[]{:S(2)}) collective-permute-start(bf16[1920,128]{1,0:T(8,128)(2,1)} %get-tuple-element.27.refs_1_), channel_id=1, source_target_pairs={{0,6},{1,7},{2,0},{3,1},{4,2},{5,3},{6,4},{7,5},{8,14},{9,15},{10,... | collective-permute-start | bytes 1474568 | tf_op jit(solution)/shard_map/ppermute | solution.py:32
  11.1 2.2 %copy-done = bf16[4096,512]{1,0:T(8,128)(2,1)S(1)} copy-done((bf16[4096,512]{1,0:T(8,128)(2,1)S(1)}, bf16[4096,512]{1,0:T(8,128)(2,1)}, u32[]{:S(2)}) %copy-start) | copy-done | bytes 4194328
  13.3 2.2 %copy-done.1 = bf16[512,4096]{1,0:T(8,128)(2,1)S(1)} copy-done((bf16[512,4096]{1,0:T(8,128)(2,1)S(1)}, bf16[512,4096]{1,0:T(8,128)(2,1)}, u32[]{:S(2)}) %copy-start.1) | copy-done | bytes 4194328
  16.8 3.3 %collective-permute-done.4.refs_5_ = bf16[1920,128]{1,0:T(8,128)(2,1)S(1)} collective-permute-done((bf16[1920,128]{1,0:T(8,128)(2,1)}, bf16[1920,128]{1,0:T(8,128)(2,1)S(1)}, u32[]{:S(2)}, u32[]{:S(2)}) %collective-permute-start.4) | collective-permute-done | bytes 491552 | tf_op jit(solution)/shard_map/ppermute | solution.py:28
  20.1 9.6 %collective-permute-done.refs_4_ = bf16[1920,128]{1,0:T(8,128)(2,1)S(1)} collective-permute-done((bf16[1920,128]{1,0:T(8,128)(2,1)}, bf16[1920,128]{1,0:T(8,128)(2,1)S(1)}, u32[]{:S(2)}, u32[]{:S(2)}) %collective-permute-start) | collective-permute-done | bytes 491552 | tf_op jit(solution)/shard_map/ppermute | solution.py:28
  32.3 2.6 %collective-permute-start.11 = (bf16[1920,128]{1,0:T(8,128)(2,1)S(1)}, bf16[1920,128]{1,0:T(8,128)(2,1)S(1)}, u32[]{:S(2)}, u32[]{:S(2)}) collective-permute-start(bf16[1920,128]{1,0:T(8,128)(2,1)S(1)} %get-tuple-element.63), channel_id=1, source_target_pairs={{0,6},{1,7},{2,0},{3,1},{4,2},{5,3},{6,4},{7,5},{8,14},{9,15},{10,... | collective-permute-start | bytes 1474568 | tf_op jit(solution)/shard_map/ppermute | solution.py:32
  34.9 6.5 %near.1 = (f32[2,256,512]{2,1,0:T(8,128)S(1)}, bf16[1536,512]{1,0:T(8,128)(2,1)S(1)}, bf16[1536,512]{1,0:T(8,128)(2,1)S(1)}) custom-call(bf16[1920,128]{1,0:T(8,128)(2,1)S(1)} %copy-done.4, bf16[1920,128]{1,0:T(8,128)(2,1)S(1)} %copy-done.5, bf16[1920,128]{1,0:T(8,128)(2,1)S(1)} %collective-permute-done.2.refs_2_, ...), custom_call_target="tpu_custom_call" | custom-call | flops 1 | bytes 1 | tf_op jit(solution)/shard_map/near/pallas_call | solution.py:345
  41.5 4.1 %collective-permute-done.1 = bf16[1920,128]{1,0:T(8,128)(2,1)S(1)} collective-permute-done((bf16[1920,128]{1,0:T(8,128)(2,1)S(1)}, bf16[1920,128]{1,0:T(8,128)(2,1)S(1)}, u32[]{:S(2)}, u32[]{:S(2)}) %collective-permute-start.1) | collective-permute-done | bytes 491552 | tf_op jit(solution)/shard_map/ppermute | solution.py:28
  49.3 4.9 %collective-permute-start.14 = (bf16[2,64,512]{2,1,0:T(8,128)(2,1)S(1)}, bf16[2,64,512]{2,1,0:T(8,128)(2,1)S(1)}, u32[]{:S(2)}, u32[]{:S(2)}) collective-permute-start(bf16[2,64,512]{2,1,0:T(8,128)(2,1)S(1)} %get-tuple-element.33), channel_id=1, source_target_pairs={{8,0},{16,8},{24,16},{32,24},{40,32},{48,40},{56,48},{64,56},{72,6... | collective-permute-start | bytes 393224 | tf_op jit(solution)/shard_map/ppermute | solution.py:41
  54.2 6.2 %attend.1 = (bf16[256,512]{1,0:T(8,128)(2,1)S(1)}, bf16[256,512]{1,0:T(8,128)(2,1)S(1)}, f32[192,512]{1,0:T(8,128)S(1)}, bf16[4,2,128,896]{3,2,1,0:T(8,128)(2,1)S(1)}, bf16[4,2,128,896]{3,2,1,0:T(8,128)(2,1)S(1)}) custom-call(s32[2,4]{1,0:T(2,128)S(1)} %bitcast.64, bf16[1920,128]{1,0:T(8,128)(2,1)S(1)} %get-tuple-element.67.refs_0_.refs_1_, ...), custom_call_target="tpu_custom_call" | custom-call | flops 3758096384 | bytes 8388608 | tf_op jit(solution)/shard_map/attend/pallas_call | solution.py:371
  60.4 2.0 %last.1 = (bf16[256,512]{1,0:T(8,128)(2,1)S(1)}, bf16[4,2,128,896]{3,2,1,0:T(8,128)(2,1)S(1)}, bf16[4,2,128,896]{3,2,1,0:T(8,128)(2,1)S(1)}) custom-call(s32[2,4]{1,0:T(2,128)S(1)} %bitcast.65, bf16[256,512]{1,0:T(8,128)(2,1)S(1)} %get-tuple-element.31.refs_9_.refs_1_, ...), custom_call_target="tpu_custom_call", output_to_operand_aliasing={{1}: (9, {}), {2}: (10, {})} | custom-call | flops 939524096 | bytes 4194304 | tf_op jit(solution)/shard_map/last/pallas_call | solution.py:391
  67.7 2.6 %collective-permute-start.24 = (bf16[1,128,896]{2,1,0:T(8,128)(2,1)S(1)}, bf16[1,128,896]{2,1,0:T(8,128)(2,1)S(1)}, u32[]{:S(2)}, u32[]{:S(2)}) collective-permute-start(bf16[1,128,896]{2,1,0:T(8,128)(2,1)S(1)} %get-tuple-element.49), channel_id=1, source_target_pairs={{0,6},{1,7},{2,0},{3,1},{4,2},{5,3},{6,4},{7,5},{8,14},{9,15},{10,... | collective-permute-start | bytes 688136 | tf_op jit(solution)/shard_map/ppermute | solution.py:32
  70.5 3.2 %collective-permute-start.18 = (bf16[128,512]{1,0:T(8,128)(2,1)S(1)}, bf16[128,512]{1,0:T(8,128)(2,1)S(1)}, u32[]{:S(2)}, u32[]{:S(2)}) collective-permute-start(bf16[128,512]{1,0:T(8,128)(2,1)S(1)} %get-tuple-element.55), channel_id=1, source_target_pairs={{0,6},{1,7},{2,0},{3,1},{4,2},{5,3},{6,4},{7,5},{8,14},{9,15},{10,... | collective-permute-start | bytes 393224 | tf_op jit(solution)/shard_map/ppermute | solution.py:32
  73.8 2.8 %collective-permute-done.22 = bf16[1,128,896]{2,1,0:T(8,128)(2,1)S(1)} collective-permute-done((bf16[1,128,896]{2,1,0:T(8,128)(2,1)S(1)}, bf16[1,128,896]{2,1,0:T(8,128)(2,1)S(1)}, u32[]{:S(2)}, u32[]{:S(2)}) %collective-permute-start.22) | collective-permute-done | bytes 229408 | tf_op jit(solution)/shard_map/ppermute | solution.py:28
  78.4 2.0 %collective-permute-start.25 = (bf16[2,128,896]{2,1,0:T(8,128)(2,1)S(1)}, bf16[2,128,896]{2,1,0:T(8,128)(2,1)S(1)}, u32[]{:S(2)}, u32[]{:S(2)}) collective-permute-start(bf16[2,128,896]{2,1,0:T(8,128)(2,1)S(1)} %pad_maximum_fusion.2), channel_id=1, source_target_pairs={{0,6},{1,7},{2,0},{3,1},{4,2},{5,3},{6,4},{7,5},{8,14},{9,15},{10,... | collective-permute-start | bytes 1376264 | tf_op jit(solution)/shard_map/ppermute | solution.py:32
  80.8 3.1 %collective-permute-start.19 = (bf16[256,512]{1,0:T(8,128)(2,1)S(1)}, bf16[256,512]{1,0:T(8,128)(2,1)}, u32[]{:S(2)}, u32[]{:S(2)}) collective-permute-start(bf16[256,512]{1,0:T(8,128)(2,1)S(1)} %pad_maximum_fusion.4), channel_id=1, source_target_pairs={{0,6},{1,7},{2,0},{3,1},{4,2},{5,3},{6,4},{7,5},{8,14},{9,15},{10,... | collective-permute-start | bytes 786440 | tf_op jit(solution)/shard_map/ppermute | solution.py:32
  83.9 7.8 %collective-permute-done.23 = bf16[2,128,896]{2,1,0:T(8,128)(2,1)S(1)} collective-permute-done((bf16[2,128,896]{2,1,0:T(8,128)(2,1)S(1)}, bf16[2,128,896]{2,1,0:T(8,128)(2,1)S(1)}, u32[]{:S(2)}, u32[]{:S(2)}) %collective-permute-start.23) | collective-permute-done | bytes 458784 | tf_op jit(solution)/shard_map/ppermute | solution.py:28
  93.1 5.9 %all-to-all-start = ((bf16[16,2,8,1024]{3,2,1,0:T(8,128)(2,1)}), bf16[16,2,8,1024]{3,2,1,0:T(8,128)(2,1)S(1)}, u32[]{:S(2)}, u32[]{:S(2)}) async-start(bf16[16,2,8,1024]{3,2,1,0:T(8,128)(2,1)} %pad_maximum_fusion), calls=%async_computation | async-start | bytes 1048576 | tf_op jit(solution)/shard_map/all_to_all | solution.py:415
  100.2 3.4 %collective-permute-start.20 = (bf16[63,512]{1,0:T(8,128)(2,1)S(1)}, bf16[63,512]{1,0:T(8,128)(2,1)S(1)}, u32[]{:S(2)}, u32[]{:S(2)}) collective-permute-start(bf16[63,512]{1,0:T(8,128)(2,1)S(1)} %slice.268), channel_id=1, source_target_pairs={{0,8},{8,16},{16,24},{24,32},{32,40},{40,48},{48,56},{56,64},{64,7... | collective-permute-start | bytes 193544 | tf_op jit(solution)/shard_map/ppermute | solution.py:41
  103.6 4.9 %collective-permute-done.20 = bf16[63,512]{1,0:T(8,128)(2,1)S(1)} collective-permute-done((bf16[63,512]{1,0:T(8,128)(2,1)S(1)}, bf16[63,512]{1,0:T(8,128)(2,1)S(1)}, u32[]{:S(2)}, u32[]{:S(2)}) %collective-permute-start.20) | collective-permute-done | bytes 64544 | tf_op jit(solution)/shard_map/ppermute | solution.py:41
  110.0 2.7 %scatter.1 = f32[96,8,896]{2,1,0:T(8,128)} custom-call(s32[32]{0:T(128)S(1)} %fusion.16.label_ref, bf16[32,8,1024]{2,1,0:T(8,128)(2,1)S(1)} %bitcast.62), custom_call_target="tpu_custom_call" | custom-call | flops 274877906944 | bytes 4294967296 | tf_op jit(solution)/shard_map/scatter/pallas_call | solution.py:436
  (82 shorter events, 19.5 us)
Async XLA Ops:
  3.6 16.4 %collective-permute-start.4 = (bf16[1920,128]{1,0:T(8,128)(2,1)}, bf16[1920,128]{1,0:T(8,128)(2,1)S(1)}, u32[]{:S(2)}, u32[]{:S(2)}) collective-permute-start(bf16[1920,128]{1,0:T(8,128)(2,1)} %get-tuple-element.27.refs_1_), channel_id=1, source_target_pairs={{0,2},{1,3},{2,4},{3,5},{4,6},{5,7},{6,0},{7,1},{8,10},{9,11},{10,... | collective-permute-start | bytes 1474568 | tf_op jit(solution)/shard_map/ppermute | solution.py:28
  5.6 14.4 %collective-permute-start.2 = (bf16[1920,128]{1,0:T(8,128)(2,1)}, bf16[1920,128]{1,0:T(8,128)(2,1)S(1)}, u32[]{:S(2)}, u32[]{:S(2)}) collective-permute-start(bf16[1920,128]{1,0:T(8,128)(2,1)} %get-tuple-element.24.refs_0_), channel_id=1, source_target_pairs={{0,6},{1,7},{2,0},{3,1},{4,2},{5,3},{6,4},{7,5},{8,14},{9,15},{10,... | collective-permute-start | bytes 1474568 | tf_op jit(solution)/shard_map/ppermute | solution.py:32
  7.8 21.9 %collective-permute-start = (bf16[1920,128]{1,0:T(8,128)(2,1)}, bf16[1920,128]{1,0:T(8,128)(2,1)S(1)}, u32[]{:S(2)}, u32[]{:S(2)}) collective-permute-start(bf16[1920,128]{1,0:T(8,128)(2,1)} %get-tuple-element.24.refs_0_), channel_id=1, source_target_pairs={{0,2},{1,3},{2,4},{3,5},{4,6},{5,7},{6,0},{7,1},{8,10},{9,11},{10,... | collective-permute-start | bytes 1474568 | tf_op jit(solution)/shard_map/ppermute | solution.py:28
  7.8 21.9 %collective-permute-start.3 = (bf16[1920,128]{1,0:T(8,128)(2,1)}, bf16[1920,128]{1,0:T(8,128)(2,1)S(1)}, u32[]{:S(2)}, u32[]{:S(2)}) collective-permute-start(bf16[1920,128]{1,0:T(8,128)(2,1)} %get-tuple-element.27.refs_1_), channel_id=1, source_target_pairs={{0,6},{1,7},{2,0},{3,1},{4,2},{5,3},{6,4},{7,5},{8,14},{9,15},{10,... | collective-permute-start | bytes 1474568 | tf_op jit(solution)/shard_map/ppermute | solution.py:32
  11.1 19.5 %collective-permute-start.5 = (bf16[1920,128]{1,0:T(8,128)(2,1)}, bf16[1920,128]{1,0:T(8,128)(2,1)S(1)}, u32[]{:S(2)}, u32[]{:S(2)}) collective-permute-start(bf16[1920,128]{1,0:T(8,128)(2,1)} %get-tuple-element.24.refs_0_), channel_id=1, source_target_pairs={{0,1},{1,0},{2,3},{3,2},{4,5},{5,4},{6,7},{7,6},{8,9},{9,8},{10,11... | collective-permute-start | bytes 1474568 | tf_op jit(solution)/shard_map/ppermute | solution.py:36
  20.0 11.0 %collective-permute-start.6 = (bf16[1920,128]{1,0:T(8,128)(2,1)S(1)}, bf16[1920,128]{1,0:T(8,128)(2,1)S(1)}, u32[]{:S(2)}, u32[]{:S(2)}) collective-permute-start(bf16[1920,128]{1,0:T(8,128)(2,1)S(1)} %copy-done.5), channel_id=1, source_target_pairs={{0,1},{1,0},{2,3},{3,2},{4,5},{5,4},{6,7},{7,6},{8,9},{9,8},{10,11... | collective-permute-start | bytes 1474568 | tf_op jit(solution)/shard_map/ppermute | solution.py:36
  30.0 4.9 %collective-permute-start.7 = (bf16[1920,128]{1,0:T(8,128)(2,1)S(1)}, bf16[1920,128]{1,0:T(8,128)(2,1)S(1)}, u32[]{:S(2)}, u32[]{:S(2)}) collective-permute-start(bf16[1920,128]{1,0:T(8,128)(2,1)S(1)} %get-tuple-element.65), channel_id=1, source_target_pairs={{0,1},{1,0},{2,3},{3,2},{4,5},{5,4},{6,7},{7,6},{8,9},{9,8},{10,11... | collective-permute-start | bytes 1474568 | tf_op jit(solution)/shard_map/ppermute | solution.py:36
  30.5 4.4 %collective-permute-start.8 = (bf16[1920,128]{1,0:T(8,128)(2,1)S(1)}, bf16[1920,128]{1,0:T(8,128)(2,1)S(1)}, u32[]{:S(2)}, u32[]{:S(2)}) collective-permute-start(bf16[1920,128]{1,0:T(8,128)(2,1)S(1)} %get-tuple-element.62), channel_id=1, source_target_pairs={{0,1},{1,0},{2,3},{3,2},{4,5},{5,4},{6,7},{7,6},{8,9},{9,8},{10,11... | collective-permute-start | bytes 1474568 | tf_op jit(solution)/shard_map/ppermute | solution.py:36
  30.6 4.3 %collective-permute-start.9 = (bf16[1920,128]{1,0:T(8,128)(2,1)S(1)}, bf16[1920,128]{1,0:T(8,128)(2,1)S(1)}, u32[]{:S(2)}, u32[]{:S(2)}) collective-permute-start(bf16[1920,128]{1,0:T(8,128)(2,1)S(1)} %get-tuple-element.60), channel_id=1, source_target_pairs={{0,1},{1,0},{2,3},{3,2},{4,5},{5,4},{6,7},{7,6},{8,9},{9,8},{10,11... | collective-permute-start | bytes 1474568 | tf_op jit(solution)/shard_map/ppermute | solution.py:36
  31.0 14.5 %collective-permute-start.1 = (bf16[1920,128]{1,0:T(8,128)(2,1)S(1)}, bf16[1920,128]{1,0:T(8,128)(2,1)S(1)}, u32[]{:S(2)}, u32[]{:S(2)}) collective-permute-start(bf16[1920,128]{1,0:T(8,128)(2,1)S(1)} %get-tuple-element.61), channel_id=1, source_target_pairs={{0,2},{1,3},{2,4},{3,5},{4,6},{5,7},{6,0},{7,1},{8,10},{9,11},{10,... | collective-permute-start | bytes 1474568 | tf_op jit(solution)/shard_map/ppermute | solution.py:28
  32.3 13.4 %collective-permute-start.11 = (bf16[1920,128]{1,0:T(8,128)(2,1)S(1)}, bf16[1920,128]{1,0:T(8,128)(2,1)S(1)}, u32[]{:S(2)}, u32[]{:S(2)}) collective-permute-start(bf16[1920,128]{1,0:T(8,128)(2,1)S(1)} %get-tuple-element.63), channel_id=1, source_target_pairs={{0,6},{1,7},{2,0},{3,1},{4,2},{5,3},{6,4},{7,5},{8,14},{9,15},{10,... | collective-permute-start | bytes 1474568 | tf_op jit(solution)/shard_map/ppermute | solution.py:32
  49.3 11.1 %collective-permute-start.14 = (bf16[2,64,512]{2,1,0:T(8,128)(2,1)S(1)}, bf16[2,64,512]{2,1,0:T(8,128)(2,1)S(1)}, u32[]{:S(2)}, u32[]{:S(2)}) collective-permute-start(bf16[2,64,512]{2,1,0:T(8,128)(2,1)S(1)} %get-tuple-element.33), channel_id=1, source_target_pairs={{8,0},{16,8},{24,16},{32,24},{40,32},{48,40},{56,48},{64,56},{72,6... | collective-permute-start | bytes 393224 | tf_op jit(solution)/shard_map/ppermute | solution.py:41
  62.3 3.9 %collective-permute-start.21 = (bf16[4,2,128,896]{3,2,1,0:T(8,128)(2,1)S(1)}, bf16[4,2,128,896]{3,2,1,0:T(8,128)(2,1)S(1)}, u32[]{:S(2)}, u32[]{:S(2)}) collective-permute-start(bf16[4,2,128,896]{3,2,1,0:T(8,128)(2,1)S(1)} %get-tuple-element.45), channel_id=1, source_target_pairs={{0,1},{1,0},{2,3},{3,2},{4,5},{5,4},{6,7},{7,6},{8,9},{9,8},{10,11... | collective-permute-start | bytes 5505032 | tf_op jit(solution)/shard_map/ppermute | solution.py:36
  63.8 6.5 %collective-permute-start.15 = (bf16[4,256,512]{2,1,0:T(8,128)(2,1)S(1)}, bf16[4,256,512]{2,1,0:T(8,128)(2,1)S(1)}, u32[]{:S(2)}, u32[]{:S(2)}) collective-permute-start(bf16[4,256,512]{2,1,0:T(8,128)(2,1)S(1)} %get-tuple-element.43), channel_id=1, source_target_pairs={{0,1},{1,0},{2,3},{3,2},{4,5},{5,4},{6,7},{7,6},{8,9},{9,8},{10,11... | collective-permute-start | bytes 3145736 | tf_op jit(solution)/shard_map/ppermute | solution.py:36
  66.5 10.1 %collective-permute-start.22 = (bf16[1,128,896]{2,1,0:T(8,128)(2,1)S(1)}, bf16[1,128,896]{2,1,0:T(8,128)(2,1)S(1)}, u32[]{:S(2)}, u32[]{:S(2)}) collective-permute-start(bf16[1,128,896]{2,1,0:T(8,128)(2,1)S(1)} %get-tuple-element.48), channel_id=1, source_target_pairs={{0,2},{1,3},{2,4},{3,5},{4,6},{5,7},{6,0},{7,1},{8,10},{9,11},{10,... | collective-permute-start | bytes 688136 | tf_op jit(solution)/shard_map/ppermute | solution.py:28
  67.7 8.9 %collective-permute-start.24 = (bf16[1,128,896]{2,1,0:T(8,128)(2,1)S(1)}, bf16[1,128,896]{2,1,0:T(8,128)(2,1)S(1)}, u32[]{:S(2)}, u32[]{:S(2)}) collective-permute-start(bf16[1,128,896]{2,1,0:T(8,128)(2,1)S(1)} %get-tuple-element.49), channel_id=1, source_target_pairs={{0,6},{1,7},{2,0},{3,1},{4,2},{5,3},{6,4},{7,5},{8,14},{9,15},{10,... | collective-permute-start | bytes 688136 | tf_op jit(solution)/shard_map/ppermute | solution.py:32
  70.5 10.0 %collective-permute-start.16 = (bf16[128,512]{1,0:T(8,128)(2,1)S(1)}, bf16[128,512]{1,0:T(8,128)(2,1)S(1)}, u32[]{:S(2)}, u32[]{:S(2)}) collective-permute-start(bf16[128,512]{1,0:T(8,128)(2,1)S(1)} %get-tuple-element.54), channel_id=1, source_target_pairs={{0,2},{1,3},{2,4},{3,5},{4,6},{5,7},{6,0},{7,1},{8,10},{9,11},{10,... | collective-permute-start | bytes 393224 | tf_op jit(solution)/shard_map/ppermute | solution.py:28
  70.5 9.9 %collective-permute-start.18 = (bf16[128,512]{1,0:T(8,128)(2,1)S(1)}, bf16[128,512]{1,0:T(8,128)(2,1)S(1)}, u32[]{:S(2)}, u32[]{:S(2)}) collective-permute-start(bf16[128,512]{1,0:T(8,128)(2,1)S(1)} %get-tuple-element.55), channel_id=1, source_target_pairs={{0,6},{1,7},{2,0},{3,1},{4,2},{5,3},{6,4},{7,5},{8,14},{9,15},{10,... | collective-permute-start | bytes 393224 | tf_op jit(solution)/shard_map/ppermute | solution.py:32
  76.9 14.9 %collective-permute-start.23 = (bf16[2,128,896]{2,1,0:T(8,128)(2,1)S(1)}, bf16[2,128,896]{2,1,0:T(8,128)(2,1)S(1)}, u32[]{:S(2)}, u32[]{:S(2)}) collective-permute-start(bf16[2,128,896]{2,1,0:T(8,128)(2,1)S(1)} %pad_maximum_fusion.1), channel_id=1, source_target_pairs={{0,2},{1,3},{2,4},{3,5},{4,6},{5,7},{6,0},{7,1},{8,10},{9,11},{10,... | collective-permute-start | bytes 1376264 | tf_op jit(solution)/shard_map/ppermute | solution.py:28
  78.4 13.5 %collective-permute-start.25 = (bf16[2,128,896]{2,1,0:T(8,128)(2,1)S(1)}, bf16[2,128,896]{2,1,0:T(8,128)(2,1)S(1)}, u32[]{:S(2)}, u32[]{:S(2)}) collective-permute-start(bf16[2,128,896]{2,1,0:T(8,128)(2,1)S(1)} %pad_maximum_fusion.2), channel_id=1, source_target_pairs={{0,6},{1,7},{2,0},{3,1},{4,2},{5,3},{6,4},{7,5},{8,14},{9,15},{10,... | collective-permute-start | bytes 1376264 | tf_op jit(solution)/shard_map/ppermute | solution.py:32
  80.6 18.4 %collective-permute-start.17 = (bf16[256,512]{1,0:T(8,128)(2,1)S(1)}, bf16[256,512]{1,0:T(8,128)(2,1)}, u32[]{:S(2)}, u32[]{:S(2)}) collective-permute-start(bf16[256,512]{1,0:T(8,128)(2,1)S(1)} %pad_maximum_fusion.3), channel_id=1, source_target_pairs={{0,2},{1,3},{2,4},{3,5},{4,6},{5,7},{6,0},{7,1},{8,10},{9,11},{10,... | collective-permute-start | bytes 786440 | tf_op jit(solution)/shard_map/ppermute | solution.py:28
  80.8 18.2 %collective-permute-start.19 = (bf16[256,512]{1,0:T(8,128)(2,1)S(1)}, bf16[256,512]{1,0:T(8,128)(2,1)}, u32[]{:S(2)}, u32[]{:S(2)}) collective-permute-start(bf16[256,512]{1,0:T(8,128)(2,1)S(1)} %pad_maximum_fusion.4), channel_id=1, source_target_pairs={{0,6},{1,7},{2,0},{3,1},{4,2},{5,3},{6,4},{7,5},{8,14},{9,15},{10,... | collective-permute-start | bytes 786440 | tf_op jit(solution)/shard_map/ppermute | solution.py:32
  93.1 16.3 %all-to-all-start = ((bf16[16,2,8,1024]{3,2,1,0:T(8,128)(2,1)}), bf16[16,2,8,1024]{3,2,1,0:T(8,128)(2,1)S(1)}, u32[]{:S(2)}, u32[]{:S(2)}) async-start(bf16[16,2,8,1024]{3,2,1,0:T(8,128)(2,1)} %pad_maximum_fusion), calls=%async_computation | async-start | bytes 1048576 | tf_op jit(solution)/shard_map/all_to_all | solution.py:415
  100.2 8.3 %collective-permute-start.20 = (bf16[63,512]{1,0:T(8,128)(2,1)S(1)}, bf16[63,512]{1,0:T(8,128)(2,1)S(1)}, u32[]{:S(2)}, u32[]{:S(2)}) collective-permute-start(bf16[63,512]{1,0:T(8,128)(2,1)S(1)} %slice.268), channel_id=1, source_target_pairs={{0,8},{8,16},{16,24},{24,32},{32,40},{40,48},{48,56},{56,64},{64,7... | collective-permute-start | bytes 193544 | tf_op jit(solution)/shard_map/ppermute | solution.py:41
  (13 other events, 86.0 us)
